TPU v7x, 32 devices: a whole 2x2x4 slice. The times are simulated.
32 devices in a mesh: ens: 4 (over y, x), space: 8 (over z, core).
Axes of the slice: x: 2, y: 2, z: 4, core: 2. Of those that a mesh axis runs over, the one named last changes fastest.
Arguments:
- latents: bfloat16 [8, 2048, 1024], P('ens', 'space'), may hold values from -6 to 6
- edge_index: int32 [4096, 4], P('space'), may hold values from 0 to 767, as said below
- edge_weight: float32 [4096, 4], P('space'), may hold values from 0.1 to 1
- truth: float32 [100, 4096], P(None, 'space'), may hold values from -6 to 6
- w_hidden: bfloat16 [1024, 1024], replicated, may hold values from -0.1875 to 0.1875
- output_weight: bfloat16 [1024, 100], replicated, may hold values from -0.1875 to 0.1875
Outputs:
- grad_latents: float32 [8, 2048, 1024], P('ens', 'space')
- grad_hidden: float32 [1024, 1024], P('space')
- grad_out: float32 [1024, 100], P('space')
Inputs may be any that keep to these rules, and one draw needn't show every extreme that they name: edge_index of a grid point holds 4 distinct values, indexing the nodes of the bands below, own and above; the first band never points below and the last never above.
All inputs are finite; a program needn't handle non-finite values.
Results may differ from a plain program's by a relative error of at most 0.012.
The roundings to bfloat16 on the way count: a program that leaves them out, or rounds other values in their place, can miss the bound.
Values may be sent and summed in bfloat16 or wider, within the bound.
No kernel may reach another device: no remote copies, remote signals or barrier semaphores. Data moves between devices by JAX's collectives and lax.ppermute only.
A program may use at most 64 MiB of HBM per device.

v0:
```python
import functools
import math

import jax
import jax.numpy as jnp
from jax import lax
from jax.experimental import pallas as pl
from jax.experimental.pallas import tpu as pltpu
from jax.sharding import PartitionSpec as P

smoothing = 0.05
f32, bf16 = jnp.float32, jnp.bfloat16
across = (((1,), (0,)), ((), ()))
right_turned = (((1,), (1,)), ((), ()))
left_turned = (((0,), (0,)), ((), ()))


def chip_swap(value):
    count = lax.axis_size("space")
    return lax.ppermute(value, "space", [(i, i ^ 1) for i in range(count)])


def link_swap(value):
    count = lax.axis_size("space")
    pairs = [(i, i + 1) for i in range(1, count - 1, 2)]
    return lax.ppermute(value, "space", pairs + [(j, i) for i, j in pairs])


def core_swap(value, axis, bits):
    ens, space = lax.axis_size("ens"), lax.axis_size("space")

    def partner(e, s):
        bit = bits[s % 2]
        return (e ^ bit) * space + s if axis == "ens" else e * space + (s ^ (2 * bit))

    return lax.ppermute(
        value,
        ("ens", "space"),
        [(e * space + s, partner(e, s)) for e in range(ens) for s in range(space)],
    )


def routes(ens):
    if ens == 4:
        return [(0, 0), (1, 2), (2, 1), (3, 3)]
    return [(k, k) for k in range(ens)]


def exchanged(values):
    others = zip(values[1:], routes(len(values))[1:])
    return [values[0]] + [core_swap(value, "ens", bits) for value, bits in others]


def neighbour(place, bits):
    return place[0] ^ jnp.where(place[2] == 0, bits[0], bits[1])


def mul(a, b, dims=across):
    return lax.dot_general(a, b, dims, preferred_element_type=f32)


def call(body, outs, place, *operands, after=(), far=(), flops=0, last=False, scratch=()):
    vmem = pl.BlockSpec(memory_space=pltpu.VMEM)
    unread = pl.BlockSpec(memory_space=pl.ANY)

    def kernel(place_ref, *refs):
        body(place_ref, *refs[len(after) :])

    return pl.pallas_call(
        kernel,
        out_shape=[
            jax.ShapeDtypeStruct(shape, kind) if last else pltpu.VMEM(shape, kind)
            for shape, kind in outs
        ],
        in_specs=[pl.BlockSpec(memory_space=pltpu.SMEM)]
        + [unread] * len(after)
        + [pl.BlockSpec(memory_space=pltpu.HBM)] * len(far)
        + [vmem] * len(operands),
        out_specs=[vmem] * len(outs),
        scratch_shapes=scratch,
        cost_estimate=pl.CostEstimate(
            flops=flops,
            transcendentals=0,
            bytes_accessed=sum(x.size * x.dtype.itemsize for x in operands)
            + sum(math.prod(shape) * jnp.dtype(kind).itemsize for shape, kind in outs),
        ),
        compiler_params=pltpu.CompilerParams(vmem_limit_bytes=20 * 1024 * 1024),
    )(
        place,
        *after,
        *[pltpu.with_memory_space_constraint(x, pltpu.HBM) for x in far],
        *[pltpu.with_memory_space_constraint(x, pltpu.VMEM) for x in operands],
    )


def sides(core, nodes):
    above, below = 2 * nodes, 0
    return (
        pl.multiple_of(jnp.where(core == 0, above, below), nodes),
        pl.multiple_of(jnp.where(core == 0, below, above), nodes),
    )


def padded(value, rows):
    zeros = jnp.zeros((rows - value.shape[0], value.shape[1]), value.dtype)
    return jnp.concatenate([value, zeros], axis=0)


def prepare_body(
    ens, place, latents, w_hidden, index, weight, w_out_t, truth,
    adjacency, adjacency_t, w_hidden_t, own, w_hidden_here, w_out_here, truth_here, sems
):
    copies = [
        pltpu.make_async_copy(w_hidden, w_hidden_here, sems.at[0]),
        pltpu.make_async_copy(latents, own, sems.at[1]),
    ]
    for copy in copies:
        copy.start()
    edges, grid = index.shape
    chunk = grid // ens
    rows = adjacency_t.shape[0]
    row = lax.broadcasted_iota(jnp.int32, (rows, chunk), 0)
    for k, bits in enumerate(routes(ens)):
        lanes = pl.ds(pl.multiple_of(neighbour(place, bits) * chunk, chunk), chunk)
        nodes = index[:, lanes]
        weights = weight[:, lanes].astype(bf16).astype(f32)
        block = jnp.zeros((rows, chunk), f32)
        for j in range(edges):
            block += jnp.where(nodes[j : j + 1] == row, weights[j : j + 1], 0.0)
        adjacency_t[:, k * chunk : (k + 1) * chunk] = block.astype(bf16)
        adjacency[k * chunk : (k + 1) * chunk, :] = block.T.astype(bf16)
    w_out_here[...] = padded(w_out_t[...].astype(f32), w_out_here.shape[0]).astype(bf16)
    truth_here[...] = padded(truth[...], truth_here.shape[0])
    for copy in copies:
        copy.wait()
    w_hidden_t[...] = w_hidden_here[...].T


def partial_body(place, own, on_chip, adjacency, partial):
    mem, nodes, _ = own.shape
    first, _ = sides(place[2], nodes)
    for m in range(mem):
        total = mul(adjacency[:, nodes : 2 * nodes], own[m])
        partial[m] = total + mul(adjacency[:, pl.ds(first, nodes)], on_chip[m])


def forward_body(
    ens, place, partial, on_link, adjacency, w_hidden, w_out_t, aggregate, preact, activated, *pieces
):
    mem, nodes, width = on_link.shape
    variables = w_out_t.shape[0]
    grid = adjacency.shape[0]
    chunk = grid // ens
    step = 256
    _, second = sides(place[2], nodes)
    for m in range(mem):
        total = partial[m] + mul(adjacency[:, pl.ds(second, nodes)], on_link[m])
        gathered = total.astype(bf16)
        aggregate[m] = gathered
        forecast = jnp.zeros((grid, variables), f32)
        for at in range(0, width, step):
            value = mul(gathered, w_hidden[:, at : at + step])
            preact[m, :, at : at + step] = value
            silu = (value / (1.0 + jnp.exp(-value))).astype(bf16)
            activated[m, :, at : at + step] = silu
            forecast += mul(silu, w_out_t[:, at : at + step], right_turned)
        turned = forecast.T
        for k in range(ens):
            rows = slice(m * variables, (m + 1) * variables)
            pieces[k][rows] = turned[:, k * chunk : (k + 1) * chunk]


def slope_body(place, preact, slope):
    for m in range(preact.shape[0]):
        value = preact[m]
        logistic = 1.0 / (1.0 + jnp.exp(-value))
        slope[m] = logistic * (1.0 + value * (1.0 - logistic))


def turn_body(place, aggregate, aggregate_t):
    mem, grid, _ = aggregate.shape
    for m in range(mem):
        aggregate_t[:, m * grid : (m + 1) * grid] = aggregate[m].T


def loss_body(ens, scale, place, truth, *refs):
    here, out = refs[:ens], refs[ens:]
    rows, chunk = here[0].shape
    mem = rows // truth.shape[0]
    members = mem * ens
    variables = truth.shape[0]
    target = truth[:, pl.ds(pl.multiple_of(place[0] * chunk, chunk), chunk)]
    forecasts = [
        here[k][m * variables : (m + 1) * variables] for k in range(ens) for m in range(mem)
    ]

    def ratio(d):
        return d * lax.rsqrt(d * d + smoothing * smoothing)

    spread = [jnp.zeros_like(target) for _ in forecasts]
    for i in range(members):
        for j in range(i + 1, members):
            term = ratio(forecasts[i] - forecasts[j])
            spread[i] += term
            spread[j] -= term
    gradients = [
        scale
        * (
            ratio(forecasts[i] - target) * (1.0 / members)
            - spread[i] * (1.0 / (members * (members - 1)))
        )
        for i in range(members)
    ]
    for k in range(ens):
        total = jnp.concatenate(gradients[k * mem : (k + 1) * mem], axis=0)
        out[k][...] = total.astype(bf16)


def backward_body(ens, place, w_out_t, slope, activated, *refs):
    dforecast, (dpreact, out_part) = refs[:ens], refs[ens:]
    mem, grid, _ = slope.shape
    variables = w_out_t.shape[0]
    gradients = jnp.concatenate([piece[...] for piece in dforecast], axis=1)
    gradients = gradients.astype(f32)
    out_total = None
    for m in range(mem):
        gradient = gradients[m * variables : (m + 1) * variables].astype(bf16)
        dactivated = mul(gradient, w_out_t[...], left_turned)
        dpreact[m * grid : (m + 1) * grid] = (dactivated * slope[m]).astype(bf16)
        part = mul(gradient, activated[m])
        out_total = part if out_total is None else out_total + part
    out_part[...] = out_total


def slot_of(core, k):
    return jnp.where(k == 1 + core, 2, jnp.where(k == 2 - core, 1, k))


def half_body(ens, chips, mine, place, dpreact, out_part, aggregate_t, half):
    e, chip, core = place[0], place[1], place[2]
    core = core if mine else 1 - core
    rows = aggregate_t.shape[2]
    lanes = dpreact.shape[1] // ens
    strip = 2 * (half.shape[2] - rows)
    for z in range(chips):
        columns = pl.ds(pl.multiple_of((2 * z + core) * rows, rows), rows)
        part = padded(out_part[:, columns], ens * strip).astype(half.dtype)
        for j in range(ens):
            slot = slot_of(core, j ^ e)
            half[slot, z ^ chip, rows:, :rows] = part[j * strip : j * strip + strip // 2]
            half[slot, z ^ chip, rows:, rows:] = part[j * strip + strip // 2 : (j + 1) * strip]
    left = aggregate_t[:, core].reshape(chips * rows, -1)
    for slot, k in ((0, 0), (1, 2 - core), (2, 1 + core), (3, 3)):
        columns = pl.ds(pl.multiple_of((e ^ k) * lanes, lanes), lanes)
        block = mul(left, dpreact[:, columns]).astype(half.dtype)
        for z in range(chips):
            half[slot, z ^ chip, :rows] = block[z * rows : (z + 1) * rows]


def window_body(place, dpreact, w_hidden_t, adjacency_t, on_link, on_chip, own):
    mem, nodes, _ = own.shape
    grid = adjacency_t.shape[1]
    first, second = sides(place[2], nodes)
    for m in range(mem):
        total = mul(dpreact[m * grid : (m + 1) * grid], w_hidden_t[...]).astype(bf16)
        on_link[m] = mul(adjacency_t[pl.ds(second, nodes)], total).astype(bf16)
        on_chip[m] = mul(adjacency_t[pl.ds(first, nodes)], total).astype(bf16)
        own[m] = mul(adjacency_t[nodes : 2 * nodes], total)


def latents_body(place, own, on_chip, on_link, total, token):
    for m in range(own.shape[0]):
        total[m] = own[m] + on_chip[m].astype(f32) + on_link[m].astype(f32)
    token[...] = jnp.zeros_like(token)


def sum_body(place, kept, received, mine, sent):
    staying = mine.shape[0]
    for k in range(kept.shape[0]):
        total = kept[k] + received[k].astype(f32)
        if k < staying:
            mine[k] = total
        else:
            sent[k - staying] = total.astype(bf16)


def chip_slots_body(place, kept, received, mine, *sent):
    count = kept.shape[1]
    for q in range(count):
        total = kept[0, q] + received[0, q].astype(f32)
        if q == 0:
            mine[...] = total
        else:
            sent[count - 1 - q][...] = total.astype(bf16)


def chip_sum_body(place, kept, *refs):
    received, out = refs[:-1], refs[-1]
    total = kept[...]
    for block in received:
        total += block[...].astype(f32)
    out[...] = total.astype(bf16)


def assemble_body(ens, place, *refs):
    pieces, (hidden, out, joined) = refs[:ens], refs[ens:]
    rows, width = hidden.shape
    lanes = width // ens
    strip = 2 * (pieces[0].shape[0] - rows)
    for k, bits in enumerate(routes(ens)):
        source = neighbour(place, bits)
        piece = pieces[k][...].astype(f32)
        hidden[:, pl.ds(pl.multiple_of(source * lanes, lanes), lanes)] = piece[:rows]
        start = pl.multiple_of(source * strip, strip)
        joined[pl.ds(start, strip // 2), :] = piece[rows:, :rows]
        joined[pl.ds(start + strip // 2, strip // 2), :] = piece[rows:, rows:]
    out[...] = joined[: out.shape[0]]


def reduced(aggregate_t, dpreact, out_part, variables, place, ens, chips, window):
    width = dpreact.shape[1]
    rows = width // (2 * chips)
    lanes = width // ens
    strip = 32 * pl.cdiv(out_part.shape[0], 32 * ens)
    aggregate_t = aggregate_t.reshape(chips, 2, rows, -1)
    block = (rows + strip // 2, lanes)

    def half(mine, kind):
        return call(
            functools.partial(half_body, ens, chips, mine), [((ens, chips) + block, kind)],
            place, dpreact, out_part, aggregate_t, flops=dpreact.size * width,
        )[0]

    received = chip_swap(half(False, bf16))
    kept = half(True, f32)
    for staying, bits in ((2, (1, 2)), (1, (2, 1))):
        shape = (staying, chips) + block
        kept, given = call(sum_body, [(shape, f32), (shape, bf16)], place, kept, received)
        received = core_swap(given, "ens", bits)
        if staying == 2:
            latents_sum = window(kept)
    kept, *given = call(
        chip_slots_body, [(block, f32)] + [(block, bf16)] * (chips - 1), place, kept, received,
        flops=10**9,
    )
    received = [core_swap(given[chips - 1 - q], "chip", (q, q)) for q in range(chips - 1, 0, -1)]
    total = call(chip_sum_body, [(block, bf16)], place, kept, *received, flops=10**9)[0]
    every = exchanged([total] * ens)
    grad_latents, token = latents_sum(total)
    hidden, out = call(
        functools.partial(assemble_body, ens), [((rows, width), f32), ((variables, rows), f32)],
        place, *every, after=[token], last=True, scratch=[pltpu.VMEM((ens * strip, rows), f32)],
    )
    return grad_latents, hidden, out.T


def reduced_any(aggregate_t, dpreact, out_part, variables):
    part = mul(aggregate_t, dpreact)
    summed = lax.psum((part, out_part[:variables].T), "ens")
    return tuple(
        lax.psum_scatter(value, "space", scatter_dimension=0, tiled=True) for value in summed
    )


def shards(latents, edge_index, edge_weight, truth, w_hidden, output_weight):
    mem, nodes, width = latents.shape
    variables, grid = truth.shape
    ens, space = lax.axis_size("ens"), lax.axis_size("space")
    chips = space // 2
    members = mem * ens
    scale = 1.0 / math.sqrt(grid * space * members)
    e, s = lax.axis_index("ens"), lax.axis_index("space")
    place = jnp.stack([e, s // 2, s % 2]).astype(jnp.int32)
    chunk = grid // ens
    w_out_t = output_weight.T

    on_link = link_swap(latents)
    on_chip = chip_swap(latents)
    rows = 8 * pl.cdiv(variables, 8)
    adjacency, adjacency_t, w_hidden_t, own, w_hidden_here, w_out_here, truth_here = call(
        functools.partial(prepare_body, ens),
        [((grid, 3 * nodes), bf16), ((3 * nodes, grid), bf16), (w_hidden.shape[::-1], bf16)]
        + [(latents.shape, bf16), (w_hidden.shape, bf16)]
        + [((rows, width), bf16), ((rows, grid), f32)],
        place, edge_index.T, edge_weight.T, w_out_t, truth, far=[latents, w_hidden],
        scratch=[pltpu.SemaphoreType.DMA((2,))],
    )
    cells = (mem, grid, width)
    partial = call(partial_body, [(cells, f32)], place, own, on_chip, adjacency)[0]
    piece = (mem * rows, chunk)
    aggregate, preact, activated, *pieces = call(
        functools.partial(forward_body, ens),
        [(cells, bf16), (cells, f32), (cells, bf16)] + [(piece, f32)] * ens,
        place, partial, on_link, adjacency, w_hidden_here, w_out_here,
        flops=2 * mem * grid * width * (nodes + width + 128),
    )
    here = exchanged(pieces)
    slope = call(slope_body, [(cells, f32)], place, preact, after=pieces)[0]
    gradients = call(
        functools.partial(loss_body, ens, scale), [(piece, bf16)] * ens, place, truth_here, *here,
        after=[slope],
    )
    dforecast = exchanged(gradients)
    aggregate_t = call(
        turn_body, [((width, mem * grid), bf16)], place, aggregate, after=gradients
    )[0]
    dpreact, out_part = call(
        functools.partial(backward_body, ens),
        [((mem * grid, width), bf16), ((rows, width), f32)],
        place, w_out_here, slope, activated, *dforecast,
        flops=4 * mem * grid * width * 128,
    )
    band = (mem, nodes, width)

    def window(*before):
        on_link, on_chip, middle = call(
            window_body, [(band, bf16)] * 2 + [(band, f32)],
            place, dpreact, w_hidden_t, adjacency_t, after=before,
            flops=2 * mem * grid * width * (width + 3 * nodes),
        )
        on_link, on_chip = link_swap(on_link), chip_swap(on_chip)

        def total(*before):
            return call(
                latents_body, [(band, f32), ((8, 128), f32)], place, middle, on_chip, on_link,
                after=before, last=True,
            )

        return total

    if width % (space * 128) == 0 and width // ens == 2 * (width // space) and ens == 4:
        return reduced(aggregate_t, dpreact, out_part, variables, place, ens, chips, window)
    return (window()()[0], *reduced_any(aggregate_t, dpreact, out_part, variables))


def solution(mesh):
    placed = (
        P("ens", "space", None),
        P("space", None),
        P("space", None),
        P(None, "space"),
        P(),
        P(),
    )
    return jax.shard_map(
        shards,
        mesh=mesh,
        in_specs=placed,
        out_specs=(P("ens", "space", None), P("space", None), P("space", None)),
        check_vma=False,
    )
```

profile of v0, /device:TPU:0, one launch (start us, length us, event | category | flops | bytes accessed | tf_op | source)
XLA Modules:
  0.0 86.4 jit_solution(15046604804024267370)
XLA Ops:
  1.1 0.7 collective-permute-start.1
  2.0 0.9 %copy-done = bf16[1024,100]{0,1:T(8,128)(2,1)S(1)} copy-done((bf16[1024,100]{0,1:T(8,128)(2,1)S(1)}, bf16[1024,100]{0,1:T(8,128)(2,1)}, u32[]{:S(2)}) %copy-start) | copy-done | bytes 204824
  2.9 0.9 %copy-done.1 = f32[100,512]{1,0:T(8,128)S(1)} copy-done((f32[100,512]{1,0:T(8,128)S(1)}, f32[100,512]{1,0:T(8,128)}, u32[]{:S(2)}) %copy-start.1) | copy-done | bytes 204824
  3.8 0.7 copy-done.2
  5.2 3.1 %shard_map.85 = (bf16[512,768]{1,0:T(8,128)(2,1)S(1)}, bf16[768,512]{1,0:T(8,128)(2,1)S(1)}, bf16[1024,1024]{1,0:T(8,128)(2,1)S(1)}, bf16[2,256,1024]{2,1,0:T(8,...) custom-call(s32[3]{0:T(128)S(1)} %pad_add_fusion.place_ref, ...), custom_call_target="tpu_custom_call" | custom-call | bytes 7667712 | tf_op jit(solution)/shard_map/pallas_call | solution.py:69
  8.4 1.8 %shard_map.86.refs_0_ = f32[2,512,1024]{2,1,0:T(8,128)S(1)} custom-call(s32[3]{0:T(128)S(1)} %pad_add_fusion.place_ref, bf16[2,256,1024]{2,1,0:T(8,128)(2,1)S(1)} %get-tuple-element.39.refs_0_, bf16[2,256,1024]{2,1,0:T(8,128)(2,1)S(1)} %collective-permute-done.refs_1_, bf16[512,768]{1,0:T(8,128)(2,1)S(1)} %get-tuple-element.40.refs_2_), custom_call_target="tpu_custom_call" | custom-call | bytes 7077888 | tf_op jit(solution)/shard_map/pallas_call | solution.py:69
  10.2 4.9 %shard_map.87 = (bf16[2,512,1024]{2,1,0:T(8,128)(2,1)S(1)}, f32[2,512,1024]{2,1,0:T(8,128)S(1)}, bf16[2,512,1024]{2,1,0:T(8,128)(2,1)S(1)}, f32[208,128]{1,0:T(8...) custom-call(s32[3]{0:T(128)S(1)} %pad_add_fusion.place_ref, ...), custom_call_target="tpu_custom_call" | custom-call | flops 2952790016 | bytes 17154048 | tf_op jit(solution)/shard_map/pallas_call | solution.py:69
  15.1 2.6 %collective-permute-start.2 = (f32[208,128]{1,0:T(8,128)S(1)}, f32[208,128]{1,0:T(8,128)S(1)}, u32[]{:S(2)}, u32[]{:S(2)}) collective-permute-start(f32[208,128]{1,0:T(8,128)S(1)} %get-tuple-element.43.refs_1_), channel_id=1, source_target_pairs={{0,8},{1,17},{2,10},{3,19},{4,12},{5,21},{6,14},{7,23},{8,0},{9,25... | collective-permute-start | bytes 319496 | tf_op jit(solution)/shard_map/ppermute | solution.py:36
  17.7 1.5 %collective-permute-start.3 = (f32[208,128]{1,0:T(8,128)S(1)}, f32[208,128]{1,0:T(8,128)S(1)}, u32[]{:S(2)}, u32[]{:S(2)}) collective-permute-start(f32[208,128]{1,0:T(8,128)S(1)} %get-tuple-element.44.refs_2_), channel_id=1, source_target_pairs={{0,16},{1,9},{2,18},{3,11},{4,20},{5,13},{6,22},{7,15},{8,24},{9,1... | collective-permute-start | bytes 319496 | tf_op jit(solution)/shard_map/ppermute | solution.py:36
  19.2 1.9 %shard_map.88.refs_0_.refs_1_ = f32[2,512,1024]{2,1,0:T(8,128)S(1)} custom-call(s32[3]{0:T(128)S(1)} %pad_add_fusion.place_ref, f32[208,128]{1,0:T(8,128)S(1)} %get-tuple-element.42.refs_0_.refs_2_, f32[208,128]{1,0:T(8,128)S(1)} %get-tuple-element.43.refs_1_, f32[208,128]{1,0:T(8,128)S(1)} %get-tuple-element.44.refs_2_, ...), custom_call_target="tpu_custom_call" | custom-call | bytes 8388608 | tf_op jit(solution)/shard_map/pallas_call | solution.py:69
  21.2 1.2 %collective-permute-done.3.refs_4_ = f32[208,128]{1,0:T(8,128)S(1)} collective-permute-done((f32[208,128]{1,0:T(8,128)S(1)}, f32[208,128]{1,0:T(8,128)S(1)}, u32[]{:S(2)}, u32[]{:S(2)}) %collective-permute-start.3) | collective-permute-done | bytes 106528 | tf_op jit(solution)/shard_map/ppermute | solution.py:36
  22.4 2.4 %collective-permute-done.4.refs_5_ = f32[208,128]{1,0:T(8,128)S(1)} collective-permute-done((f32[208,128]{1,0:T(8,128)S(1)}, f32[208,128]{1,0:T(8,128)S(1)}, u32[]{:S(2)}, u32[]{:S(2)}) %collective-permute-start.4) | collective-permute-done | bytes 106528 | tf_op jit(solution)/shard_map/ppermute | solution.py:36
  24.8 1.0 %shard_map.89 = (bf16[208,128]{1,0:T(8,128)(2,1)S(1)}, bf16[208,128]{1,0:T(8,128)(2,1)S(1)}, bf16[208,128]{1,0:T(8,128)(2,1)S(1)}, bf16[208,128]{1,0:T(8,128)(2,1)S(1)}) custom-call(s32[3]{0:T(128)S(1)} %pad_add_fusion.place_ref, f32[2,512,1024]{2,1,0:T(8,128)S(1)} %shard_map.88.refs_0_.refs_1_, f32[104,512]{1,0:T(8,128)S(1)} %get-tuple-element.48.refs_1_, ...), custom_call_target="tpu_custom_call" | custom-call | bytes 851968 | tf_op jit(solution)/shard_map/pallas_call | solution.py:69
  26.7 2.7 %collective-permute-start.7 = (bf16[208,128]{1,0:T(8,128)(2,1)S(1)}, bf16[208,128]{1,0:T(8,128)(2,1)S(1)}, u32[]{:S(2)}, u32[]{:S(2)}) collective-permute-start(bf16[208,128]{1,0:T(8,128)(2,1)S(1)} %get-tuple-element.52.refs_3_), channel_id=1, source_target_pairs={{0,24},{1,25},{2,26},{3,27},{4,28},{5,29},{6,30},{7,31},{8,16},{9,... | collective-permute-start | bytes 159752 | tf_op jit(solution)/shard_map/ppermute | solution.py:36
  29.4 1.2 %shard_map.91 = bf16[1024,1024]{1,0:T(8,128)(2,1)S(1)} custom-call(s32[3]{0:T(128)S(1)} %pad_add_fusion.place_ref, bf16[208,128]{1,0:T(8,128)(2,1)S(1)} %get-tuple-element.49.refs_3_.refs_0_, bf16[208,128]{1,0:T(8,128)(2,1)S(1)} %get-tuple-element.50.refs_1_, bf16[208,128]{1,0:T(8,128)(2,1)S(1)} %get-tuple-element.51.refs_2_, ...), custom_call_target="tpu_custom_call" | custom-call | bytes 4194304 | tf_op jit(solution)/shard_map/pallas_call | solution.py:69
  30.6 1.6 %collective-permute-done.6.refs_5_ = bf16[208,128]{1,0:T(8,128)(2,1)S(1)} collective-permute-done((bf16[208,128]{1,0:T(8,128)(2,1)S(1)}, bf16[208,128]{1,0:T(8,128)(2,1)S(1)}, u32[]{:S(2)}, u32[]{:S(2)}) %collective-permute-start.6) | collective-permute-done | bytes 53280 | tf_op jit(solution)/shard_map/ppermute | solution.py:36
  32.2 1.6 %shard_map.90 = (bf16[1024,1024]{1,0:T(8,128)(2,1)S(1)}, f32[104,1024]{1,0:T(8,128)S(1)}) custom-call(s32[3]{0:T(128)S(1)} %pad_add_fusion.place_ref, bf16[104,1024]{1,0:T(8,128)(2,1)S(1)} %get-tuple-element.38.refs_4_.refs_0_, f32[2,512,1024]{2,1,0:T(8,128)S(1)} %shard_map.88.refs_0_.refs_1_, bf16[2,512,1024]{2,1,0:T(8,128)(2,1)S(1)} %get-tuple-element.47.refs_2_, ...), custom_call_target="tpu_custom_call" | custom-call | flops 536870912 | bytes 9240576 | tf_op jit(solution)/shard_map/pallas_call | solution.py:69
  33.8 1.9 %shard_map.93 = bf16[4,4,144,256]{3,2,1,0:T(8,128)(2,1)S(1)} custom-call(s32[3]{0:T(128)S(1)} %pad_add_fusion.place_ref, bf16[1024,1024]{1,0:T(8,128)(2,1)S(1)} %get-tuple-element.53.refs_0_.refs_1_, f32[104,1024]{1,0:T(8,128)S(1)} %get-tuple-element.54.refs_1_, bf16[4,2,128,1024]{3,2,1,0:T(8,128)(2,1)S(1)} %bitcast.8), custom_call_target="tpu_custom_call" | custom-call | flops 1073741824 | bytes 5799936 | tf_op jit(solution)/shard_map/pallas_call | solution.py:69
  35.7 5.8 %collective-permute-start.8 = (bf16[4,4,144,256]{3,2,1,0:T(8,128)(2,1)S(1)}, bf16[4,4,144,256]{3,2,1,0:T(8,128)(2,1)S(1)}, u32[]{:S(2)}, u32[]{:S(2)}) collective-permute-start(bf16[4,4,144,256]{3,2,1,0:T(8,128)(2,1)S(1)} %shard_map.93), channel_id=1, source_target_pairs={{0,1},{1,0},{2,3},{3,2},{4,5},{5,4},{6,7},{7,6},{8,9},{9,8},{10,11... | collective-permute-start | bytes 3538952 | tf_op jit(solution)/shard_map/ppermute | solution.py:20
  41.5 1.9 %shard_map.92.refs_0_ = f32[4,4,144,256]{3,2,1,0:T(8,128)S(1)} custom-call(s32[3]{0:T(128)S(1)} %pad_add_fusion.place_ref, bf16[1024,1024]{1,0:T(8,128)(2,1)S(1)} %get-tuple-element.53.refs_0_.refs_1_, f32[104,1024]{1,0:T(8,128)S(1)} %get-tuple-element.54.refs_1_, bf16[4,2,128,1024]{3,2,1,0:T(8,128)(2,1)S(1)} %bitcast.9), custom_call_target="tpu_custom_call" | custom-call | flops 1073741824 | bytes 6979584 | tf_op jit(solution)/shard_map/pallas_call | solution.py:69
  44.0 0.9 %shard_map.94 = (f32[2,4,144,256]{3,2,1,0:T(8,128)S(1)}, bf16[2,4,144,256]{3,2,1,0:T(8,128)(2,1)S(1)}) custom-call(s32[3]{0:T(128)S(1)} %pad_add_fusion.place_ref, f32[4,4,144,256]{3,2,1,0:T(8,128)S(1)} %shard_map.92.refs_0_, bf16[4,4,144,256]{3,2,1,0:T(8,128)(2,1)S(1)} %collective-permute-done.8.refs_1_), custom_call_target="tpu_custom_call" | custom-call | bytes 5308416 | tf_op jit(solution)/shard_map/pallas_call | solution.py:69
  45.4 4.5 %shard_map.98 = (bf16[2,256,1024]{2,1,0:T(8,128)(2,1)S(1)}, bf16[2,256,1024]{2,1,0:T(8,128)(2,1)S(1)}, f32[2,256,1024]{2,1,0:T(8,128)S(1)}) custom-call(s32[3]{0:T(128)S(1)} %pad_add_fusion.place_ref, f32[2,4,144,256]{3,2,1,0:T(8,128)S(1)} %get-tuple-element.56.refs_0_, bf16[1024,1024]{1,0:T(8,128)(2,1)S(1)} %get-tuple-element.53.refs_0_.refs_1_, ...), custom_call_target="tpu_custom_call" | custom-call | flops 3758096384 | bytes 9175040 | tf_op jit(solution)/shard_map/pallas_call | solution.py:69
  50.2 0.7 collective-permute-start.15
  50.9 4.0 %collective-permute-done.9.refs_1_ = bf16[2,4,144,256]{3,2,1,0:T(8,128)(2,1)S(1)} collective-permute-done((bf16[2,4,144,256]{3,2,1,0:T(8,128)(2,1)S(1)}, bf16[2,4,144,256]{3,2,1,0:T(8,128)(2,1)S(1)}, u32[]{:S(2)}, u32[]{:S(2)}) %collective-permute-start.9) | collective-permute-done | bytes 589856 | tf_op jit(solution)/shard_map/ppermute | solution.py:36
  56.1 6.2 %collective-permute-done.10.refs_1_ = bf16[1,4,144,256]{3,2,1,0:T(8,128)(2,1)S(1)} collective-permute-done((bf16[1,4,144,256]{3,2,1,0:T(8,128)(2,1)S(1)}, bf16[1,4,144,256]{3,2,1,0:T(8,128)(2,1)S(1)}, u32[]{:S(2)}, u32[]{:S(2)}) %collective-permute-start.10) | collective-permute-done | bytes 294944 | tf_op jit(solution)/shard_map/ppermute | solution.py:36
  62.9 5.6 %collective-permute-start.11 = (bf16[144,256]{1,0:T(8,128)(2,1)S(1)}, bf16[144,256]{1,0:T(8,128)(2,1)S(1)}, u32[]{:S(2)}, u32[]{:S(2)}) collective-permute-start(bf16[144,256]{1,0:T(8,128)(2,1)S(1)} %get-tuple-element.61), channel_id=1, source_target_pairs={{0,6},{1,7},{2,4},{3,5},{4,2},{5,3},{6,0},{7,1},{8,14},{9,15},{10,... | collective-permute-start | bytes 221192 | tf_op jit(solution)/shard_map/ppermute | solution.py:36
  69.2 6.5 %collective-permute-done.11.refs_1_ = bf16[144,256]{1,0:T(8,128)(2,1)S(1)} collective-permute-done((bf16[144,256]{1,0:T(8,128)(2,1)S(1)}, bf16[144,256]{1,0:T(8,128)(2,1)S(1)}, u32[]{:S(2)}, u32[]{:S(2)}) %collective-permute-start.11) | collective-permute-done | bytes 73760 | tf_op jit(solution)/shard_map/ppermute | solution.py:36
  75.7 2.0 %collective-permute-done.12.refs_2_ = bf16[144,256]{1,0:T(8,128)(2,1)S(1)} collective-permute-done((bf16[144,256]{1,0:T(8,128)(2,1)S(1)}, bf16[144,256]{1,0:T(8,128)(2,1)S(1)}, u32[]{:S(2)}, u32[]{:S(2)}) %collective-permute-start.12) | collective-permute-done | bytes 73760 | tf_op jit(solution)/shard_map/ppermute | solution.py:36
  78.3 1.9 %collective-permute-start.18 = (bf16[144,256]{1,0:T(8,128)(2,1)S(1)}, bf16[144,256]{1,0:T(8,128)(2,1)S(1)}, u32[]{:S(2)}, u32[]{:S(2)}) collective-permute-start(bf16[144,256]{1,0:T(8,128)(2,1)S(1)} %shard_map.97.refs_0_.refs_1_), channel_id=1, source_target_pairs={{0,24},{1,25},{2,26},{3,27},{4,28},{5,29},{6,30},{7,31},{8,16},{9,... | collective-permute-start | bytes 221192 | tf_op jit(solution)/shard_map/ppermute | solution.py:36
  80.6 1.2 %collective-permute-start.16 = (bf16[144,256]{1,0:T(8,128)(2,1)S(1)}, bf16[144,256]{1,0:T(8,128)(2,1)S(1)}, u32[]{:S(2)}, u32[]{:S(2)}) collective-permute-start(bf16[144,256]{1,0:T(8,128)(2,1)S(1)} %shard_map.97.refs_0_.refs_1_), channel_id=1, source_target_pairs={{0,8},{1,17},{2,10},{3,19},{4,12},{5,21},{6,14},{7,23},{8,0},{9,25... | collective-permute-start | bytes 221192 | tf_op jit(solution)/shard_map/ppermute | solution.py:36
  81.9 2.1 %shard_map.99 = (f32[2,256,1024]{2,1,0:T(8,128)}, f32[8,128]{1,0:T(8,128)S(1)}) custom-call(s32[3]{0:T(128)S(1)} %pad_add_fusion.place_ref, bf16[144,256]{1,0:T(8,128)(2,1)S(1)} %shard_map.97.refs_0_.refs_1_, f32[2,256,1024]{2,1,0:T(8,128)S(1)} %get-tuple-element.66.refs_1_, bf16[2,256,1024]{2,1,0:T(8,128)(2,1)S(1)} %collective-permute-done.14.refs_2_, ...), custom_call_target="tpu_custom_call" | custom-call | bytes 6295552 | tf_op jit(solution)/shard_map/pallas_call | solution.py:69
  85.0 1.4 %shard_map.100 = (f32[128,1024]{1,0:T(8,128)}, f32[100,128]{1,0:T(8,128)}) custom-call(s32[3]{0:T(128)S(1)} %pad_add_fusion.place_ref, f32[8,128]{1,0:T(8,128)S(1)} %get-tuple-element.70.refs_0_, bf16[144,256]{1,0:T(8,128)(2,1)S(1)} %shard_map.97.refs_0_.refs_1_, bf16[144,256]{1,0:T(8,128)(2,1)S(1)} %collective-permute-done.16.refs_2_, ...), custom_call_target="tpu_custom_call" | custom-call | bytes 870400 | tf_op jit(solution)/shard_map/pallas_call | solution.py:69
  (31 shorter events, 8.0 us)
Async XLA Ops:
  0.6 7.8 %collective-permute-start = (bf16[2,256,1024]{2,1,0:T(8,128)(2,1)}, bf16[2,256,1024]{2,1,0:T(8,128)(2,1)S(1)}, u32[]{:S(2)}, u32[]{:S(2)}) collective-permute-start(bf16[2,256,1024]{2,1,0:T(8,128)(2,1)} %refs_0_.1), channel_id=1, source_target_pairs={{0,1},{1,0},{2,3},{3,2},{4,5},{5,4},{6,7},{7,6},{8,9},{9,8},{10,11... | collective-permute-start | bytes 3145736 | tf_op jit(solution)/shard_map/ppermute | solution.py:20
  1.1 9.1 %collective-permute-start.1 = (bf16[2,256,1024]{2,1,0:T(8,128)(2,1)}, bf16[2,256,1024]{2,1,0:T(8,128)(2,1)S(1)}, u32[]{:S(2)}, u32[]{:S(2)}) collective-permute-start(bf16[2,256,1024]{2,1,0:T(8,128)(2,1)} %refs_0_.1), channel_id=1, source_target_pairs={{1,2},{3,4},{5,6},{2,1},{4,3},{6,5},{9,10},{11,12},{13,14},{10,9},... | collective-permute-start | bytes 3145736 | tf_op jit(solution)/shard_map/ppermute | solution.py:26
  2.0 0.9 %copy-start = (bf16[1024,100]{0,1:T(8,128)(2,1)S(1)}, bf16[1024,100]{0,1:T(8,128)(2,1)}, u32[]{:S(2)}) copy-start(bf16[1024,100]{0,1:T(8,128)(2,1)} %param.11) | copy-start | bytes 614404
  2.9 0.9 %copy-start.1 = (f32[100,512]{1,0:T(8,128)S(1)}, f32[100,512]{1,0:T(8,128)}, u32[]{:S(2)}) copy-start(f32[100,512]{1,0:T(8,128)} %refs_5_.1) | copy-start | bytes 614404
  3.8 0.7 copy-start.2
  4.5 0.7 copy-start.3
  15.1 6.0 %collective-permute-start.2 = (f32[208,128]{1,0:T(8,128)S(1)}, f32[208,128]{1,0:T(8,128)S(1)}, u32[]{:S(2)}, u32[]{:S(2)}) collective-permute-start(f32[208,128]{1,0:T(8,128)S(1)} %get-tuple-element.43.refs_1_), channel_id=1, source_target_pairs={{0,8},{1,17},{2,10},{3,19},{4,12},{5,21},{6,14},{7,23},{8,0},{9,25... | collective-permute-start | bytes 319496 | tf_op jit(solution)/shard_map/ppermute | solution.py:36
  17.7 4.7 %collective-permute-start.3 = (f32[208,128]{1,0:T(8,128)S(1)}, f32[208,128]{1,0:T(8,128)S(1)}, u32[]{:S(2)}, u32[]{:S(2)}) collective-permute-start(f32[208,128]{1,0:T(8,128)S(1)} %get-tuple-element.44.refs_2_), channel_id=1, source_target_pairs={{0,16},{1,9},{2,18},{3,11},{4,20},{5,13},{6,22},{7,15},{8,24},{9,1... | collective-permute-start | bytes 319496 | tf_op jit(solution)/shard_map/ppermute | solution.py:36
  19.2 5.6 %collective-permute-start.4 = (f32[208,128]{1,0:T(8,128)S(1)}, f32[208,128]{1,0:T(8,128)S(1)}, u32[]{:S(2)}, u32[]{:S(2)}) collective-permute-start(f32[208,128]{1,0:T(8,128)S(1)} %get-tuple-element.45.refs_3_), channel_id=1, source_target_pairs={{0,24},{1,25},{2,26},{3,27},{4,28},{5,29},{6,30},{7,31},{8,16},{9,... | collective-permute-start | bytes 319496 | tf_op jit(solution)/shard_map/ppermute | solution.py:36
  25.9 4.7 %collective-permute-start.5 = (bf16[208,128]{1,0:T(8,128)(2,1)S(1)}, bf16[208,128]{1,0:T(8,128)(2,1)S(1)}, u32[]{:S(2)}, u32[]{:S(2)}) collective-permute-start(bf16[208,128]{1,0:T(8,128)(2,1)S(1)} %get-tuple-element.50.refs_1_), channel_id=1, source_target_pairs={{0,8},{1,17},{2,10},{3,19},{4,12},{5,21},{6,14},{7,23},{8,0},{9,25... | collective-permute-start | bytes 159752 | tf_op jit(solution)/shard_map/ppermute | solution.py:36
  26.5 5.8 %collective-permute-start.6 = (bf16[208,128]{1,0:T(8,128)(2,1)S(1)}, bf16[208,128]{1,0:T(8,128)(2,1)S(1)}, u32[]{:S(2)}, u32[]{:S(2)}) collective-permute-start(bf16[208,128]{1,0:T(8,128)(2,1)S(1)} %get-tuple-element.51.refs_2_), channel_id=1, source_target_pairs={{0,16},{1,9},{2,18},{3,11},{4,20},{5,13},{6,22},{7,15},{8,24},{9,1... | collective-permute-start | bytes 159752 | tf_op jit(solution)/shard_map/ppermute | solution.py:36
  26.7 5.5 %collective-permute-start.7 = (bf16[208,128]{1,0:T(8,128)(2,1)S(1)}, bf16[208,128]{1,0:T(8,128)(2,1)S(1)}, u32[]{:S(2)}, u32[]{:S(2)}) collective-permute-start(bf16[208,128]{1,0:T(8,128)(2,1)S(1)} %get-tuple-element.52.refs_3_), channel_id=1, source_target_pairs={{0,24},{1,25},{2,26},{3,27},{4,28},{5,29},{6,30},{7,31},{8,16},{9,... | collective-permute-start | bytes 159752 | tf_op jit(solution)/shard_map/ppermute | solution.py:36
  35.7 8.3 %collective-permute-start.8 = (bf16[4,4,144,256]{3,2,1,0:T(8,128)(2,1)S(1)}, bf16[4,4,144,256]{3,2,1,0:T(8,128)(2,1)S(1)}, u32[]{:S(2)}, u32[]{:S(2)}) collective-permute-start(bf16[4,4,144,256]{3,2,1,0:T(8,128)(2,1)S(1)} %shard_map.93), channel_id=1, source_target_pairs={{0,1},{1,0},{2,3},{3,2},{4,5},{5,4},{6,7},{7,6},{8,9},{9,8},{10,11... | collective-permute-start | bytes 3538952 | tf_op jit(solution)/shard_map/ppermute | solution.py:20
  44.9 9.9 %collective-permute-start.9 = (bf16[2,4,144,256]{3,2,1,0:T(8,128)(2,1)S(1)}, bf16[2,4,144,256]{3,2,1,0:T(8,128)(2,1)S(1)}, u32[]{:S(2)}, u32[]{:S(2)}) collective-permute-start(bf16[2,4,144,256]{3,2,1,0:T(8,128)(2,1)S(1)} %get-tuple-element.57), channel_id=1, source_target_pairs={{0,8},{1,17},{2,10},{3,19},{4,12},{5,21},{6,14},{7,23},{8,0},{9,25... | collective-permute-start | bytes 1769480 | tf_op jit(solution)/shard_map/ppermute | solution.py:36
  50.0 31.9 %collective-permute-start.14 = (bf16[2,256,1024]{2,1,0:T(8,128)(2,1)S(1)}, bf16[2,256,1024]{2,1,0:T(8,128)(2,1)S(1)}, u32[]{:S(2)}, u32[]{:S(2)}) collective-permute-start(bf16[2,256,1024]{2,1,0:T(8,128)(2,1)S(1)} %get-tuple-element.67), channel_id=1, source_target_pairs={{0,1},{1,0},{2,3},{3,2},{4,5},{5,4},{6,7},{7,6},{8,9},{9,8},{10,11... | collective-permute-start | bytes 3145736 | tf_op jit(solution)/shard_map/ppermute | solution.py:20
  50.2 31.7 %collective-permute-start.15 = (bf16[2,256,1024]{2,1,0:T(8,128)(2,1)S(1)}, bf16[2,256,1024]{2,1,0:T(8,128)(2,1)S(1)}, u32[]{:S(2)}, u32[]{:S(2)}) collective-permute-start(bf16[2,256,1024]{2,1,0:T(8,128)(2,1)S(1)} %get-tuple-element.68), channel_id=1, source_target_pairs={{1,2},{3,4},{5,6},{2,1},{4,3},{6,5},{9,10},{11,12},{13,14},{10,9},... | collective-permute-start | bytes 3145736 | tf_op jit(solution)/shard_map/ppermute | solution.py:26
  55.5 6.8 %collective-permute-start.10 = (bf16[1,4,144,256]{3,2,1,0:T(8,128)(2,1)S(1)}, bf16[1,4,144,256]{3,2,1,0:T(8,128)(2,1)S(1)}, u32[]{:S(2)}, u32[]{:S(2)}) collective-permute-start(bf16[1,4,144,256]{3,2,1,0:T(8,128)(2,1)S(1)} %get-tuple-element.59), channel_id=1, source_target_pairs={{0,16},{1,9},{2,18},{3,11},{4,20},{5,13},{6,22},{7,15},{8,24},{9,1... | collective-permute-start | bytes 884744 | tf_op jit(solution)/shard_map/ppermute | solution.py:36
  62.9 12.8 %collective-permute-start.11 = (bf16[144,256]{1,0:T(8,128)(2,1)S(1)}, bf16[144,256]{1,0:T(8,128)(2,1)S(1)}, u32[]{:S(2)}, u32[]{:S(2)}) collective-permute-start(bf16[144,256]{1,0:T(8,128)(2,1)S(1)} %get-tuple-element.61), channel_id=1, source_target_pairs={{0,6},{1,7},{2,4},{3,5},{4,2},{5,3},{6,0},{7,1},{8,14},{9,15},{10,... | collective-permute-start | bytes 221192 | tf_op jit(solution)/shard_map/ppermute | solution.py:36
  68.5 9.2 %collective-permute-start.12 = (bf16[144,256]{1,0:T(8,128)(2,1)S(1)}, bf16[144,256]{1,0:T(8,128)(2,1)S(1)}, u32[]{:S(2)}, u32[]{:S(2)}) collective-permute-start(bf16[144,256]{1,0:T(8,128)(2,1)S(1)} %get-tuple-element.62), channel_id=1, source_target_pairs={{0,4},{1,5},{2,6},{3,7},{4,0},{5,1},{6,2},{7,3},{8,12},{9,13},{10,... | collective-permute-start | bytes 221192 | tf_op jit(solution)/shard_map/ppermute | solution.py:36
  68.8 8.9 %collective-permute-start.13 = (bf16[144,256]{1,0:T(8,128)(2,1)S(1)}, bf16[144,256]{1,0:T(8,128)(2,1)S(1)}, u32[]{:S(2)}, u32[]{:S(2)}) collective-permute-start(bf16[144,256]{1,0:T(8,128)(2,1)S(1)} %get-tuple-element.63), channel_id=1, source_target_pairs={{0,2},{1,3},{2,0},{3,1},{4,6},{5,7},{6,4},{7,5},{8,10},{9,11},{10,... | collective-permute-start | bytes 221192 | tf_op jit(solution)/shard_map/ppermute | solution.py:36
  78.3 5.7 %collective-permute-start.18 = (bf16[144,256]{1,0:T(8,128)(2,1)S(1)}, bf16[144,256]{1,0:T(8,128)(2,1)S(1)}, u32[]{:S(2)}, u32[]{:S(2)}) collective-permute-start(bf16[144,256]{1,0:T(8,128)(2,1)S(1)} %shard_map.97.refs_0_.refs_1_), channel_id=1, source_target_pairs={{0,24},{1,25},{2,26},{3,27},{4,28},{5,29},{6,30},{7,31},{8,16},{9,... | collective-permute-start | bytes 221192 | tf_op jit(solution)/shard_map/ppermute | solution.py:36
  80.2 4.4 %collective-permute-start.17 = (bf16[144,256]{1,0:T(8,128)(2,1)S(1)}, bf16[144,256]{1,0:T(8,128)(2,1)S(1)}, u32[]{:S(2)}, u32[]{:S(2)}) collective-permute-start(bf16[144,256]{1,0:T(8,128)(2,1)S(1)} %shard_map.97.refs_0_.refs_1_), channel_id=1, source_target_pairs={{0,16},{1,9},{2,18},{3,11},{4,20},{5,13},{6,22},{7,15},{8,24},{9,1... | collective-permute-start | bytes 221192 | tf_op jit(solution)/shard_map/ppermute | solution.py:36
  80.6 4.4 %collective-permute-start.16 = (bf16[144,256]{1,0:T(8,128)(2,1)S(1)}, bf16[144,256]{1,0:T(8,128)(2,1)S(1)}, u32[]{:S(2)}, u32[]{:S(2)}) collective-permute-start(bf16[144,256]{1,0:T(8,128)(2,1)S(1)} %shard_map.97.refs_0_.refs_1_), channel_id=1, source_target_pairs={{0,8},{1,17},{2,10},{3,19},{4,12},{5,21},{6,14},{7,23},{8,0},{9,25... | collective-permute-start | bytes 221192 | tf_op jit(solution)/shard_map/ppermute | solution.py:36
where the time goes:
time: 86.7 us; the launch traced here: 86.4 us
  Pallas kernels  30.1 us (35%)
  starting transfers between devices  26.6 us (31%)
  waiting for transfers between devices  25.6 us (30%)
  local copies, waits for them, and re-layouts  3.26 us (4%)
    pallas_call x16, Pallas kernels, call(): pl.pallas_call(kernel, out_shape=[jax.ShapeDtypeStruct(shape, kind) if la...  30.1 us
    ppermute x14, waiting for transfers between devices, core_swap(): lax.ppermute(value, ('ens', 'space'), [(e * space + s, partner(e, s)) for...  25 us
    ppermute x14, starting transfers between devices, core_swap(): lax.ppermute(value, ('ens', 'space'), [(e * space + s, partner(e, s)) for...  18.6 us
    ppermute x3, starting transfers between devices, chip_swap(): return lax.ppermute(value, 'space', [(i, i ^ 1) for i in range(count)])  6.52 us
    unnamed x8, local copies, waits for them, and re-layouts  3.26 us
  transfers between devices with their start and end apart: 19, of which 10 were waited for; matrix products, arithmetic and copies ran while one was open for 0% of the time, Pallas kernels for 21%

commit v1 on v0

--- a/solution.py
+++ b/solution.py
@@ -102,6 +102,8 @@
 
 
 def padded(value, rows):
+    if value.shape[0] == rows:
+        return value
     zeros = jnp.zeros((rows - value.shape[0], value.shape[1]), value.dtype)
     return jnp.concatenate([value, zeros], axis=0)
 
@@ -229,32 +231,61 @@
         dpreact[m * grid : (m + 1) * grid] = (dactivated * slope[m]).astype(bf16)
         part = mul(gradient, activated[m])
         out_total = part if out_total is None else out_total + part
-    out_part[...] = out_total
-
-
-def slot_of(core, k):
-    return jnp.where(k == 1 + core, 2, jnp.where(k == 2 - core, 1, k))
-
-
-def half_body(ens, chips, mine, place, dpreact, out_part, aggregate_t, half):
-    e, chip, core = place[0], place[1], place[2]
-    core = core if mine else 1 - core
+    out_part[...] = padded(out_total, out_part.shape[0])
+
+
+def gradient_blocks(ens, chips, core, slots, place, dpreact, out_part, aggregate_t, emit):
+    e, chip = place[0], place[1]
     rows = aggregate_t.shape[2]
     lanes = dpreact.shape[1] // ens
-    strip = 2 * (half.shape[2] - rows)
-    for z in range(chips):
-        columns = pl.ds(pl.multiple_of((2 * z + core) * rows, rows), rows)
-        part = padded(out_part[:, columns], ens * strip).astype(half.dtype)
-        for j in range(ens):
-            slot = slot_of(core, j ^ e)
-            half[slot, z ^ chip, rows:, :rows] = part[j * strip : j * strip + strip // 2]
-            half[slot, z ^ chip, rows:, rows:] = part[j * strip + strip // 2 : (j + 1) * strip]
+    strip = out_part.shape[0] // ens
+    half = strip // 2
     left = aggregate_t[:, core].reshape(chips * rows, -1)
-    for slot, k in ((0, 0), (1, 2 - core), (2, 1 + core), (3, 3)):
-        columns = pl.ds(pl.multiple_of((e ^ k) * lanes, lanes), lanes)
-        block = mul(left, dpreact[:, columns]).astype(half.dtype)
+    for slot in slots:
+        source = e ^ (0, 2 - core, 1 + core, 3)[slot]
+        columns = pl.ds(pl.multiple_of(source * lanes, lanes), lanes)
+        block = mul(left, dpreact[:, columns])
+        start = pl.multiple_of(source * strip, strip)
         for z in range(chips):
-            half[slot, z ^ chip, :rows] = block[z * rows : (z + 1) * rows]
+            to = z ^ chip
+            columns = pl.ds(pl.multiple_of((2 * z + core) * rows, rows), rows)
+            upper = out_part[pl.ds(start, half), columns]
+            lower = out_part[pl.ds(start + half, half), columns]
+            emit(slot, to, slice(0, rows), slice(0, lanes), block[z * rows : (z + 1) * rows])
+            emit(slot, to, slice(rows, rows + half), slice(0, rows), upper)
+            emit(slot, to, slice(rows, rows + half), slice(rows, lanes), lower)
+
+
+def backward_half_body(ens, chips, place, w_out_t, slope, activated, aggregate_t, *refs):
+    dforecast, (dpreact, out_part, half) = refs[:ens], refs[ens:]
+    backward_body(ens, place, w_out_t, slope, activated, *dforecast, dpreact, out_part)
+
+    def emit(slot, to, rows, lanes, value):
+        half[slot - 2, to, rows, lanes] = value.astype(bf16)
+
+    core = 1 - place[2]
+    gradient_blocks(ens, chips, core, (2, 3), place, dpreact, out_part, aggregate_t, emit)
+
+
+def staying_body(ens, chips, place, dpreact, out_part, aggregate_t, half, kept):
+    def emit_half(slot, to, rows, lanes, value):
+        half[slot, to, rows, lanes] = value.astype(bf16)
+
+    def emit_kept(slot, to, rows, lanes, value):
+        kept[slot, to, rows, lanes] = value
+
+    operands = place, dpreact, out_part, aggregate_t
+    gradient_blocks(ens, chips, 1 - place[2], (0, 1), *operands, emit_half)
+    gradient_blocks(ens, chips, place[2], (0, 1), *operands, emit_kept)
+
+
+def leaving_body(ens, chips, place, dpreact, out_part, aggregate_t, received, sent):
+    def emit(slot, to, rows, lanes, value):
+        total = value + received[slot - 2, to, rows, lanes].astype(f32)
+        sent[slot - 2, to, rows, lanes] = total.astype(bf16)
+
+    core = place[2]
+    gradient_blocks(ens, chips, core, (2, 3), place, dpreact, out_part, aggregate_t, emit)
 
 
 def window_body(place, dpreact, w_hidden_t, adjacency_t, on_link, on_chip, own):
@@ -274,14 +305,10 @@
     token[...] = jnp.zeros_like(token)
 
 
-def sum_body(place, kept, received, mine, sent):
-    staying = mine.shape[0]
-    for k in range(kept.shape[0]):
-        total = kept[k] + received[k].astype(f32)
-        if k < staying:
-            mine[k] = total
-        else:
-            sent[k - staying] = total.astype(bf16)
+def staying_sum_body(place, kept, from_core, from_ens, mine, sent):
+    mine[0] = kept[0] + from_core[0].astype(f32) + from_ens[0].astype(f32)
+    total = kept[1] + from_core[1].astype(f32) + from_ens[1].astype(f32)
+    sent[0] = total.astype(bf16)
 
 
 def chip_slots_body(place, kept, received, mine, *sent):
@@ -317,28 +344,40 @@
     out[...] = joined[: out.shape[0]]
 
 
-def reduced(aggregate_t, dpreact, out_part, variables, place, ens, chips, window):
-    width = dpreact.shape[1]
+def reduced(w_out_t, slope, activated, aggregate_t, dforecast, variables, place, chips, window):
+    ens = len(dforecast)
+    mem, grid, width = slope.shape
     rows = width // (2 * chips)
     lanes = width // ens
-    strip = 32 * pl.cdiv(out_part.shape[0], 32 * ens)
+    strip = 32 * pl.cdiv(variables, 32 * ens)
     aggregate_t = aggregate_t.reshape(chips, 2, rows, -1)
     block = (rows + strip // 2, lanes)
-
-    def half(mine, kind):
-        return call(
-            functools.partial(half_body, ens, chips, mine), [((ens, chips) + block, kind)],
-            place, dpreact, out_part, aggregate_t, flops=dpreact.size * width,
-        )[0]
-
-    received = chip_swap(half(False, bf16))
-    kept = half(True, f32)
-    for staying, bits in ((2, (1, 2)), (1, (2, 1))):
-        shape = (staying, chips) + block
-        kept, given = call(sum_body, [(shape, f32), (shape, bf16)], place, kept, received)
-        received = core_swap(given, "ens", bits)
-        if staying == 2:
-            latents_sum = window(kept)
+    pair = (2, chips) + block
+    flops = mem * grid * width * width
+
+    dpreact, out_part, given = call(
+        functools.partial(backward_half_body, ens, chips),
+        [((mem * grid, width), bf16), ((ens * strip, width), f32), (pair, bf16)],
+        place, w_out_t, slope, activated, aggregate_t, *dforecast,
+        flops=flops // 2 + 4 * mem * grid * width * 128,
+    )
+    leaving = chip_swap(given)
+    given, kept = call(
+        functools.partial(staying_body, ens, chips), [(pair, bf16), (pair, f32)],
+        place, dpreact, out_part, aggregate_t, flops=flops,
+    )
+    staying = chip_swap(given)
+    given = call(
+        functools.partial(leaving_body, ens, chips), [(pair, bf16)],
+        place, dpreact, out_part, aggregate_t, leaving, after=[kept], flops=flops // 2,
+    )[0]
+    received = core_swap(given, "ens", (1, 2))
+    latents_sum = window(dpreact, given)
+    shape = (1, chips) + block
+    kept, given = call(
+        staying_sum_body, [(shape, f32), (shape, bf16)], place, kept, staying, received
+    )
+    received = core_swap(given, "ens", (2, 1))
     kept, *given = call(
         chip_slots_body, [(block, f32)] + [(block, bf16)] * (chips - 1), place, kept, received,
         flops=10**9,
@@ -404,15 +443,9 @@
     aggregate_t = call(
         turn_body, [((width, mem * grid), bf16)], place, aggregate, after=gradients
     )[0]
-    dpreact, out_part = call(
-        functools.partial(backward_body, ens),
-        [((mem * grid, width), bf16), ((rows, width), f32)],
-        place, w_out_here, slope, activated, *dforecast,
-        flops=4 * mem * grid * width * 128,
-    )
     band = (mem, nodes, width)
 
-    def window(*before):
+    def window(dpreact, *before):
         on_link, on_chip, middle = call(
             window_body, [(band, bf16)] * 2 + [(band, f32)],
             place, dpreact, w_hidden_t, adjacency_t, after=before,
@@ -429,8 +462,16 @@
         return total
 
     if width % (space * 128) == 0 and width // ens == 2 * (width // space) and ens == 4:
-        return reduced(aggregate_t, dpreact, out_part, variables, place, ens, chips, window)
-    return (window()()[0], *reduced_any(aggregate_t, dpreact, out_part, variables))
+        return reduced(
+            w_out_here, slope, activated, aggregate_t, dforecast, variables, place, chips, window
+        )
+    dpreact, out_part = call(
+        functools.partial(backward_body, ens),
+        [((mem * grid, width), bf16), ((rows, width), f32)],
+        place, w_out_here, slope, activated, *dforecast,
+        flops=4 * mem * grid * width * 128,
+    )
+    return (window(dpreact)()[0], *reduced_any(aggregate_t, dpreact, out_part, variables))
 
 
 def solution(mesh):

time: 86.7 us -> 85.5 us (0.986)
    pallas_call x16 -> x15, Pallas kernels: 30.1 us -> 29.5 us  [call(): pl.pallas_call(kernel, out_shape=[jax.ShapeDtypeStruct(shape, kind) if la...]
    ppermute x3 -> x4, starting transfers between devices: 6.52 us -> 6.69 us  [chip_swap(): return lax.ppermute(value, 'space', [(i, i ^ 1) for i in range(count)])]
  transfers between devices with their start and end apart: 19 -> 20, of which waited for: 10 -> 9; matrix products, arithmetic and copies ran while one was open for 0% -> 0% of each run, Pallas kernels for 21% -> 23%
where the time goes in v1:
time: 85.5 us; the launch traced here: 85.3 us
  Pallas kernels  29.5 us (35%)
  starting transfers between devices  26.9 us (31%)
  waiting for transfers between devices  24.8 us (29%)
  local copies, waits for them, and re-layouts  3.26 us (4%)
    pallas_call x15, Pallas kernels, call(): pl.pallas_call(kernel, out_shape=[jax.ShapeDtypeStruct(shape, kind) if la...  29.5 us
    ppermute x14, waiting for transfers between devices, core_swap(): lax.ppermute(value, ('ens', 'space'), [(e * space + s, partner(e, s)) for...  24.8 us
    ppermute x14, starting transfers between devices, core_swap(): lax.ppermute(value, ('ens', 'space'), [(e * space + s, partner(e, s)) for...  18.7 us
    ppermute x4, starting transfers between devices, chip_swap(): return lax.ppermute(value, 'space', [(i, i ^ 1) for i in range(count)])  6.69 us
    unnamed x8, local copies, waits for them, and re-layouts  3.26 us
  transfers between devices with their start and end apart: 20, of which 9 were waited for; matrix products, arithmetic and copies ran while one was open for 0% of the time, Pallas kernels for 23%

profile of v1, /device:TPU:0, one launch (start us, length us, event | category | flops | bytes accessed | tf_op | source)
XLA Modules:
  0.0 85.3 jit_solution(13093249498130249021)
XLA Ops:
  1.1 0.7 collective-permute-start.1
  2.0 0.9 %copy-done = bf16[1024,100]{0,1:T(8,128)(2,1)S(1)} copy-done((bf16[1024,100]{0,1:T(8,128)(2,1)S(1)}, bf16[1024,100]{0,1:T(8,128)(2,1)}, u32[]{:S(2)}) %copy-start) | copy-done | bytes 204824
  2.9 0.9 %copy-done.1 = f32[100,512]{1,0:T(8,128)S(1)} copy-done((f32[100,512]{1,0:T(8,128)S(1)}, f32[100,512]{1,0:T(8,128)}, u32[]{:S(2)}) %copy-start.1) | copy-done | bytes 204824
  3.8 0.7 copy-done.2
  5.2 3.1 %shard_map.85 = (bf16[512,768]{1,0:T(8,128)(2,1)S(1)}, bf16[768,512]{1,0:T(8,128)(2,1)S(1)}, bf16[1024,1024]{1,0:T(8,128)(2,1)S(1)}, bf16[2,256,1024]{2,1,0:T(8,...) custom-call(s32[3]{0:T(128)S(1)} %pad_add_fusion.place_ref, ...), custom_call_target="tpu_custom_call" | custom-call | bytes 7667712 | tf_op jit(solution)/shard_map/pallas_call | solution.py:69
  8.4 1.8 %shard_map.86.refs_0_ = f32[2,512,1024]{2,1,0:T(8,128)S(1)} custom-call(s32[3]{0:T(128)S(1)} %pad_add_fusion.place_ref, bf16[2,256,1024]{2,1,0:T(8,128)(2,1)S(1)} %get-tuple-element.40.refs_0_, bf16[2,256,1024]{2,1,0:T(8,128)(2,1)S(1)} %collective-permute-done.refs_1_, bf16[512,768]{1,0:T(8,128)(2,1)S(1)} %get-tuple-element.41.refs_2_), custom_call_target="tpu_custom_call" | custom-call | bytes 7077888 | tf_op jit(solution)/shard_map/pallas_call | solution.py:69
  10.2 4.9 %shard_map.87 = (bf16[2,512,1024]{2,1,0:T(8,128)(2,1)S(1)}, f32[2,512,1024]{2,1,0:T(8,128)S(1)}, bf16[2,512,1024]{2,1,0:T(8,128)(2,1)S(1)}, f32[208,128]{1,0:T(8...) custom-call(s32[3]{0:T(128)S(1)} %pad_add_fusion.place_ref, ...), custom_call_target="tpu_custom_call" | custom-call | flops 2952790016 | bytes 17154048 | tf_op jit(solution)/shard_map/pallas_call | solution.py:69
  15.1 2.6 %collective-permute-start.2 = (f32[208,128]{1,0:T(8,128)S(1)}, f32[208,128]{1,0:T(8,128)S(1)}, u32[]{:S(2)}, u32[]{:S(2)}) collective-permute-start(f32[208,128]{1,0:T(8,128)S(1)} %get-tuple-element.44.refs_1_), channel_id=1, source_target_pairs={{0,8},{1,17},{2,10},{3,19},{4,12},{5,21},{6,14},{7,23},{8,0},{9,25... | collective-permute-start | bytes 319496 | tf_op jit(solution)/shard_map/ppermute | solution.py:36
  17.7 1.5 %collective-permute-start.3 = (f32[208,128]{1,0:T(8,128)S(1)}, f32[208,128]{1,0:T(8,128)S(1)}, u32[]{:S(2)}, u32[]{:S(2)}) collective-permute-start(f32[208,128]{1,0:T(8,128)S(1)} %get-tuple-element.45.refs_2_), channel_id=1, source_target_pairs={{0,16},{1,9},{2,18},{3,11},{4,20},{5,13},{6,22},{7,15},{8,24},{9,1... | collective-permute-start | bytes 319496 | tf_op jit(solution)/shard_map/ppermute | solution.py:36
  19.2 1.9 %shard_map.88.refs_0_.refs_1_ = f32[2,512,1024]{2,1,0:T(8,128)S(1)} custom-call(s32[3]{0:T(128)S(1)} %pad_add_fusion.place_ref, f32[208,128]{1,0:T(8,128)S(1)} %get-tuple-element.43.refs_0_.refs_2_, f32[208,128]{1,0:T(8,128)S(1)} %get-tuple-element.44.refs_1_, f32[208,128]{1,0:T(8,128)S(1)} %get-tuple-element.45.refs_2_, ...), custom_call_target="tpu_custom_call" | custom-call | bytes 8388608 | tf_op jit(solution)/shard_map/pallas_call | solution.py:69
  21.2 1.2 %collective-permute-done.3.refs_4_ = f32[208,128]{1,0:T(8,128)S(1)} collective-permute-done((f32[208,128]{1,0:T(8,128)S(1)}, f32[208,128]{1,0:T(8,128)S(1)}, u32[]{:S(2)}, u32[]{:S(2)}) %collective-permute-start.3) | collective-permute-done | bytes 106528 | tf_op jit(solution)/shard_map/ppermute | solution.py:36
  22.4 2.4 %collective-permute-done.4.refs_5_ = f32[208,128]{1,0:T(8,128)S(1)} collective-permute-done((f32[208,128]{1,0:T(8,128)S(1)}, f32[208,128]{1,0:T(8,128)S(1)}, u32[]{:S(2)}, u32[]{:S(2)}) %collective-permute-start.4) | collective-permute-done | bytes 106528 | tf_op jit(solution)/shard_map/ppermute | solution.py:36
  24.8 1.0 %shard_map.89 = (bf16[208,128]{1,0:T(8,128)(2,1)S(1)}, bf16[208,128]{1,0:T(8,128)(2,1)S(1)}, bf16[208,128]{1,0:T(8,128)(2,1)S(1)}, bf16[208,128]{1,0:T(8,128)(2,1)S(1)}) custom-call(s32[3]{0:T(128)S(1)} %pad_add_fusion.place_ref, f32[2,512,1024]{2,1,0:T(8,128)S(1)} %shard_map.88.refs_0_.refs_1_, f32[104,512]{1,0:T(8,128)S(1)} %get-tuple-element.49.refs_1_, ...), custom_call_target="tpu_custom_call" | custom-call | bytes 851968 | tf_op jit(solution)/shard_map/pallas_call | solution.py:69
  26.7 2.7 %collective-permute-start.7 = (bf16[208,128]{1,0:T(8,128)(2,1)S(1)}, bf16[208,128]{1,0:T(8,128)(2,1)S(1)}, u32[]{:S(2)}, u32[]{:S(2)}) collective-permute-start(bf16[208,128]{1,0:T(8,128)(2,1)S(1)} %get-tuple-element.53.refs_3_), channel_id=1, source_target_pairs={{0,24},{1,25},{2,26},{3,27},{4,28},{5,29},{6,30},{7,31},{8,16},{9,... | collective-permute-start | bytes 159752 | tf_op jit(solution)/shard_map/ppermute | solution.py:36
  29.4 1.2 %shard_map.90 = bf16[1024,1024]{1,0:T(8,128)(2,1)S(1)} custom-call(s32[3]{0:T(128)S(1)} %pad_add_fusion.place_ref, bf16[208,128]{1,0:T(8,128)(2,1)S(1)} %get-tuple-element.50.refs_0_.refs_4_, bf16[208,128]{1,0:T(8,128)(2,1)S(1)} %get-tuple-element.51.refs_1_, bf16[208,128]{1,0:T(8,128)(2,1)S(1)} %get-tuple-element.52.refs_2_, ...), custom_call_target="tpu_custom_call" | custom-call | bytes 4194304 | tf_op jit(solution)/shard_map/pallas_call | solution.py:69
  30.6 1.6 %collective-permute-done.6.refs_6_ = bf16[208,128]{1,0:T(8,128)(2,1)S(1)} collective-permute-done((bf16[208,128]{1,0:T(8,128)(2,1)S(1)}, bf16[208,128]{1,0:T(8,128)(2,1)S(1)}, u32[]{:S(2)}, u32[]{:S(2)}) %collective-permute-start.6) | collective-permute-done | bytes 53280 | tf_op jit(solution)/shard_map/ppermute | solution.py:36
  32.2 2.2 %shard_map.91 = (bf16[1024,1024]{1,0:T(8,128)(2,1)S(1)}, f32[128,1024]{1,0:T(8,128)S(1)}, bf16[2,4,144,256]{3,2,1,0:T(8,128)(2,1)S(1)}) custom-call(s32[3]{0:T(128)S(1)} %pad_add_fusion.place_ref, bf16[104,1024]{1,0:T(8,128)(2,1)S(1)} %get-tuple-element.39.refs_4_.refs_0_, f32[2,512,1024]{2,1,0:T(8,128)S(1)} %shard_map.88.refs_0_.refs_1_, ...), custom_call_target="tpu_custom_call" | custom-call | flops 1073741824 | bytes 12025856 | tf_op jit(solution)/shard_map/pallas_call | solution.py:69
  34.4 5.8 %collective-permute-start.9 = (bf16[2,4,144,256]{3,2,1,0:T(8,128)(2,1)S(1)}, bf16[2,4,144,256]{3,2,1,0:T(8,128)(2,1)S(1)}, u32[]{:S(2)}, u32[]{:S(2)}) collective-permute-start(bf16[2,4,144,256]{3,2,1,0:T(8,128)(2,1)S(1)} %get-tuple-element.59), channel_id=1, source_target_pairs={{0,1},{1,0},{2,3},{3,2},{4,5},{5,4},{6,7},{7,6},{8,9},{9,8},{10,11... | collective-permute-start | bytes 1769480 | tf_op jit(solution)/shard_map/ppermute | solution.py:20
  40.2 1.9 %shard_map.92 = (bf16[2,4,144,256]{3,2,1,0:T(8,128)(2,1)S(1)}, f32[2,4,144,256]{3,2,1,0:T(8,128)S(1)}) custom-call(s32[3]{0:T(128)S(1)} %pad_add_fusion.place_ref, bf16[1024,1024]{1,0:T(8,128)(2,1)S(1)} %get-tuple-element.55.refs_0_.refs_1_, f32[128,1024]{1,0:T(8,128)S(1)} %get-tuple-element.56.refs_1_.refs_2_, bf16[4,2,128,1024]{3,2,1,0:T(8,128)(2,1)S(1)} %bitcast.9), custom_call_target="tpu_custom_call" | custom-call | flops 1073741824 | bytes 6488064 | tf_op jit(solution)/shard_map/pallas_call | solution.py:69
  42.2 1.3 %shard_map.93.refs_0_ = bf16[2,4,144,256]{3,2,1,0:T(8,128)(2,1)S(1)} custom-call(s32[3]{0:T(128)S(1)} %pad_add_fusion.place_ref, f32[2,4,144,256]{3,2,1,0:T(8,128)S(1)} %get-tuple-element.57.refs_0_, bf16[1024,1024]{1,0:T(8,128)(2,1)S(1)} %get-tuple-element.55.refs_0_.refs_1_, f32[128,1024]{1,0:T(8,128)S(1)} %get-tuple-element.56.refs_1_.refs_2_, ...), custom_call_target="tpu_custom_call" | custom-call | flops 536870912 | bytes 5898240 | tf_op jit(solution)/shard_map/pallas_call | solution.py:69
  44.0 4.7 %shard_map.97 = (bf16[2,256,1024]{2,1,0:T(8,128)(2,1)S(1)}, bf16[2,256,1024]{2,1,0:T(8,128)(2,1)S(1)}, f32[2,256,1024]{2,1,0:T(8,128)S(1)}) custom-call(s32[3]{0:T(128)S(1)} %pad_add_fusion.place_ref, bf16[2,4,144,256]{3,2,1,0:T(8,128)(2,1)S(1)} %shard_map.93.refs_0_, bf16[1024,1024]{1,0:T(8,128)(2,1)S(1)} %get-tuple-element.55.refs_0_.refs_1_, ...), custom_call_target="tpu_custom_call" | custom-call | flops 3758096384 | bytes 9175040 | tf_op jit(solution)/shard_map/pallas_call | solution.py:69
  49.0 0.7 collective-permute-start.16
  49.8 3.7 %collective-permute-done.10.refs_2_ = bf16[2,4,144,256]{3,2,1,0:T(8,128)(2,1)S(1)} collective-permute-done((bf16[2,4,144,256]{3,2,1,0:T(8,128)(2,1)S(1)}, bf16[2,4,144,256]{3,2,1,0:T(8,128)(2,1)S(1)}, u32[]{:S(2)}, u32[]{:S(2)}) %collective-permute-start.10) | collective-permute-done | bytes 589856 | tf_op jit(solution)/shard_map/ppermute | solution.py:36
  53.4 0.7 shard_map.94
  54.7 6.2 %collective-permute-done.11.refs_1_ = bf16[1,4,144,256]{3,2,1,0:T(8,128)(2,1)S(1)} collective-permute-done((bf16[1,4,144,256]{3,2,1,0:T(8,128)(2,1)S(1)}, bf16[1,4,144,256]{3,2,1,0:T(8,128)(2,1)S(1)}, u32[]{:S(2)}, u32[]{:S(2)}) %collective-permute-start.11) | collective-permute-done | bytes 294944 | tf_op jit(solution)/shard_map/ppermute | solution.py:36
  61.6 5.8 %collective-permute-start.12 = (bf16[144,256]{1,0:T(8,128)(2,1)S(1)}, bf16[144,256]{1,0:T(8,128)(2,1)S(1)}, u32[]{:S(2)}, u32[]{:S(2)}) collective-permute-start(bf16[144,256]{1,0:T(8,128)(2,1)S(1)} %get-tuple-element.63), channel_id=1, source_target_pairs={{0,6},{1,7},{2,4},{3,5},{4,2},{5,3},{6,0},{7,1},{8,14},{9,15},{10,... | collective-permute-start | bytes 221192 | tf_op jit(solution)/shard_map/ppermute | solution.py:36
  68.0 6.6 %collective-permute-done.12.refs_1_ = bf16[144,256]{1,0:T(8,128)(2,1)S(1)} collective-permute-done((bf16[144,256]{1,0:T(8,128)(2,1)S(1)}, bf16[144,256]{1,0:T(8,128)(2,1)S(1)}, u32[]{:S(2)}, u32[]{:S(2)}) %collective-permute-start.12) | collective-permute-done | bytes 73760 | tf_op jit(solution)/shard_map/ppermute | solution.py:36
  74.6 2.0 %collective-permute-done.13.refs_2_ = bf16[144,256]{1,0:T(8,128)(2,1)S(1)} collective-permute-done((bf16[144,256]{1,0:T(8,128)(2,1)S(1)}, bf16[144,256]{1,0:T(8,128)(2,1)S(1)}, u32[]{:S(2)}, u32[]{:S(2)}) %collective-permute-start.13) | collective-permute-done | bytes 73760 | tf_op jit(solution)/shard_map/ppermute | solution.py:36
  77.2 1.9 %collective-permute-start.19 = (bf16[144,256]{1,0:T(8,128)(2,1)S(1)}, bf16[144,256]{1,0:T(8,128)(2,1)S(1)}, u32[]{:S(2)}, u32[]{:S(2)}) collective-permute-start(bf16[144,256]{1,0:T(8,128)(2,1)S(1)} %shard_map.96.refs_0_.refs_1_), channel_id=1, source_target_pairs={{0,24},{1,25},{2,26},{3,27},{4,28},{5,29},{6,30},{7,31},{8,16},{9,... | collective-permute-start | bytes 221192 | tf_op jit(solution)/shard_map/ppermute | solution.py:36
  79.5 1.2 %collective-permute-start.17 = (bf16[144,256]{1,0:T(8,128)(2,1)S(1)}, bf16[144,256]{1,0:T(8,128)(2,1)S(1)}, u32[]{:S(2)}, u32[]{:S(2)}) collective-permute-start(bf16[144,256]{1,0:T(8,128)(2,1)S(1)} %shard_map.96.refs_0_.refs_1_), channel_id=1, source_target_pairs={{0,8},{1,17},{2,10},{3,19},{4,12},{5,21},{6,14},{7,23},{8,0},{9,25... | collective-permute-start | bytes 221192 | tf_op jit(solution)/shard_map/ppermute | solution.py:36
  80.7 2.2 %shard_map.98 = (f32[2,256,1024]{2,1,0:T(8,128)}, f32[8,128]{1,0:T(8,128)S(1)}) custom-call(s32[3]{0:T(128)S(1)} %pad_add_fusion.place_ref, bf16[144,256]{1,0:T(8,128)(2,1)S(1)} %shard_map.96.refs_0_.refs_1_, f32[2,256,1024]{2,1,0:T(8,128)S(1)} %get-tuple-element.68.refs_1_, bf16[2,256,1024]{2,1,0:T(8,128)(2,1)S(1)} %collective-permute-done.15.refs_2_, ...), custom_call_target="tpu_custom_call" | custom-call | bytes 6295552 | tf_op jit(solution)/shard_map/pallas_call | solution.py:69
  83.9 1.4 %shard_map.99 = (f32[128,1024]{1,0:T(8,128)}, f32[100,128]{1,0:T(8,128)}) custom-call(s32[3]{0:T(128)S(1)} %pad_add_fusion.place_ref, f32[8,128]{1,0:T(8,128)S(1)} %get-tuple-element.72.refs_0_, bf16[144,256]{1,0:T(8,128)(2,1)S(1)} %shard_map.96.refs_0_.refs_1_, bf16[144,256]{1,0:T(8,128)(2,1)S(1)} %collective-permute-done.17.refs_2_, ...), custom_call_target="tpu_custom_call" | custom-call | bytes 870400 | tf_op jit(solution)/shard_map/pallas_call | solution.py:69
  (32 shorter events, 6.9 us)
Async XLA Ops:
  0.6 7.8 %collective-permute-start = (bf16[2,256,1024]{2,1,0:T(8,128)(2,1)}, bf16[2,256,1024]{2,1,0:T(8,128)(2,1)S(1)}, u32[]{:S(2)}, u32[]{:S(2)}) collective-permute-start(bf16[2,256,1024]{2,1,0:T(8,128)(2,1)} %refs_0_.1), channel_id=1, source_target_pairs={{0,1},{1,0},{2,3},{3,2},{4,5},{5,4},{6,7},{7,6},{8,9},{9,8},{10,11... | collective-permute-start | bytes 3145736 | tf_op jit(solution)/shard_map/ppermute | solution.py:20
  1.1 9.0 %collective-permute-start.1 = (bf16[2,256,1024]{2,1,0:T(8,128)(2,1)}, bf16[2,256,1024]{2,1,0:T(8,128)(2,1)S(1)}, u32[]{:S(2)}, u32[]{:S(2)}) collective-permute-start(bf16[2,256,1024]{2,1,0:T(8,128)(2,1)} %refs_0_.1), channel_id=1, source_target_pairs={{1,2},{3,4},{5,6},{2,1},{4,3},{6,5},{9,10},{11,12},{13,14},{10,9},... | collective-permute-start | bytes 3145736 | tf_op jit(solution)/shard_map/ppermute | solution.py:26
  2.0 0.9 %copy-start = (bf16[1024,100]{0,1:T(8,128)(2,1)S(1)}, bf16[1024,100]{0,1:T(8,128)(2,1)}, u32[]{:S(2)}) copy-start(bf16[1024,100]{0,1:T(8,128)(2,1)} %param.11) | copy-start | bytes 614404
  2.9 0.9 %copy-start.1 = (f32[100,512]{1,0:T(8,128)S(1)}, f32[100,512]{1,0:T(8,128)}, u32[]{:S(2)}) copy-start(f32[100,512]{1,0:T(8,128)} %refs_5_.1) | copy-start | bytes 614404
  3.8 0.7 copy-start.2
  4.5 0.7 copy-start.3
  15.1 6.0 %collective-permute-start.2 = (f32[208,128]{1,0:T(8,128)S(1)}, f32[208,128]{1,0:T(8,128)S(1)}, u32[]{:S(2)}, u32[]{:S(2)}) collective-permute-start(f32[208,128]{1,0:T(8,128)S(1)} %get-tuple-element.44.refs_1_), channel_id=1, source_target_pairs={{0,8},{1,17},{2,10},{3,19},{4,12},{5,21},{6,14},{7,23},{8,0},{9,25... | collective-permute-start | bytes 319496 | tf_op jit(solution)/shard_map/ppermute | solution.py:36
  17.7 4.7 %collective-permute-start.3 = (f32[208,128]{1,0:T(8,128)S(1)}, f32[208,128]{1,0:T(8,128)S(1)}, u32[]{:S(2)}, u32[]{:S(2)}) collective-permute-start(f32[208,128]{1,0:T(8,128)S(1)} %get-tuple-element.45.refs_2_), channel_id=1, source_target_pairs={{0,16},{1,9},{2,18},{3,11},{4,20},{5,13},{6,22},{7,15},{8,24},{9,1... | collective-permute-start | bytes 319496 | tf_op jit(solution)/shard_map/ppermute | solution.py:36
  19.2 5.6 %collective-permute-start.4 = (f32[208,128]{1,0:T(8,128)S(1)}, f32[208,128]{1,0:T(8,128)S(1)}, u32[]{:S(2)}, u32[]{:S(2)}) collective-permute-start(f32[208,128]{1,0:T(8,128)S(1)} %get-tuple-element.46.refs_3_), channel_id=1, source_target_pairs={{0,24},{1,25},{2,26},{3,27},{4,28},{5,29},{6,30},{7,31},{8,16},{9,... | collective-permute-start | bytes 319496 | tf_op jit(solution)/shard_map/ppermute | solution.py:36
  25.9 4.7 %collective-permute-start.5 = (bf16[208,128]{1,0:T(8,128)(2,1)S(1)}, bf16[208,128]{1,0:T(8,128)(2,1)S(1)}, u32[]{:S(2)}, u32[]{:S(2)}) collective-permute-start(bf16[208,128]{1,0:T(8,128)(2,1)S(1)} %get-tuple-element.51.refs_1_), channel_id=1, source_target_pairs={{0,8},{1,17},{2,10},{3,19},{4,12},{5,21},{6,14},{7,23},{8,0},{9,25... | collective-permute-start | bytes 159752 | tf_op jit(solution)/shard_map/ppermute | solution.py:36
  26.5 5.8 %collective-permute-start.6 = (bf16[208,128]{1,0:T(8,128)(2,1)S(1)}, bf16[208,128]{1,0:T(8,128)(2,1)S(1)}, u32[]{:S(2)}, u32[]{:S(2)}) collective-permute-start(bf16[208,128]{1,0:T(8,128)(2,1)S(1)} %get-tuple-element.52.refs_2_), channel_id=1, source_target_pairs={{0,16},{1,9},{2,18},{3,11},{4,20},{5,13},{6,22},{7,15},{8,24},{9,1... | collective-permute-start | bytes 159752 | tf_op jit(solution)/shard_map/ppermute | solution.py:36
  26.7 5.5 %collective-permute-start.7 = (bf16[208,128]{1,0:T(8,128)(2,1)S(1)}, bf16[208,128]{1,0:T(8,128)(2,1)S(1)}, u32[]{:S(2)}, u32[]{:S(2)}) collective-permute-start(bf16[208,128]{1,0:T(8,128)(2,1)S(1)} %get-tuple-element.53.refs_3_), channel_id=1, source_target_pairs={{0,24},{1,25},{2,26},{3,27},{4,28},{5,29},{6,30},{7,31},{8,16},{9,... | collective-permute-start | bytes 159752 | tf_op jit(solution)/shard_map/ppermute | solution.py:36
  34.4 7.8 %collective-permute-start.9 = (bf16[2,4,144,256]{3,2,1,0:T(8,128)(2,1)S(1)}, bf16[2,4,144,256]{3,2,1,0:T(8,128)(2,1)S(1)}, u32[]{:S(2)}, u32[]{:S(2)}) collective-permute-start(bf16[2,4,144,256]{3,2,1,0:T(8,128)(2,1)S(1)} %get-tuple-element.59), channel_id=1, source_target_pairs={{0,1},{1,0},{2,3},{3,2},{4,5},{5,4},{6,7},{7,6},{8,9},{9,8},{10,11... | collective-permute-start | bytes 1769480 | tf_op jit(solution)/shard_map/ppermute | solution.py:20
  42.1 7.7 %collective-permute-start.8 = (bf16[2,4,144,256]{3,2,1,0:T(8,128)(2,1)S(1)}, bf16[2,4,144,256]{3,2,1,0:T(8,128)(2,1)S(1)}, u32[]{:S(2)}, u32[]{:S(2)}) collective-permute-start(bf16[2,4,144,256]{3,2,1,0:T(8,128)(2,1)S(1)} %get-tuple-element.58), channel_id=1, source_target_pairs={{0,1},{1,0},{2,3},{3,2},{4,5},{5,4},{6,7},{7,6},{8,9},{9,8},{10,11... | collective-permute-start | bytes 1769480 | tf_op jit(solution)/shard_map/ppermute | solution.py:20
  43.5 9.9 %collective-permute-start.10 = (bf16[2,4,144,256]{3,2,1,0:T(8,128)(2,1)S(1)}, bf16[2,4,144,256]{3,2,1,0:T(8,128)(2,1)S(1)}, u32[]{:S(2)}, u32[]{:S(2)}) collective-permute-start(bf16[2,4,144,256]{3,2,1,0:T(8,128)(2,1)S(1)} %shard_map.93.refs_0_), channel_id=1, source_target_pairs={{0,8},{1,17},{2,10},{3,19},{4,12},{5,21},{6,14},{7,23},{8,0},{9,25... | collective-permute-start | bytes 1769480 | tf_op jit(solution)/shard_map/ppermute | solution.py:36
  48.8 32.0 %collective-permute-start.15 = (bf16[2,256,1024]{2,1,0:T(8,128)(2,1)S(1)}, bf16[2,256,1024]{2,1,0:T(8,128)(2,1)S(1)}, u32[]{:S(2)}, u32[]{:S(2)}) collective-permute-start(bf16[2,256,1024]{2,1,0:T(8,128)(2,1)S(1)} %get-tuple-element.69), channel_id=1, source_target_pairs={{0,1},{1,0},{2,3},{3,2},{4,5},{5,4},{6,7},{7,6},{8,9},{9,8},{10,11... | collective-permute-start | bytes 3145736 | tf_op jit(solution)/shard_map/ppermute | solution.py:20
  49.0 31.7 %collective-permute-start.16 = (bf16[2,256,1024]{2,1,0:T(8,128)(2,1)S(1)}, bf16[2,256,1024]{2,1,0:T(8,128)(2,1)S(1)}, u32[]{:S(2)}, u32[]{:S(2)}) collective-permute-start(bf16[2,256,1024]{2,1,0:T(8,128)(2,1)S(1)} %get-tuple-element.70), channel_id=1, source_target_pairs={{1,2},{3,4},{5,6},{2,1},{4,3},{6,5},{9,10},{11,12},{13,14},{10,9},... | collective-permute-start | bytes 3145736 | tf_op jit(solution)/shard_map/ppermute | solution.py:26
  54.2 6.8 %collective-permute-start.11 = (bf16[1,4,144,256]{3,2,1,0:T(8,128)(2,1)S(1)}, bf16[1,4,144,256]{3,2,1,0:T(8,128)(2,1)S(1)}, u32[]{:S(2)}, u32[]{:S(2)}) collective-permute-start(bf16[1,4,144,256]{3,2,1,0:T(8,128)(2,1)S(1)} %get-tuple-element.61), channel_id=1, source_target_pairs={{0,16},{1,9},{2,18},{3,11},{4,20},{5,13},{6,22},{7,15},{8,24},{9,1... | collective-permute-start | bytes 884744 | tf_op jit(solution)/shard_map/ppermute | solution.py:36
  61.6 13.0 %collective-permute-start.12 = (bf16[144,256]{1,0:T(8,128)(2,1)S(1)}, bf16[144,256]{1,0:T(8,128)(2,1)S(1)}, u32[]{:S(2)}, u32[]{:S(2)}) collective-permute-start(bf16[144,256]{1,0:T(8,128)(2,1)S(1)} %get-tuple-element.63), channel_id=1, source_target_pairs={{0,6},{1,7},{2,4},{3,5},{4,2},{5,3},{6,0},{7,1},{8,14},{9,15},{10,... | collective-permute-start | bytes 221192 | tf_op jit(solution)/shard_map/ppermute | solution.py:36
  67.3 9.3 %collective-permute-start.13 = (bf16[144,256]{1,0:T(8,128)(2,1)S(1)}, bf16[144,256]{1,0:T(8,128)(2,1)S(1)}, u32[]{:S(2)}, u32[]{:S(2)}) collective-permute-start(bf16[144,256]{1,0:T(8,128)(2,1)S(1)} %get-tuple-element.64), channel_id=1, source_target_pairs={{0,4},{1,5},{2,6},{3,7},{4,0},{5,1},{6,2},{7,3},{8,12},{9,13},{10,... | collective-permute-start | bytes 221192 | tf_op jit(solution)/shard_map/ppermute | solution.py:36
  67.6 9.0 %collective-permute-start.14 = (bf16[144,256]{1,0:T(8,128)(2,1)S(1)}, bf16[144,256]{1,0:T(8,128)(2,1)S(1)}, u32[]{:S(2)}, u32[]{:S(2)}) collective-permute-start(bf16[144,256]{1,0:T(8,128)(2,1)S(1)} %get-tuple-element.65), channel_id=1, source_target_pairs={{0,2},{1,3},{2,0},{3,1},{4,6},{5,7},{6,4},{7,5},{8,10},{9,11},{10,... | collective-permute-start | bytes 221192 | tf_op jit(solution)/shard_map/ppermute | solution.py:36
  77.2 5.8 %collective-permute-start.19 = (bf16[144,256]{1,0:T(8,128)(2,1)S(1)}, bf16[144,256]{1,0:T(8,128)(2,1)S(1)}, u32[]{:S(2)}, u32[]{:S(2)}) collective-permute-start(bf16[144,256]{1,0:T(8,128)(2,1)S(1)} %shard_map.96.refs_0_.refs_1_), channel_id=1, source_target_pairs={{0,24},{1,25},{2,26},{3,27},{4,28},{5,29},{6,30},{7,31},{8,16},{9,... | collective-permute-start | bytes 221192 | tf_op jit(solution)/shard_map/ppermute | solution.py:36
  79.1 4.4 %collective-permute-start.18 = (bf16[144,256]{1,0:T(8,128)(2,1)S(1)}, bf16[144,256]{1,0:T(8,128)(2,1)S(1)}, u32[]{:S(2)}, u32[]{:S(2)}) collective-permute-start(bf16[144,256]{1,0:T(8,128)(2,1)S(1)} %shard_map.96.refs_0_.refs_1_), channel_id=1, source_target_pairs={{0,16},{1,9},{2,18},{3,11},{4,20},{5,13},{6,22},{7,15},{8,24},{9,1... | collective-permute-start | bytes 221192 | tf_op jit(solution)/shard_map/ppermute | solution.py:36
  79.5 4.4 %collective-permute-start.17 = (bf16[144,256]{1,0:T(8,128)(2,1)S(1)}, bf16[144,256]{1,0:T(8,128)(2,1)S(1)}, u32[]{:S(2)}, u32[]{:S(2)}) collective-permute-start(bf16[144,256]{1,0:T(8,128)(2,1)S(1)} %shard_map.96.refs_0_.refs_1_), channel_id=1, source_target_pairs={{0,8},{1,17},{2,10},{3,19},{4,12},{5,21},{6,14},{7,23},{8,0},{9,25... | collective-permute-start | bytes 221192 | tf_op jit(solution)/shard_map/ppermute | solution.py:36

commit v2 on v1

--- a/solution.py
+++ b/solution.py
@@ -288,20 +288,29 @@
     gradient_blocks(ens, chips, core, (2, 3), place, dpreact, out_part, aggregate_t, emit)
 
 
-def window_body(place, dpreact, w_hidden_t, adjacency_t, on_link, on_chip, own):
+def link_window_body(m, place, dpreact, w_hidden_t, adjacency_t, on_link, daggregate):
+    nodes = on_link.shape[0]
+    grid = adjacency_t.shape[1]
+    _, second = sides(place[2], nodes)
+    total = mul(dpreact[m * grid : (m + 1) * grid], w_hidden_t[...]).astype(bf16)
+    daggregate[...] = total
+    on_link[...] = mul(adjacency_t[pl.ds(second, nodes)], total).astype(bf16)
+
+
+def near_window_body(place, adjacency_t, *refs):
+    daggregates, (on_chip, own) = refs[:-2], refs[-2:]
     mem, nodes, _ = own.shape
-    grid = adjacency_t.shape[1]
-    first, second = sides(place[2], nodes)
+    first, _ = sides(place[2], nodes)
     for m in range(mem):
-        total = mul(dpreact[m * grid : (m + 1) * grid], w_hidden_t[...]).astype(bf16)
-        on_link[m] = mul(adjacency_t[pl.ds(second, nodes)], total).astype(bf16)
+        total = daggregates[m][...]
         on_chip[m] = mul(adjacency_t[pl.ds(first, nodes)], total).astype(bf16)
         own[m] = mul(adjacency_t[nodes : 2 * nodes], total)
 
 
-def latents_body(place, own, on_chip, on_link, total, token):
+def latents_body(place, own, on_chip, *refs):
+    on_link, (total, token) = refs[:-2], refs[-2:]
     for m in range(own.shape[0]):
-        total[m] = own[m] + on_chip[m].astype(f32) + on_link[m].astype(f32)
+        total[m] = own[m] + on_chip[m].astype(f32) + on_link[m][...].astype(f32)
     token[...] = jnp.zeros_like(token)
 
 
@@ -344,7 +353,10 @@
     out[...] = joined[: out.shape[0]]
 
 
-def reduced(w_out_t, slope, activated, aggregate_t, dforecast, variables, place, chips, window):
+def reduced(
+    w_out_t, slope, activated, aggregate_t, dforecast, variables, place, chips,
+    link_window, near_window,
+):
     ens = len(dforecast)
     mem, grid, width = slope.shape
     rows = width // (2 * chips)
@@ -372,18 +384,21 @@
         place, dpreact, out_part, aggregate_t, leaving, after=[kept], flops=flops // 2,
     )[0]
     received = core_swap(given, "ens", (1, 2))
-    latents_sum = window(dpreact, given)
+    parts = [link_window(0, dpreact, given)]
+    parts += [link_window(m, dpreact, parts[0][1]) for m in range(1, mem)]
+    latents_sum = near_window(parts)
     shape = (1, chips) + block
     kept, given = call(
-        staying_sum_body, [(shape, f32), (shape, bf16)], place, kept, staying, received
+        staying_sum_body, [(shape, f32), (shape, bf16)], place, kept, staying, received,
+        after=[daggregate for _, daggregate in parts],
     )
     received = core_swap(given, "ens", (2, 1))
     kept, *given = call(
         chip_slots_body, [(block, f32)] + [(block, bf16)] * (chips - 1), place, kept, received,
-        flops=10**9,
+        after=[arrived for arrived, _ in parts], flops=5 * 10**9,
     )
     received = [core_swap(given[chips - 1 - q], "chip", (q, q)) for q in range(chips - 1, 0, -1)]
-    total = call(chip_sum_body, [(block, bf16)], place, kept, *received, flops=10**9)[0]
+    total = call(chip_sum_body, [(block, bf16)], place, kept, *received, flops=5 * 10**9)[0]
     every = exchanged([total] * ens)
     grad_latents, token = latents_sum(total)
     hidden, out = call(
@@ -445,17 +460,25 @@
     )[0]
     band = (mem, nodes, width)
 
-    def window(dpreact, *before):
-        on_link, on_chip, middle = call(
-            window_body, [(band, bf16)] * 2 + [(band, f32)],
+    def link_window(m, dpreact, *before):
+        given, daggregate = call(
+            functools.partial(link_window_body, m), [(band[1:], bf16), (cells[1:], bf16)],
             place, dpreact, w_hidden_t, adjacency_t, after=before,
-            flops=2 * mem * grid * width * (width + 3 * nodes),
+            flops=2 * grid * width * (width + nodes),
         )
-        on_link, on_chip = link_swap(on_link), chip_swap(on_chip)
+        return link_swap(given), daggregate
+
+    def near_window(parts):
+        on_link, daggregates = zip(*parts)
+        on_chip, middle = call(
+            near_window_body, [(band, bf16), (band, f32)], place, adjacency_t, *daggregates,
+            after=on_link[:1], flops=4 * mem * grid * width * nodes,
+        )
+        on_chip = chip_swap(on_chip)
 
         def total(*before):
             return call(
-                latents_body, [(band, f32), ((8, 128), f32)], place, middle, on_chip, on_link,
+                latents_body, [(band, f32), ((8, 128), f32)], place, middle, on_chip, *on_link,
                 after=before, last=True,
             )
 
@@ -463,7 +486,8 @@
 
     if width % (space * 128) == 0 and width // ens == 2 * (width // space) and ens == 4:
         return reduced(
-            w_out_here, slope, activated, aggregate_t, dforecast, variables, place, chips, window
+            w_out_here, slope, activated, aggregate_t, dforecast, variables, place, chips,
+            link_window, near_window,
         )
     dpreact, out_part = call(
         functools.partial(backward_body, ens),
@@ -471,7 +495,8 @@
         place, w_out_here, slope, activated, *dforecast,
         flops=4 * mem * grid * width * 128,
     )
-    return (window(dpreact)()[0], *reduced_any(aggregate_t, dpreact, out_part, variables))
+    grad_latents = near_window([link_window(m, dpreact) for m in range(mem)])()[0]
+    return (grad_latents, *reduced_any(aggregate_t, dpreact, out_part, variables))
 
 
 def solution(mesh):

time: 85.5 us -> 85.8 us (level)
  waiting for transfers between devices: 24.8 us -> 16.3 us
  starting transfers between devices: 26.9 us -> 34.1 us
  Pallas kernels: 29.5 us -> 30.9 us
    ppermute x14, waiting for transfers between devices: 24.8 us -> 16.2 us  [core_swap(): lax.ppermute(value, ('ens', 'space'), [(e * space + s, partner(e, s)) for...]
    ppermute x4, starting transfers between devices: 6.69 us -> 12.4 us  [chip_swap(): return lax.ppermute(value, 'space', [(i, i ^ 1) for i in range(count)])]
    pallas_call x15 -> x17, Pallas kernels: 29.5 us -> 30.9 us  [call(): pl.pallas_call(kernel, out_shape=[jax.ShapeDtypeStruct(shape, kind) if la...]
    ppermute x2 -> x3, starting transfers between devices: 1.43 us -> 2.1 us  [link_swap(): return lax.ppermute(value, 'space', pairs + [(j, i) for i, j in pairs])]
  transfers between devices with their start and end apart: 20 -> 21, of which waited for: 9 -> 8; matrix products, arithmetic and copies ran while one was open for 0% -> 0% of each run, Pallas kernels for 23% -> 25%
where the time goes in v2:
time: 85.8 us; the launch traced here: 85.5 us
  starting transfers between devices  34.1 us (40%)
  Pallas kernels  30.9 us (36%)
  waiting for transfers between devices  16.3 us (19%)
  local copies, waits for them, and re-layouts  3.26 us (4%)
    pallas_call x17, Pallas kernels, call(): pl.pallas_call(kernel, out_shape=[jax.ShapeDtypeStruct(shape, kind) if la...  30.9 us
    ppermute x14, starting transfers between devices, core_swap(): lax.ppermute(value, ('ens', 'space'), [(e * space + s, partner(e, s)) for...  19.6 us
    ppermute x14, waiting for transfers between devices, core_swap(): lax.ppermute(value, ('ens', 'space'), [(e * space + s, partner(e, s)) for...  16.2 us
    ppermute x4, starting transfers between devices, chip_swap(): return lax.ppermute(value, 'space', [(i, i ^ 1) for i in range(count)])  12.4 us
    unnamed x8, local copies, waits for them, and re-layouts  3.26 us
    ppermute x3, starting transfers between devices, link_swap(): return lax.ppermute(value, 'space', pairs + [(j, i) for i, j in pairs])  2.1 us
  transfers between devices with their start and end apart: 21, of which 8 were waited for; matrix products, arithmetic and copies ran while one was open for 0% of the time, Pallas kernels for 25%

profile of v2, /device:TPU:0, one launch (start us, length us, event | category | flops | bytes accessed | tf_op | source)
XLA Modules:
  0.0 85.5 jit_solution(10564412428420254205)
XLA Ops:
  1.1 0.7 collective-permute-start.1
  2.0 0.9 %copy-done = bf16[1024,100]{0,1:T(8,128)(2,1)S(1)} copy-done((bf16[1024,100]{0,1:T(8,128)(2,1)S(1)}, bf16[1024,100]{0,1:T(8,128)(2,1)}, u32[]{:S(2)}) %copy-start) | copy-done | bytes 204824
  2.9 0.9 %copy-done.1 = f32[100,512]{1,0:T(8,128)S(1)} copy-done((f32[100,512]{1,0:T(8,128)S(1)}, f32[100,512]{1,0:T(8,128)}, u32[]{:S(2)}) %copy-start.1) | copy-done | bytes 204824
  5.2 3.1 %shard_map.85 = (bf16[512,768]{1,0:T(8,128)(2,1)S(1)}, bf16[768,512]{1,0:T(8,128)(2,1)S(1)}, bf16[1024,1024]{1,0:T(8,128)(2,1)S(1)}, bf16[2,256,1024]{2,1,0:T(8,...) custom-call(s32[3]{0:T(128)S(1)} %pad_add_fusion.place_ref, ...), custom_call_target="tpu_custom_call" | custom-call | bytes 7667712 | tf_op jit(solution)/shard_map/pallas_call | solution.py:69
  8.4 1.8 %shard_map.86.refs_0_ = f32[2,512,1024]{2,1,0:T(8,128)S(1)} custom-call(s32[3]{0:T(128)S(1)} %pad_add_fusion.place_ref, bf16[2,256,1024]{2,1,0:T(8,128)(2,1)S(1)} %get-tuple-element.43.refs_0_, bf16[2,256,1024]{2,1,0:T(8,128)(2,1)S(1)} %collective-permute-done.refs_1_, bf16[512,768]{1,0:T(8,128)(2,1)S(1)} %get-tuple-element.44.refs_2_), custom_call_target="tpu_custom_call" | custom-call | bytes 7077888 | tf_op jit(solution)/shard_map/pallas_call | solution.py:69
  10.2 4.9 %shard_map.87 = (bf16[2,512,1024]{2,1,0:T(8,128)(2,1)S(1)}, f32[2,512,1024]{2,1,0:T(8,128)S(1)}, bf16[2,512,1024]{2,1,0:T(8,128)(2,1)S(1)}, f32[208,128]{1,0:T(8...) custom-call(s32[3]{0:T(128)S(1)} %pad_add_fusion.place_ref, ...), custom_call_target="tpu_custom_call" | custom-call | flops 2952790016 | bytes 17154048 | tf_op jit(solution)/shard_map/pallas_call | solution.py:69
  15.1 2.6 %collective-permute-start.2 = (f32[208,128]{1,0:T(8,128)S(1)}, f32[208,128]{1,0:T(8,128)S(1)}, u32[]{:S(2)}, u32[]{:S(2)}) collective-permute-start(f32[208,128]{1,0:T(8,128)S(1)} %get-tuple-element.47.refs_1_), channel_id=1, source_target_pairs={{0,8},{1,17},{2,10},{3,19},{4,12},{5,21},{6,14},{7,23},{8,0},{9,25... | collective-permute-start | bytes 319496 | tf_op jit(solution)/shard_map/ppermute | solution.py:36
  17.7 1.5 %collective-permute-start.3 = (f32[208,128]{1,0:T(8,128)S(1)}, f32[208,128]{1,0:T(8,128)S(1)}, u32[]{:S(2)}, u32[]{:S(2)}) collective-permute-start(f32[208,128]{1,0:T(8,128)S(1)} %get-tuple-element.48.refs_2_), channel_id=1, source_target_pairs={{0,16},{1,9},{2,18},{3,11},{4,20},{5,13},{6,22},{7,15},{8,24},{9,1... | collective-permute-start | bytes 319496 | tf_op jit(solution)/shard_map/ppermute | solution.py:36
  19.2 1.9 %shard_map.88.refs_0_.refs_1_ = f32[2,512,1024]{2,1,0:T(8,128)S(1)} custom-call(s32[3]{0:T(128)S(1)} %pad_add_fusion.place_ref, f32[208,128]{1,0:T(8,128)S(1)} %get-tuple-element.46.refs_0_.refs_2_, f32[208,128]{1,0:T(8,128)S(1)} %get-tuple-element.47.refs_1_, f32[208,128]{1,0:T(8,128)S(1)} %get-tuple-element.48.refs_2_, ...), custom_call_target="tpu_custom_call" | custom-call | bytes 8388608 | tf_op jit(solution)/shard_map/pallas_call | solution.py:69
  21.2 1.2 %collective-permute-done.3.refs_4_ = f32[208,128]{1,0:T(8,128)S(1)} collective-permute-done((f32[208,128]{1,0:T(8,128)S(1)}, f32[208,128]{1,0:T(8,128)S(1)}, u32[]{:S(2)}, u32[]{:S(2)}) %collective-permute-start.3) | collective-permute-done | bytes 106528 | tf_op jit(solution)/shard_map/ppermute | solution.py:36
  22.4 2.4 %collective-permute-done.4.refs_5_ = f32[208,128]{1,0:T(8,128)S(1)} collective-permute-done((f32[208,128]{1,0:T(8,128)S(1)}, f32[208,128]{1,0:T(8,128)S(1)}, u32[]{:S(2)}, u32[]{:S(2)}) %collective-permute-start.4) | collective-permute-done | bytes 106528 | tf_op jit(solution)/shard_map/ppermute | solution.py:36
  24.8 1.0 %shard_map.89 = (bf16[208,128]{1,0:T(8,128)(2,1)S(1)}, bf16[208,128]{1,0:T(8,128)(2,1)S(1)}, bf16[208,128]{1,0:T(8,128)(2,1)S(1)}, bf16[208,128]{1,0:T(8,128)(2,1)S(1)}) custom-call(s32[3]{0:T(128)S(1)} %pad_add_fusion.place_ref, f32[2,512,1024]{2,1,0:T(8,128)S(1)} %shard_map.88.refs_0_.refs_1_, f32[104,512]{1,0:T(8,128)S(1)} %get-tuple-element.52.refs_1_, ...), custom_call_target="tpu_custom_call" | custom-call | bytes 851968 | tf_op jit(solution)/shard_map/pallas_call | solution.py:69
  26.7 2.7 %collective-permute-start.7 = (bf16[208,128]{1,0:T(8,128)(2,1)S(1)}, bf16[208,128]{1,0:T(8,128)(2,1)S(1)}, u32[]{:S(2)}, u32[]{:S(2)}) collective-permute-start(bf16[208,128]{1,0:T(8,128)(2,1)S(1)} %get-tuple-element.56.refs_3_), channel_id=1, source_target_pairs={{0,24},{1,25},{2,26},{3,27},{4,28},{5,29},{6,30},{7,31},{8,16},{9,... | collective-permute-start | bytes 159752 | tf_op jit(solution)/shard_map/ppermute | solution.py:36
  29.4 1.2 %shard_map.90 = bf16[1024,1024]{1,0:T(8,128)(2,1)S(1)} custom-call(s32[3]{0:T(128)S(1)} %pad_add_fusion.place_ref, bf16[208,128]{1,0:T(8,128)(2,1)S(1)} %get-tuple-element.53.refs_0_.refs_4_, bf16[208,128]{1,0:T(8,128)(2,1)S(1)} %get-tuple-element.54.refs_1_, bf16[208,128]{1,0:T(8,128)(2,1)S(1)} %get-tuple-element.55.refs_2_, ...), custom_call_target="tpu_custom_call" | custom-call | bytes 4194304 | tf_op jit(solution)/shard_map/pallas_call | solution.py:69
  30.6 1.6 %collective-permute-done.6.refs_6_ = bf16[208,128]{1,0:T(8,128)(2,1)S(1)} collective-permute-done((bf16[208,128]{1,0:T(8,128)(2,1)S(1)}, bf16[208,128]{1,0:T(8,128)(2,1)S(1)}, u32[]{:S(2)}, u32[]{:S(2)}) %collective-permute-start.6) | collective-permute-done | bytes 53280 | tf_op jit(solution)/shard_map/ppermute | solution.py:36
  32.2 2.2 %shard_map.91 = (bf16[1024,1024]{1,0:T(8,128)(2,1)S(1)}, f32[128,1024]{1,0:T(8,128)S(1)}, bf16[2,4,144,256]{3,2,1,0:T(8,128)(2,1)S(1)}) custom-call(s32[3]{0:T(128)S(1)} %pad_add_fusion.place_ref, bf16[104,1024]{1,0:T(8,128)(2,1)S(1)} %get-tuple-element.42.refs_4_.refs_0_, f32[2,512,1024]{2,1,0:T(8,128)S(1)} %shard_map.88.refs_0_.refs_1_, ...), custom_call_target="tpu_custom_call" | custom-call | flops 1073741824 | bytes 12025856 | tf_op jit(solution)/shard_map/pallas_call | solution.py:69
  34.4 5.8 %collective-permute-start.8 = (bf16[2,4,144,256]{3,2,1,0:T(8,128)(2,1)S(1)}, bf16[2,4,144,256]{3,2,1,0:T(8,128)(2,1)S(1)}, u32[]{:S(2)}, u32[]{:S(2)}) collective-permute-start(bf16[2,4,144,256]{3,2,1,0:T(8,128)(2,1)S(1)} %get-tuple-element.61), channel_id=1, source_target_pairs={{0,1},{1,0},{2,3},{3,2},{4,5},{5,4},{6,7},{7,6},{8,9},{9,8},{10,11... | collective-permute-start | bytes 1769480 | tf_op jit(solution)/shard_map/ppermute | solution.py:20
  40.2 1.9 %shard_map.92 = (bf16[2,4,144,256]{3,2,1,0:T(8,128)(2,1)S(1)}, f32[2,4,144,256]{3,2,1,0:T(8,128)S(1)}) custom-call(s32[3]{0:T(128)S(1)} %pad_add_fusion.place_ref, bf16[1024,1024]{1,0:T(8,128)(2,1)S(1)} %get-tuple-element.58.refs_0_.refs_1_, f32[128,1024]{1,0:T(8,128)S(1)} %get-tuple-element.59.refs_1_.refs_2_, bf16[4,2,128,1024]{3,2,1,0:T(8,128)(2,1)S(1)} %bitcast.9), custom_call_target="tpu_custom_call" | custom-call | flops 1073741824 | bytes 6488064 | tf_op jit(solution)/shard_map/pallas_call | solution.py:69
  42.2 1.3 %shard_map.93.refs_0_ = bf16[2,4,144,256]{3,2,1,0:T(8,128)(2,1)S(1)} custom-call(s32[3]{0:T(128)S(1)} %pad_add_fusion.place_ref, f32[2,4,144,256]{3,2,1,0:T(8,128)S(1)} %get-tuple-element.60.refs_0_.refs_2_, bf16[1024,1024]{1,0:T(8,128)(2,1)S(1)} %get-tuple-element.58.refs_0_.refs_1_, f32[128,1024]{1,0:T(8,128)S(1)} %get-tuple-element.59.refs_1_.refs_2_, ...), custom_call_target="tpu_custom_call" | custom-call | flops 536870912 | bytes 5898240 | tf_op jit(solution)/shard_map/pallas_call | solution.py:69
  44.0 2.3 %shard_map.94 = (bf16[256,1024]{1,0:T(8,128)(2,1)S(1)}, bf16[512,1024]{1,0:T(8,128)(2,1)S(1)}) custom-call(s32[3]{0:T(128)S(1)} %pad_add_fusion.place_ref, bf16[2,4,144,256]{3,2,1,0:T(8,128)(2,1)S(1)} %shard_map.93.refs_0_, bf16[1024,1024]{1,0:T(8,128)(2,1)S(1)} %get-tuple-element.58.refs_0_.refs_1_, bf16[1024,1024]{1,0:T(8,128)(2,1)S(1)} %get-tuple-element.62.refs_2_, ...), custom_call_target="tpu_custom_call" | custom-call | flops 1342177280 | bytes 6553600 | tf_op jit(solution)/shard_map/pallas_call | solution.py:69
  47.0 2.1 %shard_map.95 = (bf16[256,1024]{1,0:T(8,128)(2,1)S(1)}, bf16[512,1024]{1,0:T(8,128)(2,1)S(1)}) custom-call(s32[3]{0:T(128)S(1)} %pad_add_fusion.place_ref, bf16[512,1024]{1,0:T(8,128)(2,1)S(1)} %get-tuple-element.65.refs_0_.refs_2_, bf16[1024,1024]{1,0:T(8,128)(2,1)S(1)} %get-tuple-element.58.refs_0_.refs_1_, ...), custom_call_target="tpu_custom_call" | custom-call | flops 1342177280 | bytes 6553600 | tf_op jit(solution)/shard_map/pallas_call | solution.py:69
  49.8 3.6 %collective-permute-done.12.refs_4_ = bf16[2,4,144,256]{3,2,1,0:T(8,128)(2,1)S(1)} collective-permute-done((bf16[2,4,144,256]{3,2,1,0:T(8,128)(2,1)S(1)}, bf16[2,4,144,256]{3,2,1,0:T(8,128)(2,1)S(1)}, u32[]{:S(2)}, u32[]{:S(2)}) %collective-permute-start.12) | collective-permute-done | bytes 589856 | tf_op jit(solution)/shard_map/ppermute | solution.py:36
  53.4 0.7 shard_map.96
  54.7 1.8 %shard_map.99 = (bf16[2,256,1024]{2,1,0:T(8,128)(2,1)S(1)}, f32[2,256,1024]{2,1,0:T(8,128)S(1)}) custom-call(s32[3]{0:T(128)S(1)} %pad_add_fusion.place_ref, bf16[256,1024]{1,0:T(8,128)(2,1)S(1)} %collective-permute-done.9.refs_0_.refs_3_, bf16[768,512]{1,0:T(8,128)(2,1)S(1)} %get-tuple-element.63.refs_3_.refs_1_, ...), custom_call_target="tpu_custom_call" | custom-call | flops 1073741824 | bytes 6029312 | tf_op jit(solution)/shard_map/pallas_call | solution.py:69
  56.5 6.0 %collective-permute-start.17 = (bf16[2,256,1024]{2,1,0:T(8,128)(2,1)S(1)}, bf16[2,256,1024]{2,1,0:T(8,128)(2,1)S(1)}, u32[]{:S(2)}, u32[]{:S(2)}) collective-permute-start(bf16[2,256,1024]{2,1,0:T(8,128)(2,1)S(1)} %get-tuple-element.76), channel_id=1, source_target_pairs={{0,1},{1,0},{2,3},{3,2},{4,5},{5,4},{6,7},{7,6},{8,9},{9,8},{10,11... | collective-permute-start | bytes 3145736 | tf_op jit(solution)/shard_map/ppermute | solution.py:20
  63.2 6.6 %collective-permute-start.14 = (bf16[144,256]{1,0:T(8,128)(2,1)S(1)}, bf16[144,256]{1,0:T(8,128)(2,1)S(1)}, u32[]{:S(2)}, u32[]{:S(2)}) collective-permute-start(bf16[144,256]{1,0:T(8,128)(2,1)S(1)} %get-tuple-element.72), channel_id=1, source_target_pairs={{0,6},{1,7},{2,4},{3,5},{4,2},{5,3},{6,0},{7,1},{8,14},{9,15},{10,... | collective-permute-start | bytes 221192 | tf_op jit(solution)/shard_map/ppermute | solution.py:36
  70.4 2.6 %collective-permute-done.14.refs_1_ = bf16[144,256]{1,0:T(8,128)(2,1)S(1)} collective-permute-done((bf16[144,256]{1,0:T(8,128)(2,1)S(1)}, bf16[144,256]{1,0:T(8,128)(2,1)S(1)}, u32[]{:S(2)}, u32[]{:S(2)}) %collective-permute-start.14) | collective-permute-done | bytes 73760 | tf_op jit(solution)/shard_map/ppermute | solution.py:36
  73.0 3.8 %collective-permute-done.15.refs_2_ = bf16[144,256]{1,0:T(8,128)(2,1)S(1)} collective-permute-done((bf16[144,256]{1,0:T(8,128)(2,1)S(1)}, bf16[144,256]{1,0:T(8,128)(2,1)S(1)}, u32[]{:S(2)}, u32[]{:S(2)}) %collective-permute-start.15) | collective-permute-done | bytes 73760 | tf_op jit(solution)/shard_map/ppermute | solution.py:36
  77.4 1.9 %collective-permute-start.20 = (bf16[144,256]{1,0:T(8,128)(2,1)S(1)}, bf16[144,256]{1,0:T(8,128)(2,1)S(1)}, u32[]{:S(2)}, u32[]{:S(2)}) collective-permute-start(bf16[144,256]{1,0:T(8,128)(2,1)S(1)} %shard_map.98.refs_0_.refs_1_), channel_id=1, source_target_pairs={{0,24},{1,25},{2,26},{3,27},{4,28},{5,29},{6,30},{7,31},{8,16},{9,... | collective-permute-start | bytes 221192 | tf_op jit(solution)/shard_map/ppermute | solution.py:36
  79.7 1.2 %collective-permute-start.18 = (bf16[144,256]{1,0:T(8,128)(2,1)S(1)}, bf16[144,256]{1,0:T(8,128)(2,1)S(1)}, u32[]{:S(2)}, u32[]{:S(2)}) collective-permute-start(bf16[144,256]{1,0:T(8,128)(2,1)S(1)} %shard_map.98.refs_0_.refs_1_), channel_id=1, source_target_pairs={{0,8},{1,17},{2,10},{3,19},{4,12},{5,21},{6,14},{7,23},{8,0},{9,25... | collective-permute-start | bytes 221192 | tf_op jit(solution)/shard_map/ppermute | solution.py:36
  81.0 2.2 %shard_map.100 = (f32[2,256,1024]{2,1,0:T(8,128)}, f32[8,128]{1,0:T(8,128)S(1)}) custom-call(s32[3]{0:T(128)S(1)} %pad_add_fusion.place_ref, bf16[144,256]{1,0:T(8,128)(2,1)S(1)} %shard_map.98.refs_0_.refs_1_, f32[2,256,1024]{2,1,0:T(8,128)S(1)} %get-tuple-element.75.refs_1_, bf16[2,256,1024]{2,1,0:T(8,128)(2,1)S(1)} %collective-permute-done.17.refs_2_, ...), custom_call_target="tpu_custom_call" | custom-call | bytes 6295552 | tf_op jit(solution)/shard_map/pallas_call | solution.py:69
  84.1 1.4 %shard_map.101 = (f32[128,1024]{1,0:T(8,128)}, f32[100,128]{1,0:T(8,128)}) custom-call(s32[3]{0:T(128)S(1)} %pad_add_fusion.place_ref, f32[8,128]{1,0:T(8,128)S(1)} %get-tuple-element.78.refs_0_, bf16[144,256]{1,0:T(8,128)(2,1)S(1)} %shard_map.98.refs_0_.refs_1_, bf16[144,256]{1,0:T(8,128)(2,1)S(1)} %collective-permute-done.18.refs_2_, ...), custom_call_target="tpu_custom_call" | custom-call | bytes 870400 | tf_op jit(solution)/shard_map/pallas_call | solution.py:69
  (36 shorter events, 8.7 us)
Async XLA Ops:
  0.6 7.8 %collective-permute-start = (bf16[2,256,1024]{2,1,0:T(8,128)(2,1)}, bf16[2,256,1024]{2,1,0:T(8,128)(2,1)S(1)}, u32[]{:S(2)}, u32[]{:S(2)}) collective-permute-start(bf16[2,256,1024]{2,1,0:T(8,128)(2,1)} %refs_0_.1), channel_id=1, source_target_pairs={{0,1},{1,0},{2,3},{3,2},{4,5},{5,4},{6,7},{7,6},{8,9},{9,8},{10,11... | collective-permute-start | bytes 3145736 | tf_op jit(solution)/shard_map/ppermute | solution.py:20
  1.1 9.0 %collective-permute-start.1 = (bf16[2,256,1024]{2,1,0:T(8,128)(2,1)}, bf16[2,256,1024]{2,1,0:T(8,128)(2,1)S(1)}, u32[]{:S(2)}, u32[]{:S(2)}) collective-permute-start(bf16[2,256,1024]{2,1,0:T(8,128)(2,1)} %refs_0_.1), channel_id=1, source_target_pairs={{1,2},{3,4},{5,6},{2,1},{4,3},{6,5},{9,10},{11,12},{13,14},{10,9},... | collective-permute-start | bytes 3145736 | tf_op jit(solution)/shard_map/ppermute | solution.py:26
  2.0 0.9 %copy-start = (bf16[1024,100]{0,1:T(8,128)(2,1)S(1)}, bf16[1024,100]{0,1:T(8,128)(2,1)}, u32[]{:S(2)}) copy-start(bf16[1024,100]{0,1:T(8,128)(2,1)} %param.11) | copy-start | bytes 614404
  2.9 0.9 %copy-start.1 = (f32[100,512]{1,0:T(8,128)S(1)}, f32[100,512]{1,0:T(8,128)}, u32[]{:S(2)}) copy-start(f32[100,512]{1,0:T(8,128)} %refs_5_.1) | copy-start | bytes 614404
  3.8 0.7 copy-start.2
  4.5 0.7 copy-start.3
  15.1 6.0 %collective-permute-start.2 = (f32[208,128]{1,0:T(8,128)S(1)}, f32[208,128]{1,0:T(8,128)S(1)}, u32[]{:S(2)}, u32[]{:S(2)}) collective-permute-start(f32[208,128]{1,0:T(8,128)S(1)} %get-tuple-element.47.refs_1_), channel_id=1, source_target_pairs={{0,8},{1,17},{2,10},{3,19},{4,12},{5,21},{6,14},{7,23},{8,0},{9,25... | collective-permute-start | bytes 319496 | tf_op jit(solution)/shard_map/ppermute | solution.py:36
  17.7 4.7 %collective-permute-start.3 = (f32[208,128]{1,0:T(8,128)S(1)}, f32[208,128]{1,0:T(8,128)S(1)}, u32[]{:S(2)}, u32[]{:S(2)}) collective-permute-start(f32[208,128]{1,0:T(8,128)S(1)} %get-tuple-element.48.refs_2_), channel_id=1, source_target_pairs={{0,16},{1,9},{2,18},{3,11},{4,20},{5,13},{6,22},{7,15},{8,24},{9,1... | collective-permute-start | bytes 319496 | tf_op jit(solution)/shard_map/ppermute | solution.py:36
  19.2 5.6 %collective-permute-start.4 = (f32[208,128]{1,0:T(8,128)S(1)}, f32[208,128]{1,0:T(8,128)S(1)}, u32[]{:S(2)}, u32[]{:S(2)}) collective-permute-start(f32[208,128]{1,0:T(8,128)S(1)} %get-tuple-element.49.refs_3_), channel_id=1, source_target_pairs={{0,24},{1,25},{2,26},{3,27},{4,28},{5,29},{6,30},{7,31},{8,16},{9,... | collective-permute-start | bytes 319496 | tf_op jit(solution)/shard_map/ppermute | solution.py:36
  25.9 4.7 %collective-permute-start.5 = (bf16[208,128]{1,0:T(8,128)(2,1)S(1)}, bf16[208,128]{1,0:T(8,128)(2,1)S(1)}, u32[]{:S(2)}, u32[]{:S(2)}) collective-permute-start(bf16[208,128]{1,0:T(8,128)(2,1)S(1)} %get-tuple-element.54.refs_1_), channel_id=1, source_target_pairs={{0,8},{1,17},{2,10},{3,19},{4,12},{5,21},{6,14},{7,23},{8,0},{9,25... | collective-permute-start | bytes 159752 | tf_op jit(solution)/shard_map/ppermute | solution.py:36
  26.5 5.8 %collective-permute-start.6 = (bf16[208,128]{1,0:T(8,128)(2,1)S(1)}, bf16[208,128]{1,0:T(8,128)(2,1)S(1)}, u32[]{:S(2)}, u32[]{:S(2)}) collective-permute-start(bf16[208,128]{1,0:T(8,128)(2,1)S(1)} %get-tuple-element.55.refs_2_), channel_id=1, source_target_pairs={{0,16},{1,9},{2,18},{3,11},{4,20},{5,13},{6,22},{7,15},{8,24},{9,1... | collective-permute-start | bytes 159752 | tf_op jit(solution)/shard_map/ppermute | solution.py:36
  26.7 5.5 %collective-permute-start.7 = (bf16[208,128]{1,0:T(8,128)(2,1)S(1)}, bf16[208,128]{1,0:T(8,128)(2,1)S(1)}, u32[]{:S(2)}, u32[]{:S(2)}) collective-permute-start(bf16[208,128]{1,0:T(8,128)(2,1)S(1)} %get-tuple-element.56.refs_3_), channel_id=1, source_target_pairs={{0,24},{1,25},{2,26},{3,27},{4,28},{5,29},{6,30},{7,31},{8,16},{9,... | collective-permute-start | bytes 159752 | tf_op jit(solution)/shard_map/ppermute | solution.py:36
  34.4 7.8 %collective-permute-start.8 = (bf16[2,4,144,256]{3,2,1,0:T(8,128)(2,1)S(1)}, bf16[2,4,144,256]{3,2,1,0:T(8,128)(2,1)S(1)}, u32[]{:S(2)}, u32[]{:S(2)}) collective-permute-start(bf16[2,4,144,256]{3,2,1,0:T(8,128)(2,1)S(1)} %get-tuple-element.61), channel_id=1, source_target_pairs={{0,1},{1,0},{2,3},{3,2},{4,5},{5,4},{6,7},{7,6},{8,9},{9,8},{10,11... | collective-permute-start | bytes 1769480 | tf_op jit(solution)/shard_map/ppermute | solution.py:20
  42.1 7.7 %collective-permute-start.11 = (bf16[2,4,144,256]{3,2,1,0:T(8,128)(2,1)S(1)}, bf16[2,4,144,256]{3,2,1,0:T(8,128)(2,1)S(1)}, u32[]{:S(2)}, u32[]{:S(2)}) collective-permute-start(bf16[2,4,144,256]{3,2,1,0:T(8,128)(2,1)S(1)} %get-tuple-element.68), channel_id=1, source_target_pairs={{0,1},{1,0},{2,3},{3,2},{4,5},{5,4},{6,7},{7,6},{8,9},{9,8},{10,11... | collective-permute-start | bytes 1769480 | tf_op jit(solution)/shard_map/ppermute | solution.py:20
  43.5 9.9 %collective-permute-start.12 = (bf16[2,4,144,256]{3,2,1,0:T(8,128)(2,1)S(1)}, bf16[2,4,144,256]{3,2,1,0:T(8,128)(2,1)S(1)}, u32[]{:S(2)}, u32[]{:S(2)}) collective-permute-start(bf16[2,4,144,256]{3,2,1,0:T(8,128)(2,1)S(1)} %shard_map.93.refs_0_), channel_id=1, source_target_pairs={{0,8},{1,17},{2,10},{3,19},{4,12},{5,21},{6,14},{7,23},{8,0},{9,25... | collective-permute-start | bytes 1769480 | tf_op jit(solution)/shard_map/ppermute | solution.py:36
  46.3 8.4 %collective-permute-start.9 = (bf16[256,1024]{1,0:T(8,128)(2,1)S(1)}, bf16[256,1024]{1,0:T(8,128)(2,1)S(1)}, u32[]{:S(2)}, u32[]{:S(2)}) collective-permute-start(bf16[256,1024]{1,0:T(8,128)(2,1)S(1)} %get-tuple-element.64), channel_id=1, source_target_pairs={{1,2},{3,4},{5,6},{2,1},{4,3},{6,5},{9,10},{11,12},{13,14},{10,9},... | collective-permute-start | bytes 1572872 | tf_op jit(solution)/shard_map/ppermute | solution.py:26
  49.1 13.5 %collective-permute-start.10 = (bf16[256,1024]{1,0:T(8,128)(2,1)S(1)}, bf16[256,1024]{1,0:T(8,128)(2,1)S(1)}, u32[]{:S(2)}, u32[]{:S(2)}) collective-permute-start(bf16[256,1024]{1,0:T(8,128)(2,1)S(1)} %get-tuple-element.66), channel_id=1, source_target_pairs={{1,2},{3,4},{5,6},{2,1},{4,3},{6,5},{9,10},{11,12},{13,14},{10,9},... | collective-permute-start | bytes 1572872 | tf_op jit(solution)/shard_map/ppermute | solution.py:26
  54.1 8.4 %collective-permute-start.13 = (bf16[1,4,144,256]{3,2,1,0:T(8,128)(2,1)S(1)}, bf16[1,4,144,256]{3,2,1,0:T(8,128)(2,1)S(1)}, u32[]{:S(2)}, u32[]{:S(2)}) collective-permute-start(bf16[1,4,144,256]{3,2,1,0:T(8,128)(2,1)S(1)} %get-tuple-element.70), channel_id=1, source_target_pairs={{0,16},{1,9},{2,18},{3,11},{4,20},{5,13},{6,22},{7,15},{8,24},{9,1... | collective-permute-start | bytes 884744 | tf_op jit(solution)/shard_map/ppermute | solution.py:36
  56.5 24.4 %collective-permute-start.17 = (bf16[2,256,1024]{2,1,0:T(8,128)(2,1)S(1)}, bf16[2,256,1024]{2,1,0:T(8,128)(2,1)S(1)}, u32[]{:S(2)}, u32[]{:S(2)}) collective-permute-start(bf16[2,256,1024]{2,1,0:T(8,128)(2,1)S(1)} %get-tuple-element.76), channel_id=1, source_target_pairs={{0,1},{1,0},{2,3},{3,2},{4,5},{5,4},{6,7},{7,6},{8,9},{9,8},{10,11... | collective-permute-start | bytes 3145736 | tf_op jit(solution)/shard_map/ppermute | solution.py:20
  63.2 9.8 %collective-permute-start.14 = (bf16[144,256]{1,0:T(8,128)(2,1)S(1)}, bf16[144,256]{1,0:T(8,128)(2,1)S(1)}, u32[]{:S(2)}, u32[]{:S(2)}) collective-permute-start(bf16[144,256]{1,0:T(8,128)(2,1)S(1)} %get-tuple-element.72), channel_id=1, source_target_pairs={{0,6},{1,7},{2,4},{3,5},{4,2},{5,3},{6,0},{7,1},{8,14},{9,15},{10,... | collective-permute-start | bytes 221192 | tf_op jit(solution)/shard_map/ppermute | solution.py:36
  69.8 7.0 %collective-permute-start.15 = (bf16[144,256]{1,0:T(8,128)(2,1)S(1)}, bf16[144,256]{1,0:T(8,128)(2,1)S(1)}, u32[]{:S(2)}, u32[]{:S(2)}) collective-permute-start(bf16[144,256]{1,0:T(8,128)(2,1)S(1)} %get-tuple-element.73), channel_id=1, source_target_pairs={{0,4},{1,5},{2,6},{3,7},{4,0},{5,1},{6,2},{7,3},{8,12},{9,13},{10,... | collective-permute-start | bytes 221192 | tf_op jit(solution)/shard_map/ppermute | solution.py:36
  69.8 7.0 %collective-permute-start.16 = (bf16[144,256]{1,0:T(8,128)(2,1)S(1)}, bf16[144,256]{1,0:T(8,128)(2,1)S(1)}, u32[]{:S(2)}, u32[]{:S(2)}) collective-permute-start(bf16[144,256]{1,0:T(8,128)(2,1)S(1)} %get-tuple-element.74), channel_id=1, source_target_pairs={{0,2},{1,3},{2,0},{3,1},{4,6},{5,7},{6,4},{7,5},{8,10},{9,11},{10,... | collective-permute-start | bytes 221192 | tf_op jit(solution)/shard_map/ppermute | solution.py:36
  77.4 5.8 %collective-permute-start.20 = (bf16[144,256]{1,0:T(8,128)(2,1)S(1)}, bf16[144,256]{1,0:T(8,128)(2,1)S(1)}, u32[]{:S(2)}, u32[]{:S(2)}) collective-permute-start(bf16[144,256]{1,0:T(8,128)(2,1)S(1)} %shard_map.98.refs_0_.refs_1_), channel_id=1, source_target_pairs={{0,24},{1,25},{2,26},{3,27},{4,28},{5,29},{6,30},{7,31},{8,16},{9,... | collective-permute-start | bytes 221192 | tf_op jit(solution)/shard_map/ppermute | solution.py:36
  79.3 4.5 %collective-permute-start.19 = (bf16[144,256]{1,0:T(8,128)(2,1)S(1)}, bf16[144,256]{1,0:T(8,128)(2,1)S(1)}, u32[]{:S(2)}, u32[]{:S(2)}) collective-permute-start(bf16[144,256]{1,0:T(8,128)(2,1)S(1)} %shard_map.98.refs_0_.refs_1_), channel_id=1, source_target_pairs={{0,16},{1,9},{2,18},{3,11},{4,20},{5,13},{6,22},{7,15},{8,24},{9,1... | collective-permute-start | bytes 221192 | tf_op jit(solution)/shard_map/ppermute | solution.py:36
  79.7 4.4 %collective-permute-start.18 = (bf16[144,256]{1,0:T(8,128)(2,1)S(1)}, bf16[144,256]{1,0:T(8,128)(2,1)S(1)}, u32[]{:S(2)}, u32[]{:S(2)}) collective-permute-start(bf16[144,256]{1,0:T(8,128)(2,1)S(1)} %shard_map.98.refs_0_.refs_1_), channel_id=1, source_target_pairs={{0,8},{1,17},{2,10},{3,19},{4,12},{5,21},{6,14},{7,23},{8,0},{9,25... | collective-permute-start | bytes 221192 | tf_op jit(solution)/shard_map/ppermute | solution.py:36

commit v3 on v1

--- a/solution.py
+++ b/solution.py
@@ -289,14 +289,17 @@
 
 
 def window_body(place, dpreact, w_hidden_t, adjacency_t, on_link, on_chip, own):
-    mem, nodes, _ = own.shape
+    mem, nodes, width = own.shape
     grid = adjacency_t.shape[1]
+    step = 256
     first, second = sides(place[2], nodes)
     for m in range(mem):
-        total = mul(dpreact[m * grid : (m + 1) * grid], w_hidden_t[...]).astype(bf16)
-        on_link[m] = mul(adjacency_t[pl.ds(second, nodes)], total).astype(bf16)
-        on_chip[m] = mul(adjacency_t[pl.ds(first, nodes)], total).astype(bf16)
-        own[m] = mul(adjacency_t[nodes : 2 * nodes], total)
+        for at in range(0, width, step):
+            lanes = slice(at, at + step)
+            total = mul(dpreact[m * grid : (m + 1) * grid], w_hidden_t[:, lanes]).astype(bf16)
+            on_link[m, :, lanes] = mul(adjacency_t[pl.ds(second, nodes)], total).astype(bf16)
+            on_chip[m, :, lanes] = mul(adjacency_t[pl.ds(first, nodes)], total).astype(bf16)
+            own[m, :, lanes] = mul(adjacency_t[nodes : 2 * nodes], total)
 
 
 def latents_body(place, own, on_chip, on_link, total, token):

time: 85.5 us -> 89.7 us (1.049)
  Pallas kernels: 29.5 us -> 33.7 us
  waiting for transfers between devices: 24.8 us -> 20.6 us
  starting transfers between devices: 26.9 us -> 31 us
    pallas_call x15, Pallas kernels: 29.5 us -> 33.7 us  [call(): pl.pallas_call(kernel, out_shape=[jax.ShapeDtypeStruct(shape, kind) if la...]
    ppermute x14, waiting for transfers between devices: 24.8 us -> 20.6 us  [core_swap(): lax.ppermute(value, ('ens', 'space'), [(e * space + s, partner(e, s)) for...]
    ppermute x14, starting transfers between devices: 18.7 us -> 22.9 us  [core_swap(): lax.ppermute(value, ('ens', 'space'), [(e * space + s, partner(e, s)) for...]
  transfers between devices with their start and end apart: 20 -> 20, of which waited for: 9 -> 8; matrix products, arithmetic and copies ran while one was open for 0% -> 0% of each run, Pallas kernels for 23% -> 27%
where the time goes in v3:
time: 89.7 us; the launch traced here: 89.4 us
  Pallas kernels  33.7 us (38%)
  starting transfers between devices  31 us (35%)
  waiting for transfers between devices  20.6 us (23%)
  local copies, waits for them, and re-layouts  3.26 us (4%)
    pallas_call x15, Pallas kernels, call(): pl.pallas_call(kernel, out_shape=[jax.ShapeDtypeStruct(shape, kind) if la...  33.7 us
    ppermute x14, starting transfers between devices, core_swap(): lax.ppermute(value, ('ens', 'space'), [(e * space + s, partner(e, s)) for...  22.9 us
    ppermute x14, waiting for transfers between devices, core_swap(): lax.ppermute(value, ('ens', 'space'), [(e * space + s, partner(e, s)) for...  20.6 us
    ppermute x4, starting transfers between devices, chip_swap(): return lax.ppermute(value, 'space', [(i, i ^ 1) for i in range(count)])  6.69 us
    unnamed x8, local copies, waits for them, and re-layouts  3.26 us
  transfers between devices with their start and end apart: 20, of which 8 were waited for; matrix products, arithmetic and copies ran while one was open for 0% of the time, Pallas kernels for 27%

profile of v3, /device:TPU:0, one launch (start us, length us, event | category | flops | bytes accessed | tf_op | source)
XLA Modules:
  0.0 89.4 jit_solution(1075551662244748900)
XLA Ops:
  1.1 0.7 collective-permute-start.1
  2.0 0.9 %copy-done = bf16[1024,100]{0,1:T(8,128)(2,1)S(1)} copy-done((bf16[1024,100]{0,1:T(8,128)(2,1)S(1)}, bf16[1024,100]{0,1:T(8,128)(2,1)}, u32[]{:S(2)}) %copy-start) | copy-done | bytes 204824
  2.9 0.9 %copy-done.1 = f32[100,512]{1,0:T(8,128)S(1)} copy-done((f32[100,512]{1,0:T(8,128)S(1)}, f32[100,512]{1,0:T(8,128)}, u32[]{:S(2)}) %copy-start.1) | copy-done | bytes 204824
  3.8 0.7 copy-done.2
  5.2 3.1 %shard_map.85 = (bf16[512,768]{1,0:T(8,128)(2,1)S(1)}, bf16[768,512]{1,0:T(8,128)(2,1)S(1)}, bf16[1024,1024]{1,0:T(8,128)(2,1)S(1)}, bf16[2,256,1024]{2,1,0:T(8,...) custom-call(s32[3]{0:T(128)S(1)} %pad_add_fusion.place_ref, ...), custom_call_target="tpu_custom_call" | custom-call | bytes 7667712 | tf_op jit(solution)/shard_map/pallas_call | solution.py:69
  8.4 1.8 %shard_map.86.refs_0_ = f32[2,512,1024]{2,1,0:T(8,128)S(1)} custom-call(s32[3]{0:T(128)S(1)} %pad_add_fusion.place_ref, bf16[2,256,1024]{2,1,0:T(8,128)(2,1)S(1)} %get-tuple-element.40.refs_0_, bf16[2,256,1024]{2,1,0:T(8,128)(2,1)S(1)} %collective-permute-done.refs_1_, bf16[512,768]{1,0:T(8,128)(2,1)S(1)} %get-tuple-element.41.refs_2_), custom_call_target="tpu_custom_call" | custom-call | bytes 7077888 | tf_op jit(solution)/shard_map/pallas_call | solution.py:69
  10.2 4.9 %shard_map.87 = (bf16[2,512,1024]{2,1,0:T(8,128)(2,1)S(1)}, f32[2,512,1024]{2,1,0:T(8,128)S(1)}, bf16[2,512,1024]{2,1,0:T(8,128)(2,1)S(1)}, f32[208,128]{1,0:T(8...) custom-call(s32[3]{0:T(128)S(1)} %pad_add_fusion.place_ref, ...), custom_call_target="tpu_custom_call" | custom-call | flops 2952790016 | bytes 17154048 | tf_op jit(solution)/shard_map/pallas_call | solution.py:69
  15.1 2.6 %collective-permute-start.2 = (f32[208,128]{1,0:T(8,128)S(1)}, f32[208,128]{1,0:T(8,128)S(1)}, u32[]{:S(2)}, u32[]{:S(2)}) collective-permute-start(f32[208,128]{1,0:T(8,128)S(1)} %get-tuple-element.44.refs_1_), channel_id=1, source_target_pairs={{0,8},{1,17},{2,10},{3,19},{4,12},{5,21},{6,14},{7,23},{8,0},{9,25... | collective-permute-start | bytes 319496 | tf_op jit(solution)/shard_map/ppermute | solution.py:36
  17.7 1.5 %collective-permute-start.3 = (f32[208,128]{1,0:T(8,128)S(1)}, f32[208,128]{1,0:T(8,128)S(1)}, u32[]{:S(2)}, u32[]{:S(2)}) collective-permute-start(f32[208,128]{1,0:T(8,128)S(1)} %get-tuple-element.45.refs_2_), channel_id=1, source_target_pairs={{0,16},{1,9},{2,18},{3,11},{4,20},{5,13},{6,22},{7,15},{8,24},{9,1... | collective-permute-start | bytes 319496 | tf_op jit(solution)/shard_map/ppermute | solution.py:36
  19.2 1.9 %shard_map.88.refs_0_.refs_1_ = f32[2,512,1024]{2,1,0:T(8,128)S(1)} custom-call(s32[3]{0:T(128)S(1)} %pad_add_fusion.place_ref, f32[208,128]{1,0:T(8,128)S(1)} %get-tuple-element.43.refs_0_.refs_2_, f32[208,128]{1,0:T(8,128)S(1)} %get-tuple-element.44.refs_1_, f32[208,128]{1,0:T(8,128)S(1)} %get-tuple-element.45.refs_2_, ...), custom_call_target="tpu_custom_call" | custom-call | bytes 8388608 | tf_op jit(solution)/shard_map/pallas_call | solution.py:69
  21.2 1.2 %collective-permute-done.3.refs_4_ = f32[208,128]{1,0:T(8,128)S(1)} collective-permute-done((f32[208,128]{1,0:T(8,128)S(1)}, f32[208,128]{1,0:T(8,128)S(1)}, u32[]{:S(2)}, u32[]{:S(2)}) %collective-permute-start.3) | collective-permute-done | bytes 106528 | tf_op jit(solution)/shard_map/ppermute | solution.py:36
  22.4 2.4 %collective-permute-done.4.refs_5_ = f32[208,128]{1,0:T(8,128)S(1)} collective-permute-done((f32[208,128]{1,0:T(8,128)S(1)}, f32[208,128]{1,0:T(8,128)S(1)}, u32[]{:S(2)}, u32[]{:S(2)}) %collective-permute-start.4) | collective-permute-done | bytes 106528 | tf_op jit(solution)/shard_map/ppermute | solution.py:36
  24.8 1.0 %shard_map.89 = (bf16[208,128]{1,0:T(8,128)(2,1)S(1)}, bf16[208,128]{1,0:T(8,128)(2,1)S(1)}, bf16[208,128]{1,0:T(8,128)(2,1)S(1)}, bf16[208,128]{1,0:T(8,128)(2,1)S(1)}) custom-call(s32[3]{0:T(128)S(1)} %pad_add_fusion.place_ref, f32[2,512,1024]{2,1,0:T(8,128)S(1)} %shard_map.88.refs_0_.refs_1_, f32[104,512]{1,0:T(8,128)S(1)} %get-tuple-element.49.refs_1_, ...), custom_call_target="tpu_custom_call" | custom-call | bytes 851968 | tf_op jit(solution)/shard_map/pallas_call | solution.py:69
  26.7 2.7 %collective-permute-start.7 = (bf16[208,128]{1,0:T(8,128)(2,1)S(1)}, bf16[208,128]{1,0:T(8,128)(2,1)S(1)}, u32[]{:S(2)}, u32[]{:S(2)}) collective-permute-start(bf16[208,128]{1,0:T(8,128)(2,1)S(1)} %get-tuple-element.53.refs_3_), channel_id=1, source_target_pairs={{0,24},{1,25},{2,26},{3,27},{4,28},{5,29},{6,30},{7,31},{8,16},{9,... | collective-permute-start | bytes 159752 | tf_op jit(solution)/shard_map/ppermute | solution.py:36
  29.4 1.2 %shard_map.90 = bf16[1024,1024]{1,0:T(8,128)(2,1)S(1)} custom-call(s32[3]{0:T(128)S(1)} %pad_add_fusion.place_ref, bf16[208,128]{1,0:T(8,128)(2,1)S(1)} %get-tuple-element.50.refs_0_.refs_4_, bf16[208,128]{1,0:T(8,128)(2,1)S(1)} %get-tuple-element.51.refs_1_, bf16[208,128]{1,0:T(8,128)(2,1)S(1)} %get-tuple-element.52.refs_2_, ...), custom_call_target="tpu_custom_call" | custom-call | bytes 4194304 | tf_op jit(solution)/shard_map/pallas_call | solution.py:69
  30.6 1.6 %collective-permute-done.6.refs_6_ = bf16[208,128]{1,0:T(8,128)(2,1)S(1)} collective-permute-done((bf16[208,128]{1,0:T(8,128)(2,1)S(1)}, bf16[208,128]{1,0:T(8,128)(2,1)S(1)}, u32[]{:S(2)}, u32[]{:S(2)}) %collective-permute-start.6) | collective-permute-done | bytes 53280 | tf_op jit(solution)/shard_map/ppermute | solution.py:36
  32.2 2.2 %shard_map.91 = (bf16[1024,1024]{1,0:T(8,128)(2,1)S(1)}, f32[128,1024]{1,0:T(8,128)S(1)}, bf16[2,4,144,256]{3,2,1,0:T(8,128)(2,1)S(1)}) custom-call(s32[3]{0:T(128)S(1)} %pad_add_fusion.place_ref, bf16[104,1024]{1,0:T(8,128)(2,1)S(1)} %get-tuple-element.39.refs_4_.refs_0_, f32[2,512,1024]{2,1,0:T(8,128)S(1)} %shard_map.88.refs_0_.refs_1_, ...), custom_call_target="tpu_custom_call" | custom-call | flops 1073741824 | bytes 12025856 | tf_op jit(solution)/shard_map/pallas_call | solution.py:69
  34.4 5.8 %collective-permute-start.9 = (bf16[2,4,144,256]{3,2,1,0:T(8,128)(2,1)S(1)}, bf16[2,4,144,256]{3,2,1,0:T(8,128)(2,1)S(1)}, u32[]{:S(2)}, u32[]{:S(2)}) collective-permute-start(bf16[2,4,144,256]{3,2,1,0:T(8,128)(2,1)S(1)} %get-tuple-element.59), channel_id=1, source_target_pairs={{0,1},{1,0},{2,3},{3,2},{4,5},{5,4},{6,7},{7,6},{8,9},{9,8},{10,11... | collective-permute-start | bytes 1769480 | tf_op jit(solution)/shard_map/ppermute | solution.py:20
  40.2 1.9 %shard_map.92 = (bf16[2,4,144,256]{3,2,1,0:T(8,128)(2,1)S(1)}, f32[2,4,144,256]{3,2,1,0:T(8,128)S(1)}) custom-call(s32[3]{0:T(128)S(1)} %pad_add_fusion.place_ref, bf16[1024,1024]{1,0:T(8,128)(2,1)S(1)} %get-tuple-element.55.refs_0_.refs_1_, f32[128,1024]{1,0:T(8,128)S(1)} %get-tuple-element.56.refs_1_.refs_2_, bf16[4,2,128,1024]{3,2,1,0:T(8,128)(2,1)S(1)} %bitcast.9), custom_call_target="tpu_custom_call" | custom-call | flops 1073741824 | bytes 6488064 | tf_op jit(solution)/shard_map/pallas_call | solution.py:69
  42.2 1.3 %shard_map.93.refs_0_ = bf16[2,4,144,256]{3,2,1,0:T(8,128)(2,1)S(1)} custom-call(s32[3]{0:T(128)S(1)} %pad_add_fusion.place_ref, f32[2,4,144,256]{3,2,1,0:T(8,128)S(1)} %get-tuple-element.57.refs_0_, bf16[1024,1024]{1,0:T(8,128)(2,1)S(1)} %get-tuple-element.55.refs_0_.refs_1_, f32[128,1024]{1,0:T(8,128)S(1)} %get-tuple-element.56.refs_1_.refs_2_, ...), custom_call_target="tpu_custom_call" | custom-call | flops 536870912 | bytes 5898240 | tf_op jit(solution)/shard_map/pallas_call | solution.py:69
  44.0 8.9 %shard_map.97 = (bf16[2,256,1024]{2,1,0:T(8,128)(2,1)S(1)}, bf16[2,256,1024]{2,1,0:T(8,128)(2,1)S(1)}, f32[2,256,1024]{2,1,0:T(8,128)S(1)}) custom-call(s32[3]{0:T(128)S(1)} %pad_add_fusion.place_ref, bf16[2,4,144,256]{3,2,1,0:T(8,128)(2,1)S(1)} %shard_map.93.refs_0_, bf16[1024,1024]{1,0:T(8,128)(2,1)S(1)} %get-tuple-element.55.refs_0_.refs_1_, ...), custom_call_target="tpu_custom_call" | custom-call | flops 3758096384 | bytes 9175040 | tf_op jit(solution)/shard_map/pallas_call | solution.py:69
  53.2 0.7 collective-permute-start.16
  53.9 0.7 shard_map.94
  54.7 1.6 %collective-permute-start.11 = (bf16[1,4,144,256]{3,2,1,0:T(8,128)(2,1)S(1)}, bf16[1,4,144,256]{3,2,1,0:T(8,128)(2,1)S(1)}, u32[]{:S(2)}, u32[]{:S(2)}) collective-permute-start(bf16[1,4,144,256]{3,2,1,0:T(8,128)(2,1)S(1)} %get-tuple-element.61), channel_id=1, source_target_pairs={{0,16},{1,9},{2,18},{3,11},{4,20},{5,13},{6,22},{7,15},{8,24},{9,1... | collective-permute-start | bytes 884744 | tf_op jit(solution)/shard_map/ppermute | solution.py:36
  56.3 5.2 %collective-permute-done.11.refs_1_ = bf16[1,4,144,256]{3,2,1,0:T(8,128)(2,1)S(1)} collective-permute-done((bf16[1,4,144,256]{3,2,1,0:T(8,128)(2,1)S(1)}, bf16[1,4,144,256]{3,2,1,0:T(8,128)(2,1)S(1)}, u32[]{:S(2)}, u32[]{:S(2)}) %collective-permute-start.11) | collective-permute-done | bytes 294944 | tf_op jit(solution)/shard_map/ppermute | solution.py:36
  62.1 8.8 %collective-permute-start.12 = (bf16[144,256]{1,0:T(8,128)(2,1)S(1)}, bf16[144,256]{1,0:T(8,128)(2,1)S(1)}, u32[]{:S(2)}, u32[]{:S(2)}) collective-permute-start(bf16[144,256]{1,0:T(8,128)(2,1)S(1)} %get-tuple-element.63), channel_id=1, source_target_pairs={{0,6},{1,7},{2,4},{3,5},{4,2},{5,3},{6,0},{7,1},{8,14},{9,15},{10,... | collective-permute-start | bytes 221192 | tf_op jit(solution)/shard_map/ppermute | solution.py:36
  71.5 7.2 %collective-permute-done.12.refs_1_ = bf16[144,256]{1,0:T(8,128)(2,1)S(1)} collective-permute-done((bf16[144,256]{1,0:T(8,128)(2,1)S(1)}, bf16[144,256]{1,0:T(8,128)(2,1)S(1)}, u32[]{:S(2)}, u32[]{:S(2)}) %collective-permute-start.12) | collective-permute-done | bytes 73760 | tf_op jit(solution)/shard_map/ppermute | solution.py:36
  78.7 2.0 %collective-permute-done.13.refs_2_ = bf16[144,256]{1,0:T(8,128)(2,1)S(1)} collective-permute-done((bf16[144,256]{1,0:T(8,128)(2,1)S(1)}, bf16[144,256]{1,0:T(8,128)(2,1)S(1)}, u32[]{:S(2)}, u32[]{:S(2)}) %collective-permute-start.13) | collective-permute-done | bytes 73760 | tf_op jit(solution)/shard_map/ppermute | solution.py:36
  81.3 1.9 %collective-permute-start.19 = (bf16[144,256]{1,0:T(8,128)(2,1)S(1)}, bf16[144,256]{1,0:T(8,128)(2,1)S(1)}, u32[]{:S(2)}, u32[]{:S(2)}) collective-permute-start(bf16[144,256]{1,0:T(8,128)(2,1)S(1)} %shard_map.96.refs_0_.refs_1_), channel_id=1, source_target_pairs={{0,24},{1,25},{2,26},{3,27},{4,28},{5,29},{6,30},{7,31},{8,16},{9,... | collective-permute-start | bytes 221192 | tf_op jit(solution)/shard_map/ppermute | solution.py:36
  83.7 1.2 %collective-permute-start.17 = (bf16[144,256]{1,0:T(8,128)(2,1)S(1)}, bf16[144,256]{1,0:T(8,128)(2,1)S(1)}, u32[]{:S(2)}, u32[]{:S(2)}) collective-permute-start(bf16[144,256]{1,0:T(8,128)(2,1)S(1)} %shard_map.96.refs_0_.refs_1_), channel_id=1, source_target_pairs={{0,8},{1,17},{2,10},{3,19},{4,12},{5,21},{6,14},{7,23},{8,0},{9,25... | collective-permute-start | bytes 221192 | tf_op jit(solution)/shard_map/ppermute | solution.py:36
  84.9 2.2 %shard_map.98 = (f32[2,256,1024]{2,1,0:T(8,128)}, f32[8,128]{1,0:T(8,128)S(1)}) custom-call(s32[3]{0:T(128)S(1)} %pad_add_fusion.place_ref, bf16[144,256]{1,0:T(8,128)(2,1)S(1)} %shard_map.96.refs_0_.refs_1_, f32[2,256,1024]{2,1,0:T(8,128)S(1)} %get-tuple-element.68.refs_1_, bf16[2,256,1024]{2,1,0:T(8,128)(2,1)S(1)} %collective-permute-done.15.refs_2_, ...), custom_call_target="tpu_custom_call" | custom-call | bytes 6295552 | tf_op jit(solution)/shard_map/pallas_call | solution.py:69
  88.0 1.4 %shard_map.99 = (f32[128,1024]{1,0:T(8,128)}, f32[100,128]{1,0:T(8,128)}) custom-call(s32[3]{0:T(128)S(1)} %pad_add_fusion.place_ref, f32[8,128]{1,0:T(8,128)S(1)} %get-tuple-element.72.refs_0_, bf16[144,256]{1,0:T(8,128)(2,1)S(1)} %shard_map.96.refs_0_.refs_1_, bf16[144,256]{1,0:T(8,128)(2,1)S(1)} %collective-permute-done.17.refs_2_, ...), custom_call_target="tpu_custom_call" | custom-call | bytes 870400 | tf_op jit(solution)/shard_map/pallas_call | solution.py:69
  (32 shorter events, 6.3 us)
Async XLA Ops:
  0.6 7.8 %collective-permute-start = (bf16[2,256,1024]{2,1,0:T(8,128)(2,1)}, bf16[2,256,1024]{2,1,0:T(8,128)(2,1)S(1)}, u32[]{:S(2)}, u32[]{:S(2)}) collective-permute-start(bf16[2,256,1024]{2,1,0:T(8,128)(2,1)} %refs_0_.1), channel_id=1, source_target_pairs={{0,1},{1,0},{2,3},{3,2},{4,5},{5,4},{6,7},{7,6},{8,9},{9,8},{10,11... | collective-permute-start | bytes 3145736 | tf_op jit(solution)/shard_map/ppermute | solution.py:20
  1.1 9.0 %collective-permute-start.1 = (bf16[2,256,1024]{2,1,0:T(8,128)(2,1)}, bf16[2,256,1024]{2,1,0:T(8,128)(2,1)S(1)}, u32[]{:S(2)}, u32[]{:S(2)}) collective-permute-start(bf16[2,256,1024]{2,1,0:T(8,128)(2,1)} %refs_0_.1), channel_id=1, source_target_pairs={{1,2},{3,4},{5,6},{2,1},{4,3},{6,5},{9,10},{11,12},{13,14},{10,9},... | collective-permute-start | bytes 3145736 | tf_op jit(solution)/shard_map/ppermute | solution.py:26
  2.0 0.9 %copy-start = (bf16[1024,100]{0,1:T(8,128)(2,1)S(1)}, bf16[1024,100]{0,1:T(8,128)(2,1)}, u32[]{:S(2)}) copy-start(bf16[1024,100]{0,1:T(8,128)(2,1)} %param.11) | copy-start | bytes 614404
  2.9 0.9 %copy-start.1 = (f32[100,512]{1,0:T(8,128)S(1)}, f32[100,512]{1,0:T(8,128)}, u32[]{:S(2)}) copy-start(f32[100,512]{1,0:T(8,128)} %refs_5_.1) | copy-start | bytes 614404
  3.8 0.7 copy-start.2
  4.5 0.7 copy-start.3
  15.1 6.0 %collective-permute-start.2 = (f32[208,128]{1,0:T(8,128)S(1)}, f32[208,128]{1,0:T(8,128)S(1)}, u32[]{:S(2)}, u32[]{:S(2)}) collective-permute-start(f32[208,128]{1,0:T(8,128)S(1)} %get-tuple-element.44.refs_1_), channel_id=1, source_target_pairs={{0,8},{1,17},{2,10},{3,19},{4,12},{5,21},{6,14},{7,23},{8,0},{9,25... | collective-permute-start | bytes 319496 | tf_op jit(solution)/shard_map/ppermute | solution.py:36
  17.7 4.7 %collective-permute-start.3 = (f32[208,128]{1,0:T(8,128)S(1)}, f32[208,128]{1,0:T(8,128)S(1)}, u32[]{:S(2)}, u32[]{:S(2)}) collective-permute-start(f32[208,128]{1,0:T(8,128)S(1)} %get-tuple-element.45.refs_2_), channel_id=1, source_target_pairs={{0,16},{1,9},{2,18},{3,11},{4,20},{5,13},{6,22},{7,15},{8,24},{9,1... | collective-permute-start | bytes 319496 | tf_op jit(solution)/shard_map/ppermute | solution.py:36
  19.2 5.6 %collective-permute-start.4 = (f32[208,128]{1,0:T(8,128)S(1)}, f32[208,128]{1,0:T(8,128)S(1)}, u32[]{:S(2)}, u32[]{:S(2)}) collective-permute-start(f32[208,128]{1,0:T(8,128)S(1)} %get-tuple-element.46.refs_3_), channel_id=1, source_target_pairs={{0,24},{1,25},{2,26},{3,27},{4,28},{5,29},{6,30},{7,31},{8,16},{9,... | collective-permute-start | bytes 319496 | tf_op jit(solution)/shard_map/ppermute | solution.py:36
  25.9 4.7 %collective-permute-start.5 = (bf16[208,128]{1,0:T(8,128)(2,1)S(1)}, bf16[208,128]{1,0:T(8,128)(2,1)S(1)}, u32[]{:S(2)}, u32[]{:S(2)}) collective-permute-start(bf16[208,128]{1,0:T(8,128)(2,1)S(1)} %get-tuple-element.51.refs_1_), channel_id=1, source_target_pairs={{0,8},{1,17},{2,10},{3,19},{4,12},{5,21},{6,14},{7,23},{8,0},{9,25... | collective-permute-start | bytes 159752 | tf_op jit(solution)/shard_map/ppermute | solution.py:36
  26.5 5.8 %collective-permute-start.6 = (bf16[208,128]{1,0:T(8,128)(2,1)S(1)}, bf16[208,128]{1,0:T(8,128)(2,1)S(1)}, u32[]{:S(2)}, u32[]{:S(2)}) collective-permute-start(bf16[208,128]{1,0:T(8,128)(2,1)S(1)} %get-tuple-element.52.refs_2_), channel_id=1, source_target_pairs={{0,16},{1,9},{2,18},{3,11},{4,20},{5,13},{6,22},{7,15},{8,24},{9,1... | collective-permute-start | bytes 159752 | tf_op jit(solution)/shard_map/ppermute | solution.py:36
  26.7 5.5 %collective-permute-start.7 = (bf16[208,128]{1,0:T(8,128)(2,1)S(1)}, bf16[208,128]{1,0:T(8,128)(2,1)S(1)}, u32[]{:S(2)}, u32[]{:S(2)}) collective-permute-start(bf16[208,128]{1,0:T(8,128)(2,1)S(1)} %get-tuple-element.53.refs_3_), channel_id=1, source_target_pairs={{0,24},{1,25},{2,26},{3,27},{4,28},{5,29},{6,30},{7,31},{8,16},{9,... | collective-permute-start | bytes 159752 | tf_op jit(solution)/shard_map/ppermute | solution.py:36
  34.4 7.8 %collective-permute-start.9 = (bf16[2,4,144,256]{3,2,1,0:T(8,128)(2,1)S(1)}, bf16[2,4,144,256]{3,2,1,0:T(8,128)(2,1)S(1)}, u32[]{:S(2)}, u32[]{:S(2)}) collective-permute-start(bf16[2,4,144,256]{3,2,1,0:T(8,128)(2,1)S(1)} %get-tuple-element.59), channel_id=1, source_target_pairs={{0,1},{1,0},{2,3},{3,2},{4,5},{5,4},{6,7},{7,6},{8,9},{9,8},{10,11... | collective-permute-start | bytes 1769480 | tf_op jit(solution)/shard_map/ppermute | solution.py:20
  42.1 11.8 %collective-permute-start.8 = (bf16[2,4,144,256]{3,2,1,0:T(8,128)(2,1)S(1)}, bf16[2,4,144,256]{3,2,1,0:T(8,128)(2,1)S(1)}, u32[]{:S(2)}, u32[]{:S(2)}) collective-permute-start(bf16[2,4,144,256]{3,2,1,0:T(8,128)(2,1)S(1)} %get-tuple-element.58), channel_id=1, source_target_pairs={{0,1},{1,0},{2,3},{3,2},{4,5},{5,4},{6,7},{7,6},{8,9},{9,8},{10,11... | collective-permute-start | bytes 1769480 | tf_op jit(solution)/shard_map/ppermute | solution.py:20
  43.5 10.4 %collective-permute-start.10 = (bf16[2,4,144,256]{3,2,1,0:T(8,128)(2,1)S(1)}, bf16[2,4,144,256]{3,2,1,0:T(8,128)(2,1)S(1)}, u32[]{:S(2)}, u32[]{:S(2)}) collective-permute-start(bf16[2,4,144,256]{3,2,1,0:T(8,128)(2,1)S(1)} %shard_map.93.refs_0_), channel_id=1, source_target_pairs={{0,8},{1,17},{2,10},{3,19},{4,12},{5,21},{6,14},{7,23},{8,0},{9,25... | collective-permute-start | bytes 1769480 | tf_op jit(solution)/shard_map/ppermute | solution.py:36
  52.9 32.0 %collective-permute-start.15 = (bf16[2,256,1024]{2,1,0:T(8,128)(2,1)S(1)}, bf16[2,256,1024]{2,1,0:T(8,128)(2,1)S(1)}, u32[]{:S(2)}, u32[]{:S(2)}) collective-permute-start(bf16[2,256,1024]{2,1,0:T(8,128)(2,1)S(1)} %get-tuple-element.69), channel_id=1, source_target_pairs={{0,1},{1,0},{2,3},{3,2},{4,5},{5,4},{6,7},{7,6},{8,9},{9,8},{10,11... | collective-permute-start | bytes 3145736 | tf_op jit(solution)/shard_map/ppermute | solution.py:20
  53.2 31.7 %collective-permute-start.16 = (bf16[2,256,1024]{2,1,0:T(8,128)(2,1)S(1)}, bf16[2,256,1024]{2,1,0:T(8,128)(2,1)S(1)}, u32[]{:S(2)}, u32[]{:S(2)}) collective-permute-start(bf16[2,256,1024]{2,1,0:T(8,128)(2,1)S(1)} %get-tuple-element.70), channel_id=1, source_target_pairs={{1,2},{3,4},{5,6},{2,1},{4,3},{6,5},{9,10},{11,12},{13,14},{10,9},... | collective-permute-start | bytes 3145736 | tf_op jit(solution)/shard_map/ppermute | solution.py:26
  54.7 6.8 %collective-permute-start.11 = (bf16[1,4,144,256]{3,2,1,0:T(8,128)(2,1)S(1)}, bf16[1,4,144,256]{3,2,1,0:T(8,128)(2,1)S(1)}, u32[]{:S(2)}, u32[]{:S(2)}) collective-permute-start(bf16[1,4,144,256]{3,2,1,0:T(8,128)(2,1)S(1)} %get-tuple-element.61), channel_id=1, source_target_pairs={{0,16},{1,9},{2,18},{3,11},{4,20},{5,13},{6,22},{7,15},{8,24},{9,1... | collective-permute-start | bytes 884744 | tf_op jit(solution)/shard_map/ppermute | solution.py:36
  62.1 16.7 %collective-permute-start.12 = (bf16[144,256]{1,0:T(8,128)(2,1)S(1)}, bf16[144,256]{1,0:T(8,128)(2,1)S(1)}, u32[]{:S(2)}, u32[]{:S(2)}) collective-permute-start(bf16[144,256]{1,0:T(8,128)(2,1)S(1)} %get-tuple-element.63), channel_id=1, source_target_pairs={{0,6},{1,7},{2,4},{3,5},{4,2},{5,3},{6,0},{7,1},{8,14},{9,15},{10,... | collective-permute-start | bytes 221192 | tf_op jit(solution)/shard_map/ppermute | solution.py:36
  70.9 9.9 %collective-permute-start.13 = (bf16[144,256]{1,0:T(8,128)(2,1)S(1)}, bf16[144,256]{1,0:T(8,128)(2,1)S(1)}, u32[]{:S(2)}, u32[]{:S(2)}) collective-permute-start(bf16[144,256]{1,0:T(8,128)(2,1)S(1)} %get-tuple-element.64), channel_id=1, source_target_pairs={{0,4},{1,5},{2,6},{3,7},{4,0},{5,1},{6,2},{7,3},{8,12},{9,13},{10,... | collective-permute-start | bytes 221192 | tf_op jit(solution)/shard_map/ppermute | solution.py:36
  70.9 9.9 %collective-permute-start.14 = (bf16[144,256]{1,0:T(8,128)(2,1)S(1)}, bf16[144,256]{1,0:T(8,128)(2,1)S(1)}, u32[]{:S(2)}, u32[]{:S(2)}) collective-permute-start(bf16[144,256]{1,0:T(8,128)(2,1)S(1)} %get-tuple-element.65), channel_id=1, source_target_pairs={{0,2},{1,3},{2,0},{3,1},{4,6},{5,7},{6,4},{7,5},{8,10},{9,11},{10,... | collective-permute-start | bytes 221192 | tf_op jit(solution)/shard_map/ppermute | solution.py:36
  81.3 5.8 %collective-permute-start.19 = (bf16[144,256]{1,0:T(8,128)(2,1)S(1)}, bf16[144,256]{1,0:T(8,128)(2,1)S(1)}, u32[]{:S(2)}, u32[]{:S(2)}) collective-permute-start(bf16[144,256]{1,0:T(8,128)(2,1)S(1)} %shard_map.96.refs_0_.refs_1_), channel_id=1, source_target_pairs={{0,24},{1,25},{2,26},{3,27},{4,28},{5,29},{6,30},{7,31},{8,16},{9,... | collective-permute-start | bytes 221192 | tf_op jit(solution)/shard_map/ppermute | solution.py:36
  83.3 4.4 %collective-permute-start.18 = (bf16[144,256]{1,0:T(8,128)(2,1)S(1)}, bf16[144,256]{1,0:T(8,128)(2,1)S(1)}, u32[]{:S(2)}, u32[]{:S(2)}) collective-permute-start(bf16[144,256]{1,0:T(8,128)(2,1)S(1)} %shard_map.96.refs_0_.refs_1_), channel_id=1, source_target_pairs={{0,16},{1,9},{2,18},{3,11},{4,20},{5,13},{6,22},{7,15},{8,24},{9,1... | collective-permute-start | bytes 221192 | tf_op jit(solution)/shard_map/ppermute | solution.py:36
  83.7 4.4 %collective-permute-start.17 = (bf16[144,256]{1,0:T(8,128)(2,1)S(1)}, bf16[144,256]{1,0:T(8,128)(2,1)S(1)}, u32[]{:S(2)}, u32[]{:S(2)}) collective-permute-start(bf16[144,256]{1,0:T(8,128)(2,1)S(1)} %shard_map.96.refs_0_.refs_1_), channel_id=1, source_target_pairs={{0,8},{1,17},{2,10},{3,19},{4,12},{5,21},{6,14},{7,23},{8,0},{9,25... | collective-permute-start | bytes 221192 | tf_op jit(solution)/shard_map/ppermute | solution.py:36

commit v4 on v1

--- a/solution.py
+++ b/solution.py
@@ -153,7 +153,7 @@
     variables = w_out_t.shape[0]
     grid = adjacency.shape[0]
     chunk = grid // ens
-    step = 256
+    step = 512
     _, second = sides(place[2], nodes)
     for m in range(mem):
         total = partial[m] + mul(adjacency[:, pl.ds(second, nodes)], on_link[m])

time: 85.5 us -> 85.2 us (level)
  transfers between devices with their start and end apart: 20 -> 20, of which waited for: 9 -> 9; matrix products, arithmetic and copies ran while one was open for 0% -> 0% of each run, Pallas kernels for 23% -> 24%
where the time goes in v4:
time: 85.2 us; the launch traced here: 84.9 us
  Pallas kernels  29.1 us (34%)
  starting transfers between devices  26.9 us (32%)
  waiting for transfers between devices  24.8 us (29%)
  local copies, waits for them, and re-layouts  3.26 us (4%)
    pallas_call x15, Pallas kernels, call(): pl.pallas_call(kernel, out_shape=[jax.ShapeDtypeStruct(shape, kind) if la...  29.1 us
    ppermute x14, waiting for transfers between devices, core_swap(): lax.ppermute(value, ('ens', 'space'), [(e * space + s, partner(e, s)) for...  24.8 us
    ppermute x14, starting transfers between devices, core_swap(): lax.ppermute(value, ('ens', 'space'), [(e * space + s, partner(e, s)) for...  18.7 us
    ppermute x4, starting transfers between devices, chip_swap(): return lax.ppermute(value, 'space', [(i, i ^ 1) for i in range(count)])  6.71 us
    unnamed x8, local copies, waits for them, and re-layouts  3.26 us
  transfers between devices with their start and end apart: 20, of which 9 were waited for; matrix products, arithmetic and copies ran while one was open for 0% of the time, Pallas kernels for 24%

profile of v4, /device:TPU:0, one launch (start us, length us, event | category | flops | bytes accessed | tf_op | source)
XLA Modules:
  0.0 84.9 jit_solution(16476426324523386545)
XLA Ops:
  1.1 0.7 collective-permute-start.1
  2.0 0.9 %copy-done = bf16[1024,100]{0,1:T(8,128)(2,1)S(1)} copy-done((bf16[1024,100]{0,1:T(8,128)(2,1)S(1)}, bf16[1024,100]{0,1:T(8,128)(2,1)}, u32[]{:S(2)}) %copy-start) | copy-done | bytes 204824
  2.9 0.9 %copy-done.1 = f32[100,512]{1,0:T(8,128)S(1)} copy-done((f32[100,512]{1,0:T(8,128)S(1)}, f32[100,512]{1,0:T(8,128)}, u32[]{:S(2)}) %copy-start.1) | copy-done | bytes 204824
  3.8 0.7 copy-done.2
  5.2 3.1 %shard_map.85 = (bf16[512,768]{1,0:T(8,128)(2,1)S(1)}, bf16[768,512]{1,0:T(8,128)(2,1)S(1)}, bf16[1024,1024]{1,0:T(8,128)(2,1)S(1)}, bf16[2,256,1024]{2,1,0:T(8,...) custom-call(s32[3]{0:T(128)S(1)} %pad_add_fusion.place_ref, ...), custom_call_target="tpu_custom_call" | custom-call | bytes 7667712 | tf_op jit(solution)/shard_map/pallas_call | solution.py:69
  8.4 1.8 %shard_map.86.refs_0_ = f32[2,512,1024]{2,1,0:T(8,128)S(1)} custom-call(s32[3]{0:T(128)S(1)} %pad_add_fusion.place_ref, bf16[2,256,1024]{2,1,0:T(8,128)(2,1)S(1)} %get-tuple-element.40.refs_0_, bf16[2,256,1024]{2,1,0:T(8,128)(2,1)S(1)} %collective-permute-done.refs_1_, bf16[512,768]{1,0:T(8,128)(2,1)S(1)} %get-tuple-element.41.refs_2_), custom_call_target="tpu_custom_call" | custom-call | bytes 7077888 | tf_op jit(solution)/shard_map/pallas_call | solution.py:69
  10.2 4.5 %shard_map.87 = (bf16[2,512,1024]{2,1,0:T(8,128)(2,1)S(1)}, f32[2,512,1024]{2,1,0:T(8,128)S(1)}, bf16[2,512,1024]{2,1,0:T(8,128)(2,1)S(1)}, f32[208,128]{1,0:T(8...) custom-call(s32[3]{0:T(128)S(1)} %pad_add_fusion.place_ref, ...), custom_call_target="tpu_custom_call" | custom-call | flops 2952790016 | bytes 17154048 | tf_op jit(solution)/shard_map/pallas_call | solution.py:69
  14.7 2.6 %collective-permute-start.2 = (f32[208,128]{1,0:T(8,128)S(1)}, f32[208,128]{1,0:T(8,128)S(1)}, u32[]{:S(2)}, u32[]{:S(2)}) collective-permute-start(f32[208,128]{1,0:T(8,128)S(1)} %get-tuple-element.44.refs_1_), channel_id=1, source_target_pairs={{0,8},{1,17},{2,10},{3,19},{4,12},{5,21},{6,14},{7,23},{8,0},{9,25... | collective-permute-start | bytes 319496 | tf_op jit(solution)/shard_map/ppermute | solution.py:36
  17.3 1.5 %collective-permute-start.3 = (f32[208,128]{1,0:T(8,128)S(1)}, f32[208,128]{1,0:T(8,128)S(1)}, u32[]{:S(2)}, u32[]{:S(2)}) collective-permute-start(f32[208,128]{1,0:T(8,128)S(1)} %get-tuple-element.45.refs_2_), channel_id=1, source_target_pairs={{0,16},{1,9},{2,18},{3,11},{4,20},{5,13},{6,22},{7,15},{8,24},{9,1... | collective-permute-start | bytes 319496 | tf_op jit(solution)/shard_map/ppermute | solution.py:36
  18.9 1.9 %shard_map.88.refs_0_.refs_1_ = f32[2,512,1024]{2,1,0:T(8,128)S(1)} custom-call(s32[3]{0:T(128)S(1)} %pad_add_fusion.place_ref, f32[208,128]{1,0:T(8,128)S(1)} %get-tuple-element.43.refs_0_.refs_2_, f32[208,128]{1,0:T(8,128)S(1)} %get-tuple-element.44.refs_1_, f32[208,128]{1,0:T(8,128)S(1)} %get-tuple-element.45.refs_2_, ...), custom_call_target="tpu_custom_call" | custom-call | bytes 8388608 | tf_op jit(solution)/shard_map/pallas_call | solution.py:69
  20.8 1.2 %collective-permute-done.3.refs_4_ = f32[208,128]{1,0:T(8,128)S(1)} collective-permute-done((f32[208,128]{1,0:T(8,128)S(1)}, f32[208,128]{1,0:T(8,128)S(1)}, u32[]{:S(2)}, u32[]{:S(2)}) %collective-permute-start.3) | collective-permute-done | bytes 106528 | tf_op jit(solution)/shard_map/ppermute | solution.py:36
  22.0 2.4 %collective-permute-done.4.refs_5_ = f32[208,128]{1,0:T(8,128)S(1)} collective-permute-done((f32[208,128]{1,0:T(8,128)S(1)}, f32[208,128]{1,0:T(8,128)S(1)}, u32[]{:S(2)}, u32[]{:S(2)}) %collective-permute-start.4) | collective-permute-done | bytes 106528 | tf_op jit(solution)/shard_map/ppermute | solution.py:36
  24.4 1.0 %shard_map.89 = (bf16[208,128]{1,0:T(8,128)(2,1)S(1)}, bf16[208,128]{1,0:T(8,128)(2,1)S(1)}, bf16[208,128]{1,0:T(8,128)(2,1)S(1)}, bf16[208,128]{1,0:T(8,128)(2,1)S(1)}) custom-call(s32[3]{0:T(128)S(1)} %pad_add_fusion.place_ref, f32[2,512,1024]{2,1,0:T(8,128)S(1)} %shard_map.88.refs_0_.refs_1_, f32[104,512]{1,0:T(8,128)S(1)} %get-tuple-element.49.refs_1_, ...), custom_call_target="tpu_custom_call" | custom-call | bytes 851968 | tf_op jit(solution)/shard_map/pallas_call | solution.py:69
  26.3 2.7 %collective-permute-start.7 = (bf16[208,128]{1,0:T(8,128)(2,1)S(1)}, bf16[208,128]{1,0:T(8,128)(2,1)S(1)}, u32[]{:S(2)}, u32[]{:S(2)}) collective-permute-start(bf16[208,128]{1,0:T(8,128)(2,1)S(1)} %get-tuple-element.53.refs_3_), channel_id=1, source_target_pairs={{0,24},{1,25},{2,26},{3,27},{4,28},{5,29},{6,30},{7,31},{8,16},{9,... | collective-permute-start | bytes 159752 | tf_op jit(solution)/shard_map/ppermute | solution.py:36
  29.0 1.2 %shard_map.90 = bf16[1024,1024]{1,0:T(8,128)(2,1)S(1)} custom-call(s32[3]{0:T(128)S(1)} %pad_add_fusion.place_ref, bf16[208,128]{1,0:T(8,128)(2,1)S(1)} %get-tuple-element.50.refs_0_.refs_4_, bf16[208,128]{1,0:T(8,128)(2,1)S(1)} %get-tuple-element.51.refs_1_, bf16[208,128]{1,0:T(8,128)(2,1)S(1)} %get-tuple-element.52.refs_2_, ...), custom_call_target="tpu_custom_call" | custom-call | bytes 4194304 | tf_op jit(solution)/shard_map/pallas_call | solution.py:69
  30.2 1.6 %collective-permute-done.6.refs_6_ = bf16[208,128]{1,0:T(8,128)(2,1)S(1)} collective-permute-done((bf16[208,128]{1,0:T(8,128)(2,1)S(1)}, bf16[208,128]{1,0:T(8,128)(2,1)S(1)}, u32[]{:S(2)}, u32[]{:S(2)}) %collective-permute-start.6) | collective-permute-done | bytes 53280 | tf_op jit(solution)/shard_map/ppermute | solution.py:36
  31.9 2.2 %shard_map.91 = (bf16[1024,1024]{1,0:T(8,128)(2,1)S(1)}, f32[128,1024]{1,0:T(8,128)S(1)}, bf16[2,4,144,256]{3,2,1,0:T(8,128)(2,1)S(1)}) custom-call(s32[3]{0:T(128)S(1)} %pad_add_fusion.place_ref, bf16[104,1024]{1,0:T(8,128)(2,1)S(1)} %get-tuple-element.39.refs_4_.refs_0_, f32[2,512,1024]{2,1,0:T(8,128)S(1)} %shard_map.88.refs_0_.refs_1_, ...), custom_call_target="tpu_custom_call" | custom-call | flops 1073741824 | bytes 12025856 | tf_op jit(solution)/shard_map/pallas_call | solution.py:69
  34.0 5.8 %collective-permute-start.9 = (bf16[2,4,144,256]{3,2,1,0:T(8,128)(2,1)S(1)}, bf16[2,4,144,256]{3,2,1,0:T(8,128)(2,1)S(1)}, u32[]{:S(2)}, u32[]{:S(2)}) collective-permute-start(bf16[2,4,144,256]{3,2,1,0:T(8,128)(2,1)S(1)} %get-tuple-element.59), channel_id=1, source_target_pairs={{0,1},{1,0},{2,3},{3,2},{4,5},{5,4},{6,7},{7,6},{8,9},{9,8},{10,11... | collective-permute-start | bytes 1769480 | tf_op jit(solution)/shard_map/ppermute | solution.py:20
  39.8 1.9 %shard_map.92 = (bf16[2,4,144,256]{3,2,1,0:T(8,128)(2,1)S(1)}, f32[2,4,144,256]{3,2,1,0:T(8,128)S(1)}) custom-call(s32[3]{0:T(128)S(1)} %pad_add_fusion.place_ref, bf16[1024,1024]{1,0:T(8,128)(2,1)S(1)} %get-tuple-element.55.refs_0_.refs_1_, f32[128,1024]{1,0:T(8,128)S(1)} %get-tuple-element.56.refs_1_.refs_2_, bf16[4,2,128,1024]{3,2,1,0:T(8,128)(2,1)S(1)} %bitcast.9), custom_call_target="tpu_custom_call" | custom-call | flops 1073741824 | bytes 6488064 | tf_op jit(solution)/shard_map/pallas_call | solution.py:69
  41.8 1.3 %shard_map.93.refs_0_ = bf16[2,4,144,256]{3,2,1,0:T(8,128)(2,1)S(1)} custom-call(s32[3]{0:T(128)S(1)} %pad_add_fusion.place_ref, f32[2,4,144,256]{3,2,1,0:T(8,128)S(1)} %get-tuple-element.57.refs_0_, bf16[1024,1024]{1,0:T(8,128)(2,1)S(1)} %get-tuple-element.55.refs_0_.refs_1_, f32[128,1024]{1,0:T(8,128)S(1)} %get-tuple-element.56.refs_1_.refs_2_, ...), custom_call_target="tpu_custom_call" | custom-call | flops 536870912 | bytes 5898240 | tf_op jit(solution)/shard_map/pallas_call | solution.py:69
  43.6 4.7 %shard_map.97 = (bf16[2,256,1024]{2,1,0:T(8,128)(2,1)S(1)}, bf16[2,256,1024]{2,1,0:T(8,128)(2,1)S(1)}, f32[2,256,1024]{2,1,0:T(8,128)S(1)}) custom-call(s32[3]{0:T(128)S(1)} %pad_add_fusion.place_ref, bf16[2,4,144,256]{3,2,1,0:T(8,128)(2,1)S(1)} %shard_map.93.refs_0_, bf16[1024,1024]{1,0:T(8,128)(2,1)S(1)} %get-tuple-element.55.refs_0_.refs_1_, ...), custom_call_target="tpu_custom_call" | custom-call | flops 3758096384 | bytes 9175040 | tf_op jit(solution)/shard_map/pallas_call | solution.py:69
  48.7 0.7 collective-permute-start.16
  49.4 3.7 %collective-permute-done.10.refs_2_ = bf16[2,4,144,256]{3,2,1,0:T(8,128)(2,1)S(1)} collective-permute-done((bf16[2,4,144,256]{3,2,1,0:T(8,128)(2,1)S(1)}, bf16[2,4,144,256]{3,2,1,0:T(8,128)(2,1)S(1)}, u32[]{:S(2)}, u32[]{:S(2)}) %collective-permute-start.10) | collective-permute-done | bytes 589856 | tf_op jit(solution)/shard_map/ppermute | solution.py:36
  53.1 0.7 shard_map.94
  54.3 6.2 %collective-permute-done.11.refs_1_ = bf16[1,4,144,256]{3,2,1,0:T(8,128)(2,1)S(1)} collective-permute-done((bf16[1,4,144,256]{3,2,1,0:T(8,128)(2,1)S(1)}, bf16[1,4,144,256]{3,2,1,0:T(8,128)(2,1)S(1)}, u32[]{:S(2)}, u32[]{:S(2)}) %collective-permute-start.11) | collective-permute-done | bytes 294944 | tf_op jit(solution)/shard_map/ppermute | solution.py:36
  61.2 5.8 %collective-permute-start.12 = (bf16[144,256]{1,0:T(8,128)(2,1)S(1)}, bf16[144,256]{1,0:T(8,128)(2,1)S(1)}, u32[]{:S(2)}, u32[]{:S(2)}) collective-permute-start(bf16[144,256]{1,0:T(8,128)(2,1)S(1)} %get-tuple-element.63), channel_id=1, source_target_pairs={{0,6},{1,7},{2,4},{3,5},{4,2},{5,3},{6,0},{7,1},{8,14},{9,15},{10,... | collective-permute-start | bytes 221192 | tf_op jit(solution)/shard_map/ppermute | solution.py:36
  67.6 6.6 %collective-permute-done.12.refs_1_ = bf16[144,256]{1,0:T(8,128)(2,1)S(1)} collective-permute-done((bf16[144,256]{1,0:T(8,128)(2,1)S(1)}, bf16[144,256]{1,0:T(8,128)(2,1)S(1)}, u32[]{:S(2)}, u32[]{:S(2)}) %collective-permute-start.12) | collective-permute-done | bytes 73760 | tf_op jit(solution)/shard_map/ppermute | solution.py:36
  74.2 2.0 %collective-permute-done.13.refs_2_ = bf16[144,256]{1,0:T(8,128)(2,1)S(1)} collective-permute-done((bf16[144,256]{1,0:T(8,128)(2,1)S(1)}, bf16[144,256]{1,0:T(8,128)(2,1)S(1)}, u32[]{:S(2)}, u32[]{:S(2)}) %collective-permute-start.13) | collective-permute-done | bytes 73760 | tf_op jit(solution)/shard_map/ppermute | solution.py:36
  76.8 1.9 %collective-permute-start.19 = (bf16[144,256]{1,0:T(8,128)(2,1)S(1)}, bf16[144,256]{1,0:T(8,128)(2,1)S(1)}, u32[]{:S(2)}, u32[]{:S(2)}) collective-permute-start(bf16[144,256]{1,0:T(8,128)(2,1)S(1)} %shard_map.96.refs_0_.refs_1_), channel_id=1, source_target_pairs={{0,24},{1,25},{2,26},{3,27},{4,28},{5,29},{6,30},{7,31},{8,16},{9,... | collective-permute-start | bytes 221192 | tf_op jit(solution)/shard_map/ppermute | solution.py:36
  79.2 1.2 %collective-permute-start.17 = (bf16[144,256]{1,0:T(8,128)(2,1)S(1)}, bf16[144,256]{1,0:T(8,128)(2,1)S(1)}, u32[]{:S(2)}, u32[]{:S(2)}) collective-permute-start(bf16[144,256]{1,0:T(8,128)(2,1)S(1)} %shard_map.96.refs_0_.refs_1_), channel_id=1, source_target_pairs={{0,8},{1,17},{2,10},{3,19},{4,12},{5,21},{6,14},{7,23},{8,0},{9,25... | collective-permute-start | bytes 221192 | tf_op jit(solution)/shard_map/ppermute | solution.py:36
  80.4 2.2 %shard_map.98 = (f32[2,256,1024]{2,1,0:T(8,128)}, f32[8,128]{1,0:T(8,128)S(1)}) custom-call(s32[3]{0:T(128)S(1)} %pad_add_fusion.place_ref, bf16[144,256]{1,0:T(8,128)(2,1)S(1)} %shard_map.96.refs_0_.refs_1_, f32[2,256,1024]{2,1,0:T(8,128)S(1)} %get-tuple-element.68.refs_1_, bf16[2,256,1024]{2,1,0:T(8,128)(2,1)S(1)} %collective-permute-done.15.refs_2_, ...), custom_call_target="tpu_custom_call" | custom-call | bytes 6295552 | tf_op jit(solution)/shard_map/pallas_call | solution.py:69
  83.5 1.4 %shard_map.99 = (f32[128,1024]{1,0:T(8,128)}, f32[100,128]{1,0:T(8,128)}) custom-call(s32[3]{0:T(128)S(1)} %pad_add_fusion.place_ref, f32[8,128]{1,0:T(8,128)S(1)} %get-tuple-element.72.refs_0_, bf16[144,256]{1,0:T(8,128)(2,1)S(1)} %shard_map.96.refs_0_.refs_1_, bf16[144,256]{1,0:T(8,128)(2,1)S(1)} %collective-permute-done.17.refs_2_, ...), custom_call_target="tpu_custom_call" | custom-call | bytes 870400 | tf_op jit(solution)/shard_map/pallas_call | solution.py:69
  (32 shorter events, 6.9 us)
Async XLA Ops:
  0.6 7.8 %collective-permute-start = (bf16[2,256,1024]{2,1,0:T(8,128)(2,1)}, bf16[2,256,1024]{2,1,0:T(8,128)(2,1)S(1)}, u32[]{:S(2)}, u32[]{:S(2)}) collective-permute-start(bf16[2,256,1024]{2,1,0:T(8,128)(2,1)} %refs_0_.1), channel_id=1, source_target_pairs={{0,1},{1,0},{2,3},{3,2},{4,5},{5,4},{6,7},{7,6},{8,9},{9,8},{10,11... | collective-permute-start | bytes 3145736 | tf_op jit(solution)/shard_map/ppermute | solution.py:20
  1.1 9.0 %collective-permute-start.1 = (bf16[2,256,1024]{2,1,0:T(8,128)(2,1)}, bf16[2,256,1024]{2,1,0:T(8,128)(2,1)S(1)}, u32[]{:S(2)}, u32[]{:S(2)}) collective-permute-start(bf16[2,256,1024]{2,1,0:T(8,128)(2,1)} %refs_0_.1), channel_id=1, source_target_pairs={{1,2},{3,4},{5,6},{2,1},{4,3},{6,5},{9,10},{11,12},{13,14},{10,9},... | collective-permute-start | bytes 3145736 | tf_op jit(solution)/shard_map/ppermute | solution.py:26
  2.0 0.9 %copy-start = (bf16[1024,100]{0,1:T(8,128)(2,1)S(1)}, bf16[1024,100]{0,1:T(8,128)(2,1)}, u32[]{:S(2)}) copy-start(bf16[1024,100]{0,1:T(8,128)(2,1)} %param.11) | copy-start | bytes 614404
  2.9 0.9 %copy-start.1 = (f32[100,512]{1,0:T(8,128)S(1)}, f32[100,512]{1,0:T(8,128)}, u32[]{:S(2)}) copy-start(f32[100,512]{1,0:T(8,128)} %refs_5_.1) | copy-start | bytes 614404
  3.8 0.7 copy-start.2
  4.5 0.7 copy-start.3
  14.7 6.0 %collective-permute-start.2 = (f32[208,128]{1,0:T(8,128)S(1)}, f32[208,128]{1,0:T(8,128)S(1)}, u32[]{:S(2)}, u32[]{:S(2)}) collective-permute-start(f32[208,128]{1,0:T(8,128)S(1)} %get-tuple-element.44.refs_1_), channel_id=1, source_target_pairs={{0,8},{1,17},{2,10},{3,19},{4,12},{5,21},{6,14},{7,23},{8,0},{9,25... | collective-permute-start | bytes 319496 | tf_op jit(solution)/shard_map/ppermute | solution.py:36
  17.3 4.7 %collective-permute-start.3 = (f32[208,128]{1,0:T(8,128)S(1)}, f32[208,128]{1,0:T(8,128)S(1)}, u32[]{:S(2)}, u32[]{:S(2)}) collective-permute-start(f32[208,128]{1,0:T(8,128)S(1)} %get-tuple-element.45.refs_2_), channel_id=1, source_target_pairs={{0,16},{1,9},{2,18},{3,11},{4,20},{5,13},{6,22},{7,15},{8,24},{9,1... | collective-permute-start | bytes 319496 | tf_op jit(solution)/shard_map/ppermute | solution.py:36
  18.8 5.6 %collective-permute-start.4 = (f32[208,128]{1,0:T(8,128)S(1)}, f32[208,128]{1,0:T(8,128)S(1)}, u32[]{:S(2)}, u32[]{:S(2)}) collective-permute-start(f32[208,128]{1,0:T(8,128)S(1)} %get-tuple-element.46.refs_3_), channel_id=1, source_target_pairs={{0,24},{1,25},{2,26},{3,27},{4,28},{5,29},{6,30},{7,31},{8,16},{9,... | collective-permute-start | bytes 319496 | tf_op jit(solution)/shard_map/ppermute | solution.py:36
  25.5 4.7 %collective-permute-start.5 = (bf16[208,128]{1,0:T(8,128)(2,1)S(1)}, bf16[208,128]{1,0:T(8,128)(2,1)S(1)}, u32[]{:S(2)}, u32[]{:S(2)}) collective-permute-start(bf16[208,128]{1,0:T(8,128)(2,1)S(1)} %get-tuple-element.51.refs_1_), channel_id=1, source_target_pairs={{0,8},{1,17},{2,10},{3,19},{4,12},{5,21},{6,14},{7,23},{8,0},{9,25... | collective-permute-start | bytes 159752 | tf_op jit(solution)/shard_map/ppermute | solution.py:36
  26.1 5.8 %collective-permute-start.6 = (bf16[208,128]{1,0:T(8,128)(2,1)S(1)}, bf16[208,128]{1,0:T(8,128)(2,1)S(1)}, u32[]{:S(2)}, u32[]{:S(2)}) collective-permute-start(bf16[208,128]{1,0:T(8,128)(2,1)S(1)} %get-tuple-element.52.refs_2_), channel_id=1, source_target_pairs={{0,16},{1,9},{2,18},{3,11},{4,20},{5,13},{6,22},{7,15},{8,24},{9,1... | collective-permute-start | bytes 159752 | tf_op jit(solution)/shard_map/ppermute | solution.py:36
  26.3 5.5 %collective-permute-start.7 = (bf16[208,128]{1,0:T(8,128)(2,1)S(1)}, bf16[208,128]{1,0:T(8,128)(2,1)S(1)}, u32[]{:S(2)}, u32[]{:S(2)}) collective-permute-start(bf16[208,128]{1,0:T(8,128)(2,1)S(1)} %get-tuple-element.53.refs_3_), channel_id=1, source_target_pairs={{0,24},{1,25},{2,26},{3,27},{4,28},{5,29},{6,30},{7,31},{8,16},{9,... | collective-permute-start | bytes 159752 | tf_op jit(solution)/shard_map/ppermute | solution.py:36
  34.0 7.8 %collective-permute-start.9 = (bf16[2,4,144,256]{3,2,1,0:T(8,128)(2,1)S(1)}, bf16[2,4,144,256]{3,2,1,0:T(8,128)(2,1)S(1)}, u32[]{:S(2)}, u32[]{:S(2)}) collective-permute-start(bf16[2,4,144,256]{3,2,1,0:T(8,128)(2,1)S(1)} %get-tuple-element.59), channel_id=1, source_target_pairs={{0,1},{1,0},{2,3},{3,2},{4,5},{5,4},{6,7},{7,6},{8,9},{9,8},{10,11... | collective-permute-start | bytes 1769480 | tf_op jit(solution)/shard_map/ppermute | solution.py:20
  41.7 7.7 %collective-permute-start.8 = (bf16[2,4,144,256]{3,2,1,0:T(8,128)(2,1)S(1)}, bf16[2,4,144,256]{3,2,1,0:T(8,128)(2,1)S(1)}, u32[]{:S(2)}, u32[]{:S(2)}) collective-permute-start(bf16[2,4,144,256]{3,2,1,0:T(8,128)(2,1)S(1)} %get-tuple-element.58), channel_id=1, source_target_pairs={{0,1},{1,0},{2,3},{3,2},{4,5},{5,4},{6,7},{7,6},{8,9},{9,8},{10,11... | collective-permute-start | bytes 1769480 | tf_op jit(solution)/shard_map/ppermute | solution.py:20
  43.1 9.9 %collective-permute-start.10 = (bf16[2,4,144,256]{3,2,1,0:T(8,128)(2,1)S(1)}, bf16[2,4,144,256]{3,2,1,0:T(8,128)(2,1)S(1)}, u32[]{:S(2)}, u32[]{:S(2)}) collective-permute-start(bf16[2,4,144,256]{3,2,1,0:T(8,128)(2,1)S(1)} %shard_map.93.refs_0_), channel_id=1, source_target_pairs={{0,8},{1,17},{2,10},{3,19},{4,12},{5,21},{6,14},{7,23},{8,0},{9,25... | collective-permute-start | bytes 1769480 | tf_op jit(solution)/shard_map/ppermute | solution.py:36
  48.4 32.0 %collective-permute-start.15 = (bf16[2,256,1024]{2,1,0:T(8,128)(2,1)S(1)}, bf16[2,256,1024]{2,1,0:T(8,128)(2,1)S(1)}, u32[]{:S(2)}, u32[]{:S(2)}) collective-permute-start(bf16[2,256,1024]{2,1,0:T(8,128)(2,1)S(1)} %get-tuple-element.69), channel_id=1, source_target_pairs={{0,1},{1,0},{2,3},{3,2},{4,5},{5,4},{6,7},{7,6},{8,9},{9,8},{10,11... | collective-permute-start | bytes 3145736 | tf_op jit(solution)/shard_map/ppermute | solution.py:20
  48.7 31.7 %collective-permute-start.16 = (bf16[2,256,1024]{2,1,0:T(8,128)(2,1)S(1)}, bf16[2,256,1024]{2,1,0:T(8,128)(2,1)S(1)}, u32[]{:S(2)}, u32[]{:S(2)}) collective-permute-start(bf16[2,256,1024]{2,1,0:T(8,128)(2,1)S(1)} %get-tuple-element.70), channel_id=1, source_target_pairs={{1,2},{3,4},{5,6},{2,1},{4,3},{6,5},{9,10},{11,12},{13,14},{10,9},... | collective-permute-start | bytes 3145736 | tf_op jit(solution)/shard_map/ppermute | solution.py:26
  53.8 6.8 %collective-permute-start.11 = (bf16[1,4,144,256]{3,2,1,0:T(8,128)(2,1)S(1)}, bf16[1,4,144,256]{3,2,1,0:T(8,128)(2,1)S(1)}, u32[]{:S(2)}, u32[]{:S(2)}) collective-permute-start(bf16[1,4,144,256]{3,2,1,0:T(8,128)(2,1)S(1)} %get-tuple-element.61), channel_id=1, source_target_pairs={{0,16},{1,9},{2,18},{3,11},{4,20},{5,13},{6,22},{7,15},{8,24},{9,1... | collective-permute-start | bytes 884744 | tf_op jit(solution)/shard_map/ppermute | solution.py:36
  61.2 13.0 %collective-permute-start.12 = (bf16[144,256]{1,0:T(8,128)(2,1)S(1)}, bf16[144,256]{1,0:T(8,128)(2,1)S(1)}, u32[]{:S(2)}, u32[]{:S(2)}) collective-permute-start(bf16[144,256]{1,0:T(8,128)(2,1)S(1)} %get-tuple-element.63), channel_id=1, source_target_pairs={{0,6},{1,7},{2,4},{3,5},{4,2},{5,3},{6,0},{7,1},{8,14},{9,15},{10,... | collective-permute-start | bytes 221192 | tf_op jit(solution)/shard_map/ppermute | solution.py:36
  66.9 9.3 %collective-permute-start.13 = (bf16[144,256]{1,0:T(8,128)(2,1)S(1)}, bf16[144,256]{1,0:T(8,128)(2,1)S(1)}, u32[]{:S(2)}, u32[]{:S(2)}) collective-permute-start(bf16[144,256]{1,0:T(8,128)(2,1)S(1)} %get-tuple-element.64), channel_id=1, source_target_pairs={{0,4},{1,5},{2,6},{3,7},{4,0},{5,1},{6,2},{7,3},{8,12},{9,13},{10,... | collective-permute-start | bytes 221192 | tf_op jit(solution)/shard_map/ppermute | solution.py:36
  67.2 9.0 %collective-permute-start.14 = (bf16[144,256]{1,0:T(8,128)(2,1)S(1)}, bf16[144,256]{1,0:T(8,128)(2,1)S(1)}, u32[]{:S(2)}, u32[]{:S(2)}) collective-permute-start(bf16[144,256]{1,0:T(8,128)(2,1)S(1)} %get-tuple-element.65), channel_id=1, source_target_pairs={{0,2},{1,3},{2,0},{3,1},{4,6},{5,7},{6,4},{7,5},{8,10},{9,11},{10,... | collective-permute-start | bytes 221192 | tf_op jit(solution)/shard_map/ppermute | solution.py:36
  76.8 5.8 %collective-permute-start.19 = (bf16[144,256]{1,0:T(8,128)(2,1)S(1)}, bf16[144,256]{1,0:T(8,128)(2,1)S(1)}, u32[]{:S(2)}, u32[]{:S(2)}) collective-permute-start(bf16[144,256]{1,0:T(8,128)(2,1)S(1)} %shard_map.96.refs_0_.refs_1_), channel_id=1, source_target_pairs={{0,24},{1,25},{2,26},{3,27},{4,28},{5,29},{6,30},{7,31},{8,16},{9,... | collective-permute-start | bytes 221192 | tf_op jit(solution)/shard_map/ppermute | solution.py:36
  78.7 4.4 %collective-permute-start.18 = (bf16[144,256]{1,0:T(8,128)(2,1)S(1)}, bf16[144,256]{1,0:T(8,128)(2,1)S(1)}, u32[]{:S(2)}, u32[]{:S(2)}) collective-permute-start(bf16[144,256]{1,0:T(8,128)(2,1)S(1)} %shard_map.96.refs_0_.refs_1_), channel_id=1, source_target_pairs={{0,16},{1,9},{2,18},{3,11},{4,20},{5,13},{6,22},{7,15},{8,24},{9,1... | collective-permute-start | bytes 221192 | tf_op jit(solution)/shard_map/ppermute | solution.py:36
  79.2 4.4 %collective-permute-start.17 = (bf16[144,256]{1,0:T(8,128)(2,1)S(1)}, bf16[144,256]{1,0:T(8,128)(2,1)S(1)}, u32[]{:S(2)}, u32[]{:S(2)}) collective-permute-start(bf16[144,256]{1,0:T(8,128)(2,1)S(1)} %shard_map.96.refs_0_.refs_1_), channel_id=1, source_target_pairs={{0,8},{1,17},{2,10},{3,19},{4,12},{5,21},{6,14},{7,23},{8,0},{9,25... | collective-permute-start | bytes 221192 | tf_op jit(solution)/shard_map/ppermute | solution.py:36

commit v5 on v4

--- a/solution.py
+++ b/solution.py
@@ -153,7 +153,7 @@
     variables = w_out_t.shape[0]
     grid = adjacency.shape[0]
     chunk = grid // ens
-    step = 512
+    step = 1024
     _, second = sides(place[2], nodes)
     for m in range(mem):
         total = partial[m] + mul(adjacency[:, pl.ds(second, nodes)], on_link[m])

time: 85.2 us -> 84.9 us (level)
  no operation moved by 1% of the time
where the time goes in v5:
time: 84.9 us; the launch traced here: 84.6 us
  Pallas kernels  28.8 us (34%)
  starting transfers between devices  27 us (32%)
  waiting for transfers between devices  24.6 us (29%)
  local copies, waits for them, and re-layouts  3.26 us (4%)
    pallas_call x15, Pallas kernels, call(): pl.pallas_call(kernel, out_shape=[jax.ShapeDtypeStruct(shape, kind) if la...  28.8 us
    ppermute x14, waiting for transfers between devices, core_swap(): lax.ppermute(value, ('ens', 'space'), [(e * space + s, partner(e, s)) for...  24.6 us
    ppermute x14, starting transfers between devices, core_swap(): lax.ppermute(value, ('ens', 'space'), [(e * space + s, partner(e, s)) for...  18.7 us
    ppermute x4, starting transfers between devices, chip_swap(): return lax.ppermute(value, 'space', [(i, i ^ 1) for i in range(count)])  6.85 us
    unnamed x8, local copies, waits for them, and re-layouts  3.26 us
  transfers between devices with their start and end apart: 20, of which 9 were waited for; matrix products, arithmetic and copies ran while one was open for 0% of the time, Pallas kernels for 24%

profile of v5, /device:TPU:0, one launch (start us, length us, event | category | flops | bytes accessed | tf_op | source)
XLA Modules:
  0.0 84.6 jit_solution(568475875866218330)
XLA Ops:
  1.1 0.7 collective-permute-start.1
  2.0 0.9 %copy-done = bf16[1024,100]{0,1:T(8,128)(2,1)S(1)} copy-done((bf16[1024,100]{0,1:T(8,128)(2,1)S(1)}, bf16[1024,100]{0,1:T(8,128)(2,1)}, u32[]{:S(2)}) %copy-start) | copy-done | bytes 204824
  2.9 0.9 %copy-done.1 = f32[100,512]{1,0:T(8,128)S(1)} copy-done((f32[100,512]{1,0:T(8,128)S(1)}, f32[100,512]{1,0:T(8,128)}, u32[]{:S(2)}) %copy-start.1) | copy-done | bytes 204824
  3.8 0.7 copy-done.2
  5.2 3.1 %shard_map.85 = (bf16[512,768]{1,0:T(8,128)(2,1)S(1)}, bf16[768,512]{1,0:T(8,128)(2,1)S(1)}, bf16[1024,1024]{1,0:T(8,128)(2,1)S(1)}, bf16[2,256,1024]{2,1,0:T(8,...) custom-call(s32[3]{0:T(128)S(1)} %pad_add_fusion.place_ref, ...), custom_call_target="tpu_custom_call" | custom-call | bytes 7667712 | tf_op jit(solution)/shard_map/pallas_call | solution.py:69
  8.4 1.8 %shard_map.86.refs_0_ = f32[2,512,1024]{2,1,0:T(8,128)S(1)} custom-call(s32[3]{0:T(128)S(1)} %pad_add_fusion.place_ref, bf16[2,256,1024]{2,1,0:T(8,128)(2,1)S(1)} %get-tuple-element.40.refs_0_, bf16[2,256,1024]{2,1,0:T(8,128)(2,1)S(1)} %collective-permute-done.refs_1_, bf16[512,768]{1,0:T(8,128)(2,1)S(1)} %get-tuple-element.41.refs_2_), custom_call_target="tpu_custom_call" | custom-call | bytes 7077888 | tf_op jit(solution)/shard_map/pallas_call | solution.py:69
  10.2 4.2 %shard_map.87 = (bf16[2,512,1024]{2,1,0:T(8,128)(2,1)S(1)}, f32[2,512,1024]{2,1,0:T(8,128)S(1)}, bf16[2,512,1024]{2,1,0:T(8,128)(2,1)S(1)}, f32[208,128]{1,0:T(8...) custom-call(s32[3]{0:T(128)S(1)} %pad_add_fusion.place_ref, ...), custom_call_target="tpu_custom_call" | custom-call | flops 2952790016 | bytes 17154048 | tf_op jit(solution)/shard_map/pallas_call | solution.py:69
  14.4 2.6 %collective-permute-start.2 = (f32[208,128]{1,0:T(8,128)S(1)}, f32[208,128]{1,0:T(8,128)S(1)}, u32[]{:S(2)}, u32[]{:S(2)}) collective-permute-start(f32[208,128]{1,0:T(8,128)S(1)} %get-tuple-element.44.refs_1_), channel_id=1, source_target_pairs={{0,8},{1,17},{2,10},{3,19},{4,12},{5,21},{6,14},{7,23},{8,0},{9,25... | collective-permute-start | bytes 319496 | tf_op jit(solution)/shard_map/ppermute | solution.py:36
  17.0 1.5 %collective-permute-start.3 = (f32[208,128]{1,0:T(8,128)S(1)}, f32[208,128]{1,0:T(8,128)S(1)}, u32[]{:S(2)}, u32[]{:S(2)}) collective-permute-start(f32[208,128]{1,0:T(8,128)S(1)} %get-tuple-element.45.refs_2_), channel_id=1, source_target_pairs={{0,16},{1,9},{2,18},{3,11},{4,20},{5,13},{6,22},{7,15},{8,24},{9,1... | collective-permute-start | bytes 319496 | tf_op jit(solution)/shard_map/ppermute | solution.py:36
  18.6 1.9 %shard_map.88.refs_0_.refs_1_ = f32[2,512,1024]{2,1,0:T(8,128)S(1)} custom-call(s32[3]{0:T(128)S(1)} %pad_add_fusion.place_ref, f32[208,128]{1,0:T(8,128)S(1)} %get-tuple-element.43.refs_0_.refs_2_, f32[208,128]{1,0:T(8,128)S(1)} %get-tuple-element.44.refs_1_, f32[208,128]{1,0:T(8,128)S(1)} %get-tuple-element.45.refs_2_, ...), custom_call_target="tpu_custom_call" | custom-call | bytes 8388608 | tf_op jit(solution)/shard_map/pallas_call | solution.py:69
  20.5 1.2 %collective-permute-done.3.refs_4_ = f32[208,128]{1,0:T(8,128)S(1)} collective-permute-done((f32[208,128]{1,0:T(8,128)S(1)}, f32[208,128]{1,0:T(8,128)S(1)}, u32[]{:S(2)}, u32[]{:S(2)}) %collective-permute-start.3) | collective-permute-done | bytes 106528 | tf_op jit(solution)/shard_map/ppermute | solution.py:36
  21.7 2.4 %collective-permute-done.4.refs_5_ = f32[208,128]{1,0:T(8,128)S(1)} collective-permute-done((f32[208,128]{1,0:T(8,128)S(1)}, f32[208,128]{1,0:T(8,128)S(1)}, u32[]{:S(2)}, u32[]{:S(2)}) %collective-permute-start.4) | collective-permute-done | bytes 106528 | tf_op jit(solution)/shard_map/ppermute | solution.py:36
  24.1 1.0 %shard_map.89 = (bf16[208,128]{1,0:T(8,128)(2,1)S(1)}, bf16[208,128]{1,0:T(8,128)(2,1)S(1)}, bf16[208,128]{1,0:T(8,128)(2,1)S(1)}, bf16[208,128]{1,0:T(8,128)(2,1)S(1)}) custom-call(s32[3]{0:T(128)S(1)} %pad_add_fusion.place_ref, f32[2,512,1024]{2,1,0:T(8,128)S(1)} %shard_map.88.refs_0_.refs_1_, f32[104,512]{1,0:T(8,128)S(1)} %get-tuple-element.49.refs_1_, ...), custom_call_target="tpu_custom_call" | custom-call | bytes 851968 | tf_op jit(solution)/shard_map/pallas_call | solution.py:69
  26.0 2.7 %collective-permute-start.7 = (bf16[208,128]{1,0:T(8,128)(2,1)S(1)}, bf16[208,128]{1,0:T(8,128)(2,1)S(1)}, u32[]{:S(2)}, u32[]{:S(2)}) collective-permute-start(bf16[208,128]{1,0:T(8,128)(2,1)S(1)} %get-tuple-element.53.refs_3_), channel_id=1, source_target_pairs={{0,24},{1,25},{2,26},{3,27},{4,28},{5,29},{6,30},{7,31},{8,16},{9,... | collective-permute-start | bytes 159752 | tf_op jit(solution)/shard_map/ppermute | solution.py:36
  28.7 1.2 %shard_map.90 = bf16[1024,1024]{1,0:T(8,128)(2,1)S(1)} custom-call(s32[3]{0:T(128)S(1)} %pad_add_fusion.place_ref, bf16[208,128]{1,0:T(8,128)(2,1)S(1)} %get-tuple-element.50.refs_0_.refs_4_, bf16[208,128]{1,0:T(8,128)(2,1)S(1)} %get-tuple-element.51.refs_1_, bf16[208,128]{1,0:T(8,128)(2,1)S(1)} %get-tuple-element.52.refs_2_, ...), custom_call_target="tpu_custom_call" | custom-call | bytes 4194304 | tf_op jit(solution)/shard_map/pallas_call | solution.py:69
  29.9 1.7 %collective-permute-done.6.refs_6_ = bf16[208,128]{1,0:T(8,128)(2,1)S(1)} collective-permute-done((bf16[208,128]{1,0:T(8,128)(2,1)S(1)}, bf16[208,128]{1,0:T(8,128)(2,1)S(1)}, u32[]{:S(2)}, u32[]{:S(2)}) %collective-permute-start.6) | collective-permute-done | bytes 53280 | tf_op jit(solution)/shard_map/ppermute | solution.py:36
  31.6 2.2 %shard_map.91 = (bf16[1024,1024]{1,0:T(8,128)(2,1)S(1)}, f32[128,1024]{1,0:T(8,128)S(1)}, bf16[2,4,144,256]{3,2,1,0:T(8,128)(2,1)S(1)}) custom-call(s32[3]{0:T(128)S(1)} %pad_add_fusion.place_ref, bf16[104,1024]{1,0:T(8,128)(2,1)S(1)} %get-tuple-element.39.refs_4_.refs_0_, f32[2,512,1024]{2,1,0:T(8,128)S(1)} %shard_map.88.refs_0_.refs_1_, ...), custom_call_target="tpu_custom_call" | custom-call | flops 1073741824 | bytes 12025856 | tf_op jit(solution)/shard_map/pallas_call | solution.py:69
  33.8 5.9 %collective-permute-start.9 = (bf16[2,4,144,256]{3,2,1,0:T(8,128)(2,1)S(1)}, bf16[2,4,144,256]{3,2,1,0:T(8,128)(2,1)S(1)}, u32[]{:S(2)}, u32[]{:S(2)}) collective-permute-start(bf16[2,4,144,256]{3,2,1,0:T(8,128)(2,1)S(1)} %get-tuple-element.59), channel_id=1, source_target_pairs={{0,1},{1,0},{2,3},{3,2},{4,5},{5,4},{6,7},{7,6},{8,9},{9,8},{10,11... | collective-permute-start | bytes 1769480 | tf_op jit(solution)/shard_map/ppermute | solution.py:20
  39.7 1.9 %shard_map.92 = (bf16[2,4,144,256]{3,2,1,0:T(8,128)(2,1)S(1)}, f32[2,4,144,256]{3,2,1,0:T(8,128)S(1)}) custom-call(s32[3]{0:T(128)S(1)} %pad_add_fusion.place_ref, bf16[1024,1024]{1,0:T(8,128)(2,1)S(1)} %get-tuple-element.55.refs_0_.refs_1_, f32[128,1024]{1,0:T(8,128)S(1)} %get-tuple-element.56.refs_1_.refs_2_, bf16[4,2,128,1024]{3,2,1,0:T(8,128)(2,1)S(1)} %bitcast.9), custom_call_target="tpu_custom_call" | custom-call | flops 1073741824 | bytes 6488064 | tf_op jit(solution)/shard_map/pallas_call | solution.py:69
  41.7 1.3 %shard_map.93.refs_0_ = bf16[2,4,144,256]{3,2,1,0:T(8,128)(2,1)S(1)} custom-call(s32[3]{0:T(128)S(1)} %pad_add_fusion.place_ref, f32[2,4,144,256]{3,2,1,0:T(8,128)S(1)} %get-tuple-element.57.refs_0_, bf16[1024,1024]{1,0:T(8,128)(2,1)S(1)} %get-tuple-element.55.refs_0_.refs_1_, f32[128,1024]{1,0:T(8,128)S(1)} %get-tuple-element.56.refs_1_.refs_2_, ...), custom_call_target="tpu_custom_call" | custom-call | flops 536870912 | bytes 5898240 | tf_op jit(solution)/shard_map/pallas_call | solution.py:69
  43.6 4.7 %shard_map.97 = (bf16[2,256,1024]{2,1,0:T(8,128)(2,1)S(1)}, bf16[2,256,1024]{2,1,0:T(8,128)(2,1)S(1)}, f32[2,256,1024]{2,1,0:T(8,128)S(1)}) custom-call(s32[3]{0:T(128)S(1)} %pad_add_fusion.place_ref, bf16[2,4,144,256]{3,2,1,0:T(8,128)(2,1)S(1)} %shard_map.93.refs_0_, bf16[1024,1024]{1,0:T(8,128)(2,1)S(1)} %get-tuple-element.55.refs_0_.refs_1_, ...), custom_call_target="tpu_custom_call" | custom-call | flops 3758096384 | bytes 9175040 | tf_op jit(solution)/shard_map/pallas_call | solution.py:69
  48.7 0.7 collective-permute-start.16
  49.4 3.5 %collective-permute-done.10.refs_2_ = bf16[2,4,144,256]{3,2,1,0:T(8,128)(2,1)S(1)} collective-permute-done((bf16[2,4,144,256]{3,2,1,0:T(8,128)(2,1)S(1)}, bf16[2,4,144,256]{3,2,1,0:T(8,128)(2,1)S(1)}, u32[]{:S(2)}, u32[]{:S(2)}) %collective-permute-start.10) | collective-permute-done | bytes 589856 | tf_op jit(solution)/shard_map/ppermute | solution.py:36
  53.0 0.7 shard_map.94
  54.3 6.1 %collective-permute-done.11.refs_1_ = bf16[1,4,144,256]{3,2,1,0:T(8,128)(2,1)S(1)} collective-permute-done((bf16[1,4,144,256]{3,2,1,0:T(8,128)(2,1)S(1)}, bf16[1,4,144,256]{3,2,1,0:T(8,128)(2,1)S(1)}, u32[]{:S(2)}, u32[]{:S(2)}) %collective-permute-start.11) | collective-permute-done | bytes 294944 | tf_op jit(solution)/shard_map/ppermute | solution.py:36
  61.1 5.5 %collective-permute-start.12 = (bf16[144,256]{1,0:T(8,128)(2,1)S(1)}, bf16[144,256]{1,0:T(8,128)(2,1)S(1)}, u32[]{:S(2)}, u32[]{:S(2)}) collective-permute-start(bf16[144,256]{1,0:T(8,128)(2,1)S(1)} %get-tuple-element.63), channel_id=1, source_target_pairs={{0,6},{1,7},{2,4},{3,5},{4,2},{5,3},{6,0},{7,1},{8,14},{9,15},{10,... | collective-permute-start | bytes 221192 | tf_op jit(solution)/shard_map/ppermute | solution.py:36
  67.3 6.6 %collective-permute-done.12.refs_1_ = bf16[144,256]{1,0:T(8,128)(2,1)S(1)} collective-permute-done((bf16[144,256]{1,0:T(8,128)(2,1)S(1)}, bf16[144,256]{1,0:T(8,128)(2,1)S(1)}, u32[]{:S(2)}, u32[]{:S(2)}) %collective-permute-start.12) | collective-permute-done | bytes 73760 | tf_op jit(solution)/shard_map/ppermute | solution.py:36
  73.9 2.0 %collective-permute-done.13.refs_2_ = bf16[144,256]{1,0:T(8,128)(2,1)S(1)} collective-permute-done((bf16[144,256]{1,0:T(8,128)(2,1)S(1)}, bf16[144,256]{1,0:T(8,128)(2,1)S(1)}, u32[]{:S(2)}, u32[]{:S(2)}) %collective-permute-start.13) | collective-permute-done | bytes 73760 | tf_op jit(solution)/shard_map/ppermute | solution.py:36
  76.5 1.9 %collective-permute-start.19 = (bf16[144,256]{1,0:T(8,128)(2,1)S(1)}, bf16[144,256]{1,0:T(8,128)(2,1)S(1)}, u32[]{:S(2)}, u32[]{:S(2)}) collective-permute-start(bf16[144,256]{1,0:T(8,128)(2,1)S(1)} %shard_map.96.refs_0_.refs_1_), channel_id=1, source_target_pairs={{0,24},{1,25},{2,26},{3,27},{4,28},{5,29},{6,30},{7,31},{8,16},{9,... | collective-permute-start | bytes 221192 | tf_op jit(solution)/shard_map/ppermute | solution.py:36
  78.9 1.2 %collective-permute-start.17 = (bf16[144,256]{1,0:T(8,128)(2,1)S(1)}, bf16[144,256]{1,0:T(8,128)(2,1)S(1)}, u32[]{:S(2)}, u32[]{:S(2)}) collective-permute-start(bf16[144,256]{1,0:T(8,128)(2,1)S(1)} %shard_map.96.refs_0_.refs_1_), channel_id=1, source_target_pairs={{0,8},{1,17},{2,10},{3,19},{4,12},{5,21},{6,14},{7,23},{8,0},{9,25... | collective-permute-start | bytes 221192 | tf_op jit(solution)/shard_map/ppermute | solution.py:36
  80.1 2.2 %shard_map.98 = (f32[2,256,1024]{2,1,0:T(8,128)}, f32[8,128]{1,0:T(8,128)S(1)}) custom-call(s32[3]{0:T(128)S(1)} %pad_add_fusion.place_ref, bf16[144,256]{1,0:T(8,128)(2,1)S(1)} %shard_map.96.refs_0_.refs_1_, f32[2,256,1024]{2,1,0:T(8,128)S(1)} %get-tuple-element.68.refs_1_, bf16[2,256,1024]{2,1,0:T(8,128)(2,1)S(1)} %collective-permute-done.15.refs_2_, ...), custom_call_target="tpu_custom_call" | custom-call | bytes 6295552 | tf_op jit(solution)/shard_map/pallas_call | solution.py:69
  83.2 1.4 %shard_map.99 = (f32[128,1024]{1,0:T(8,128)}, f32[100,128]{1,0:T(8,128)}) custom-call(s32[3]{0:T(128)S(1)} %pad_add_fusion.place_ref, f32[8,128]{1,0:T(8,128)S(1)} %get-tuple-element.72.refs_0_, bf16[144,256]{1,0:T(8,128)(2,1)S(1)} %shard_map.96.refs_0_.refs_1_, bf16[144,256]{1,0:T(8,128)(2,1)S(1)} %collective-permute-done.17.refs_2_, ...), custom_call_target="tpu_custom_call" | custom-call | bytes 870400 | tf_op jit(solution)/shard_map/pallas_call | solution.py:69
  (32 shorter events, 7.1 us)
Async XLA Ops:
  0.6 7.8 %collective-permute-start = (bf16[2,256,1024]{2,1,0:T(8,128)(2,1)}, bf16[2,256,1024]{2,1,0:T(8,128)(2,1)S(1)}, u32[]{:S(2)}, u32[]{:S(2)}) collective-permute-start(bf16[2,256,1024]{2,1,0:T(8,128)(2,1)} %refs_0_.1), channel_id=1, source_target_pairs={{0,1},{1,0},{2,3},{3,2},{4,5},{5,4},{6,7},{7,6},{8,9},{9,8},{10,11... | collective-permute-start | bytes 3145736 | tf_op jit(solution)/shard_map/ppermute | solution.py:20
  1.1 9.0 %collective-permute-start.1 = (bf16[2,256,1024]{2,1,0:T(8,128)(2,1)}, bf16[2,256,1024]{2,1,0:T(8,128)(2,1)S(1)}, u32[]{:S(2)}, u32[]{:S(2)}) collective-permute-start(bf16[2,256,1024]{2,1,0:T(8,128)(2,1)} %refs_0_.1), channel_id=1, source_target_pairs={{1,2},{3,4},{5,6},{2,1},{4,3},{6,5},{9,10},{11,12},{13,14},{10,9},... | collective-permute-start | bytes 3145736 | tf_op jit(solution)/shard_map/ppermute | solution.py:26
  2.0 0.9 %copy-start = (bf16[1024,100]{0,1:T(8,128)(2,1)S(1)}, bf16[1024,100]{0,1:T(8,128)(2,1)}, u32[]{:S(2)}) copy-start(bf16[1024,100]{0,1:T(8,128)(2,1)} %param.11) | copy-start | bytes 614404
  2.9 0.9 %copy-start.1 = (f32[100,512]{1,0:T(8,128)S(1)}, f32[100,512]{1,0:T(8,128)}, u32[]{:S(2)}) copy-start(f32[100,512]{1,0:T(8,128)} %refs_5_.1) | copy-start | bytes 614404
  3.8 0.7 copy-start.2
  4.5 0.7 copy-start.3
  14.4 6.0 %collective-permute-start.2 = (f32[208,128]{1,0:T(8,128)S(1)}, f32[208,128]{1,0:T(8,128)S(1)}, u32[]{:S(2)}, u32[]{:S(2)}) collective-permute-start(f32[208,128]{1,0:T(8,128)S(1)} %get-tuple-element.44.refs_1_), channel_id=1, source_target_pairs={{0,8},{1,17},{2,10},{3,19},{4,12},{5,21},{6,14},{7,23},{8,0},{9,25... | collective-permute-start | bytes 319496 | tf_op jit(solution)/shard_map/ppermute | solution.py:36
  17.0 4.7 %collective-permute-start.3 = (f32[208,128]{1,0:T(8,128)S(1)}, f32[208,128]{1,0:T(8,128)S(1)}, u32[]{:S(2)}, u32[]{:S(2)}) collective-permute-start(f32[208,128]{1,0:T(8,128)S(1)} %get-tuple-element.45.refs_2_), channel_id=1, source_target_pairs={{0,16},{1,9},{2,18},{3,11},{4,20},{5,13},{6,22},{7,15},{8,24},{9,1... | collective-permute-start | bytes 319496 | tf_op jit(solution)/shard_map/ppermute | solution.py:36
  18.5 5.6 %collective-permute-start.4 = (f32[208,128]{1,0:T(8,128)S(1)}, f32[208,128]{1,0:T(8,128)S(1)}, u32[]{:S(2)}, u32[]{:S(2)}) collective-permute-start(f32[208,128]{1,0:T(8,128)S(1)} %get-tuple-element.46.refs_3_), channel_id=1, source_target_pairs={{0,24},{1,25},{2,26},{3,27},{4,28},{5,29},{6,30},{7,31},{8,16},{9,... | collective-permute-start | bytes 319496 | tf_op jit(solution)/shard_map/ppermute | solution.py:36
  25.2 4.8 %collective-permute-start.5 = (bf16[208,128]{1,0:T(8,128)(2,1)S(1)}, bf16[208,128]{1,0:T(8,128)(2,1)S(1)}, u32[]{:S(2)}, u32[]{:S(2)}) collective-permute-start(bf16[208,128]{1,0:T(8,128)(2,1)S(1)} %get-tuple-element.51.refs_1_), channel_id=1, source_target_pairs={{0,8},{1,17},{2,10},{3,19},{4,12},{5,21},{6,14},{7,23},{8,0},{9,25... | collective-permute-start | bytes 159752 | tf_op jit(solution)/shard_map/ppermute | solution.py:36
  25.8 5.8 %collective-permute-start.6 = (bf16[208,128]{1,0:T(8,128)(2,1)S(1)}, bf16[208,128]{1,0:T(8,128)(2,1)S(1)}, u32[]{:S(2)}, u32[]{:S(2)}) collective-permute-start(bf16[208,128]{1,0:T(8,128)(2,1)S(1)} %get-tuple-element.52.refs_2_), channel_id=1, source_target_pairs={{0,16},{1,9},{2,18},{3,11},{4,20},{5,13},{6,22},{7,15},{8,24},{9,1... | collective-permute-start | bytes 159752 | tf_op jit(solution)/shard_map/ppermute | solution.py:36
  26.0 5.6 %collective-permute-start.7 = (bf16[208,128]{1,0:T(8,128)(2,1)S(1)}, bf16[208,128]{1,0:T(8,128)(2,1)S(1)}, u32[]{:S(2)}, u32[]{:S(2)}) collective-permute-start(bf16[208,128]{1,0:T(8,128)(2,1)S(1)} %get-tuple-element.53.refs_3_), channel_id=1, source_target_pairs={{0,24},{1,25},{2,26},{3,27},{4,28},{5,29},{6,30},{7,31},{8,16},{9,... | collective-permute-start | bytes 159752 | tf_op jit(solution)/shard_map/ppermute | solution.py:36
  33.8 7.9 %collective-permute-start.9 = (bf16[2,4,144,256]{3,2,1,0:T(8,128)(2,1)S(1)}, bf16[2,4,144,256]{3,2,1,0:T(8,128)(2,1)S(1)}, u32[]{:S(2)}, u32[]{:S(2)}) collective-permute-start(bf16[2,4,144,256]{3,2,1,0:T(8,128)(2,1)S(1)} %get-tuple-element.59), channel_id=1, source_target_pairs={{0,1},{1,0},{2,3},{3,2},{4,5},{5,4},{6,7},{7,6},{8,9},{9,8},{10,11... | collective-permute-start | bytes 1769480 | tf_op jit(solution)/shard_map/ppermute | solution.py:20
  41.6 7.8 %collective-permute-start.8 = (bf16[2,4,144,256]{3,2,1,0:T(8,128)(2,1)S(1)}, bf16[2,4,144,256]{3,2,1,0:T(8,128)(2,1)S(1)}, u32[]{:S(2)}, u32[]{:S(2)}) collective-permute-start(bf16[2,4,144,256]{3,2,1,0:T(8,128)(2,1)S(1)} %get-tuple-element.58), channel_id=1, source_target_pairs={{0,1},{1,0},{2,3},{3,2},{4,5},{5,4},{6,7},{7,6},{8,9},{9,8},{10,11... | collective-permute-start | bytes 1769480 | tf_op jit(solution)/shard_map/ppermute | solution.py:20
  43.0 9.9 %collective-permute-start.10 = (bf16[2,4,144,256]{3,2,1,0:T(8,128)(2,1)S(1)}, bf16[2,4,144,256]{3,2,1,0:T(8,128)(2,1)S(1)}, u32[]{:S(2)}, u32[]{:S(2)}) collective-permute-start(bf16[2,4,144,256]{3,2,1,0:T(8,128)(2,1)S(1)} %shard_map.93.refs_0_), channel_id=1, source_target_pairs={{0,8},{1,17},{2,10},{3,19},{4,12},{5,21},{6,14},{7,23},{8,0},{9,25... | collective-permute-start | bytes 1769480 | tf_op jit(solution)/shard_map/ppermute | solution.py:36
  48.3 31.7 %collective-permute-start.15 = (bf16[2,256,1024]{2,1,0:T(8,128)(2,1)S(1)}, bf16[2,256,1024]{2,1,0:T(8,128)(2,1)S(1)}, u32[]{:S(2)}, u32[]{:S(2)}) collective-permute-start(bf16[2,256,1024]{2,1,0:T(8,128)(2,1)S(1)} %get-tuple-element.69), channel_id=1, source_target_pairs={{0,1},{1,0},{2,3},{3,2},{4,5},{5,4},{6,7},{7,6},{8,9},{9,8},{10,11... | collective-permute-start | bytes 3145736 | tf_op jit(solution)/shard_map/ppermute | solution.py:20
  48.7 31.4 %collective-permute-start.16 = (bf16[2,256,1024]{2,1,0:T(8,128)(2,1)S(1)}, bf16[2,256,1024]{2,1,0:T(8,128)(2,1)S(1)}, u32[]{:S(2)}, u32[]{:S(2)}) collective-permute-start(bf16[2,256,1024]{2,1,0:T(8,128)(2,1)S(1)} %get-tuple-element.70), channel_id=1, source_target_pairs={{1,2},{3,4},{5,6},{2,1},{4,3},{6,5},{9,10},{11,12},{13,14},{10,9},... | collective-permute-start | bytes 3145736 | tf_op jit(solution)/shard_map/ppermute | solution.py:26
  53.7 6.8 %collective-permute-start.11 = (bf16[1,4,144,256]{3,2,1,0:T(8,128)(2,1)S(1)}, bf16[1,4,144,256]{3,2,1,0:T(8,128)(2,1)S(1)}, u32[]{:S(2)}, u32[]{:S(2)}) collective-permute-start(bf16[1,4,144,256]{3,2,1,0:T(8,128)(2,1)S(1)} %get-tuple-element.61), channel_id=1, source_target_pairs={{0,16},{1,9},{2,18},{3,11},{4,20},{5,13},{6,22},{7,15},{8,24},{9,1... | collective-permute-start | bytes 884744 | tf_op jit(solution)/shard_map/ppermute | solution.py:36
  61.1 12.8 %collective-permute-start.12 = (bf16[144,256]{1,0:T(8,128)(2,1)S(1)}, bf16[144,256]{1,0:T(8,128)(2,1)S(1)}, u32[]{:S(2)}, u32[]{:S(2)}) collective-permute-start(bf16[144,256]{1,0:T(8,128)(2,1)S(1)} %get-tuple-element.63), channel_id=1, source_target_pairs={{0,6},{1,7},{2,4},{3,5},{4,2},{5,3},{6,0},{7,1},{8,14},{9,15},{10,... | collective-permute-start | bytes 221192 | tf_op jit(solution)/shard_map/ppermute | solution.py:36
  66.6 9.3 %collective-permute-start.13 = (bf16[144,256]{1,0:T(8,128)(2,1)S(1)}, bf16[144,256]{1,0:T(8,128)(2,1)S(1)}, u32[]{:S(2)}, u32[]{:S(2)}) collective-permute-start(bf16[144,256]{1,0:T(8,128)(2,1)S(1)} %get-tuple-element.64), channel_id=1, source_target_pairs={{0,4},{1,5},{2,6},{3,7},{4,0},{5,1},{6,2},{7,3},{8,12},{9,13},{10,... | collective-permute-start | bytes 221192 | tf_op jit(solution)/shard_map/ppermute | solution.py:36
  66.9 9.0 %collective-permute-start.14 = (bf16[144,256]{1,0:T(8,128)(2,1)S(1)}, bf16[144,256]{1,0:T(8,128)(2,1)S(1)}, u32[]{:S(2)}, u32[]{:S(2)}) collective-permute-start(bf16[144,256]{1,0:T(8,128)(2,1)S(1)} %get-tuple-element.65), channel_id=1, source_target_pairs={{0,2},{1,3},{2,0},{3,1},{4,6},{5,7},{6,4},{7,5},{8,10},{9,11},{10,... | collective-permute-start | bytes 221192 | tf_op jit(solution)/shard_map/ppermute | solution.py:36
  76.5 5.8 %collective-permute-start.19 = (bf16[144,256]{1,0:T(8,128)(2,1)S(1)}, bf16[144,256]{1,0:T(8,128)(2,1)S(1)}, u32[]{:S(2)}, u32[]{:S(2)}) collective-permute-start(bf16[144,256]{1,0:T(8,128)(2,1)S(1)} %shard_map.96.refs_0_.refs_1_), channel_id=1, source_target_pairs={{0,24},{1,25},{2,26},{3,27},{4,28},{5,29},{6,30},{7,31},{8,16},{9,... | collective-permute-start | bytes 221192 | tf_op jit(solution)/shard_map/ppermute | solution.py:36
  78.4 4.4 %collective-permute-start.18 = (bf16[144,256]{1,0:T(8,128)(2,1)S(1)}, bf16[144,256]{1,0:T(8,128)(2,1)S(1)}, u32[]{:S(2)}, u32[]{:S(2)}) collective-permute-start(bf16[144,256]{1,0:T(8,128)(2,1)S(1)} %shard_map.96.refs_0_.refs_1_), channel_id=1, source_target_pairs={{0,16},{1,9},{2,18},{3,11},{4,20},{5,13},{6,22},{7,15},{8,24},{9,1... | collective-permute-start | bytes 221192 | tf_op jit(solution)/shard_map/ppermute | solution.py:36
  78.9 4.4 %collective-permute-start.17 = (bf16[144,256]{1,0:T(8,128)(2,1)S(1)}, bf16[144,256]{1,0:T(8,128)(2,1)S(1)}, u32[]{:S(2)}, u32[]{:S(2)}) collective-permute-start(bf16[144,256]{1,0:T(8,128)(2,1)S(1)} %shard_map.96.refs_0_.refs_1_), channel_id=1, source_target_pairs={{0,8},{1,17},{2,10},{3,19},{4,12},{5,21},{6,14},{7,23},{8,0},{9,25... | collective-permute-start | bytes 221192 | tf_op jit(solution)/shard_map/ppermute | solution.py:36

commit v6 on v5

--- a/solution.py
+++ b/solution.py
@@ -292,8 +292,9 @@
     mem, nodes, _ = own.shape
     grid = adjacency_t.shape[1]
     first, second = sides(place[2], nodes)
+    daggregate = mul(dpreact[...], w_hidden_t[...]).astype(bf16)
     for m in range(mem):
-        total = mul(dpreact[m * grid : (m + 1) * grid], w_hidden_t[...]).astype(bf16)
+        total = daggregate[m * grid : (m + 1) * grid]
         on_link[m] = mul(adjacency_t[pl.ds(second, nodes)], total).astype(bf16)
         on_chip[m] = mul(adjacency_t[pl.ds(first, nodes)], total).astype(bf16)
         own[m] = mul(adjacency_t[nodes : 2 * nodes], total)

time: 84.9 us -> 84.9 us (level)
  no operation moved by 1% of the time
where the time goes in v6:
time: 84.9 us; the launch traced here: 84.6 us
  Pallas kernels  28.8 us (34%)
  starting transfers between devices  27 us (32%)
  waiting for transfers between devices  24.7 us (29%)
  local copies, waits for them, and re-layouts  3.26 us (4%)
    pallas_call x15, Pallas kernels, call(): pl.pallas_call(kernel, out_shape=[jax.ShapeDtypeStruct(shape, kind) if la...  28.8 us
    ppermute x14, waiting for transfers between devices, core_swap(): lax.ppermute(value, ('ens', 'space'), [(e * space + s, partner(e, s)) for...  24.6 us
    ppermute x14, starting transfers between devices, core_swap(): lax.ppermute(value, ('ens', 'space'), [(e * space + s, partner(e, s)) for...  18.7 us
    ppermute x4, starting transfers between devices, chip_swap(): return lax.ppermute(value, 'space', [(i, i ^ 1) for i in range(count)])  6.85 us
    unnamed x8, local copies, waits for them, and re-layouts  3.26 us
  transfers between devices with their start and end apart: 20, of which 9 were waited for; matrix products, arithmetic and copies ran while one was open for 0% of the time, Pallas kernels for 24%

profile of v6, /device:TPU:0, one launch (start us, length us, event | category | flops | bytes accessed | tf_op | source)
XLA Modules:
  0.0 84.6 jit_solution(1476663250689509742)
XLA Ops:
  1.1 0.7 collective-permute-start.1
  2.0 0.9 %copy-done = bf16[1024,100]{0,1:T(8,128)(2,1)S(1)} copy-done((bf16[1024,100]{0,1:T(8,128)(2,1)S(1)}, bf16[1024,100]{0,1:T(8,128)(2,1)}, u32[]{:S(2)}) %copy-start) | copy-done | bytes 204824
  2.9 0.9 %copy-done.1 = f32[100,512]{1,0:T(8,128)S(1)} copy-done((f32[100,512]{1,0:T(8,128)S(1)}, f32[100,512]{1,0:T(8,128)}, u32[]{:S(2)}) %copy-start.1) | copy-done | bytes 204824
  3.8 0.7 copy-done.2
  5.2 3.1 %shard_map.85 = (bf16[512,768]{1,0:T(8,128)(2,1)S(1)}, bf16[768,512]{1,0:T(8,128)(2,1)S(1)}, bf16[1024,1024]{1,0:T(8,128)(2,1)S(1)}, bf16[2,256,1024]{2,1,0:T(8,...) custom-call(s32[3]{0:T(128)S(1)} %pad_add_fusion.place_ref, ...), custom_call_target="tpu_custom_call" | custom-call | bytes 7667712 | tf_op jit(solution)/shard_map/pallas_call | solution.py:69
  8.4 1.8 %shard_map.86.refs_0_ = f32[2,512,1024]{2,1,0:T(8,128)S(1)} custom-call(s32[3]{0:T(128)S(1)} %pad_add_fusion.place_ref, bf16[2,256,1024]{2,1,0:T(8,128)(2,1)S(1)} %get-tuple-element.40.refs_0_, bf16[2,256,1024]{2,1,0:T(8,128)(2,1)S(1)} %collective-permute-done.refs_1_, bf16[512,768]{1,0:T(8,128)(2,1)S(1)} %get-tuple-element.41.refs_2_), custom_call_target="tpu_custom_call" | custom-call | bytes 7077888 | tf_op jit(solution)/shard_map/pallas_call | solution.py:69
  10.2 4.2 %shard_map.87 = (bf16[2,512,1024]{2,1,0:T(8,128)(2,1)S(1)}, f32[2,512,1024]{2,1,0:T(8,128)S(1)}, bf16[2,512,1024]{2,1,0:T(8,128)(2,1)S(1)}, f32[208,128]{1,0:T(8...) custom-call(s32[3]{0:T(128)S(1)} %pad_add_fusion.place_ref, ...), custom_call_target="tpu_custom_call" | custom-call | flops 2952790016 | bytes 17154048 | tf_op jit(solution)/shard_map/pallas_call | solution.py:69
  14.4 2.6 %collective-permute-start.2 = (f32[208,128]{1,0:T(8,128)S(1)}, f32[208,128]{1,0:T(8,128)S(1)}, u32[]{:S(2)}, u32[]{:S(2)}) collective-permute-start(f32[208,128]{1,0:T(8,128)S(1)} %get-tuple-element.44.refs_1_), channel_id=1, source_target_pairs={{0,8},{1,17},{2,10},{3,19},{4,12},{5,21},{6,14},{7,23},{8,0},{9,25... | collective-permute-start | bytes 319496 | tf_op jit(solution)/shard_map/ppermute | solution.py:36
  17.0 1.5 %collective-permute-start.3 = (f32[208,128]{1,0:T(8,128)S(1)}, f32[208,128]{1,0:T(8,128)S(1)}, u32[]{:S(2)}, u32[]{:S(2)}) collective-permute-start(f32[208,128]{1,0:T(8,128)S(1)} %get-tuple-element.45.refs_2_), channel_id=1, source_target_pairs={{0,16},{1,9},{2,18},{3,11},{4,20},{5,13},{6,22},{7,15},{8,24},{9,1... | collective-permute-start | bytes 319496 | tf_op jit(solution)/shard_map/ppermute | solution.py:36
  18.6 1.9 %shard_map.88.refs_0_.refs_1_ = f32[2,512,1024]{2,1,0:T(8,128)S(1)} custom-call(s32[3]{0:T(128)S(1)} %pad_add_fusion.place_ref, f32[208,128]{1,0:T(8,128)S(1)} %get-tuple-element.43.refs_0_.refs_2_, f32[208,128]{1,0:T(8,128)S(1)} %get-tuple-element.44.refs_1_, f32[208,128]{1,0:T(8,128)S(1)} %get-tuple-element.45.refs_2_, ...), custom_call_target="tpu_custom_call" | custom-call | bytes 8388608 | tf_op jit(solution)/shard_map/pallas_call | solution.py:69
  20.5 1.2 %collective-permute-done.3.refs_4_ = f32[208,128]{1,0:T(8,128)S(1)} collective-permute-done((f32[208,128]{1,0:T(8,128)S(1)}, f32[208,128]{1,0:T(8,128)S(1)}, u32[]{:S(2)}, u32[]{:S(2)}) %collective-permute-start.3) | collective-permute-done | bytes 106528 | tf_op jit(solution)/shard_map/ppermute | solution.py:36
  21.7 2.4 %collective-permute-done.4.refs_5_ = f32[208,128]{1,0:T(8,128)S(1)} collective-permute-done((f32[208,128]{1,0:T(8,128)S(1)}, f32[208,128]{1,0:T(8,128)S(1)}, u32[]{:S(2)}, u32[]{:S(2)}) %collective-permute-start.4) | collective-permute-done | bytes 106528 | tf_op jit(solution)/shard_map/ppermute | solution.py:36
  24.1 1.0 %shard_map.89 = (bf16[208,128]{1,0:T(8,128)(2,1)S(1)}, bf16[208,128]{1,0:T(8,128)(2,1)S(1)}, bf16[208,128]{1,0:T(8,128)(2,1)S(1)}, bf16[208,128]{1,0:T(8,128)(2,1)S(1)}) custom-call(s32[3]{0:T(128)S(1)} %pad_add_fusion.place_ref, f32[2,512,1024]{2,1,0:T(8,128)S(1)} %shard_map.88.refs_0_.refs_1_, f32[104,512]{1,0:T(8,128)S(1)} %get-tuple-element.49.refs_1_, ...), custom_call_target="tpu_custom_call" | custom-call | bytes 851968 | tf_op jit(solution)/shard_map/pallas_call | solution.py:69
  26.0 2.7 %collective-permute-start.7 = (bf16[208,128]{1,0:T(8,128)(2,1)S(1)}, bf16[208,128]{1,0:T(8,128)(2,1)S(1)}, u32[]{:S(2)}, u32[]{:S(2)}) collective-permute-start(bf16[208,128]{1,0:T(8,128)(2,1)S(1)} %get-tuple-element.53.refs_3_), channel_id=1, source_target_pairs={{0,24},{1,25},{2,26},{3,27},{4,28},{5,29},{6,30},{7,31},{8,16},{9,... | collective-permute-start | bytes 159752 | tf_op jit(solution)/shard_map/ppermute | solution.py:36
  28.7 1.2 %shard_map.90 = bf16[1024,1024]{1,0:T(8,128)(2,1)S(1)} custom-call(s32[3]{0:T(128)S(1)} %pad_add_fusion.place_ref, bf16[208,128]{1,0:T(8,128)(2,1)S(1)} %get-tuple-element.50.refs_0_.refs_4_, bf16[208,128]{1,0:T(8,128)(2,1)S(1)} %get-tuple-element.51.refs_1_, bf16[208,128]{1,0:T(8,128)(2,1)S(1)} %get-tuple-element.52.refs_2_, ...), custom_call_target="tpu_custom_call" | custom-call | bytes 4194304 | tf_op jit(solution)/shard_map/pallas_call | solution.py:69
  29.9 1.7 %collective-permute-done.6.refs_6_ = bf16[208,128]{1,0:T(8,128)(2,1)S(1)} collective-permute-done((bf16[208,128]{1,0:T(8,128)(2,1)S(1)}, bf16[208,128]{1,0:T(8,128)(2,1)S(1)}, u32[]{:S(2)}, u32[]{:S(2)}) %collective-permute-start.6) | collective-permute-done | bytes 53280 | tf_op jit(solution)/shard_map/ppermute | solution.py:36
  31.6 2.2 %shard_map.91 = (bf16[1024,1024]{1,0:T(8,128)(2,1)S(1)}, f32[128,1024]{1,0:T(8,128)S(1)}, bf16[2,4,144,256]{3,2,1,0:T(8,128)(2,1)S(1)}) custom-call(s32[3]{0:T(128)S(1)} %pad_add_fusion.place_ref, bf16[104,1024]{1,0:T(8,128)(2,1)S(1)} %get-tuple-element.39.refs_4_.refs_0_, f32[2,512,1024]{2,1,0:T(8,128)S(1)} %shard_map.88.refs_0_.refs_1_, ...), custom_call_target="tpu_custom_call" | custom-call | flops 1073741824 | bytes 12025856 | tf_op jit(solution)/shard_map/pallas_call | solution.py:69
  33.8 5.9 %collective-permute-start.9 = (bf16[2,4,144,256]{3,2,1,0:T(8,128)(2,1)S(1)}, bf16[2,4,144,256]{3,2,1,0:T(8,128)(2,1)S(1)}, u32[]{:S(2)}, u32[]{:S(2)}) collective-permute-start(bf16[2,4,144,256]{3,2,1,0:T(8,128)(2,1)S(1)} %get-tuple-element.59), channel_id=1, source_target_pairs={{0,1},{1,0},{2,3},{3,2},{4,5},{5,4},{6,7},{7,6},{8,9},{9,8},{10,11... | collective-permute-start | bytes 1769480 | tf_op jit(solution)/shard_map/ppermute | solution.py:20
  39.7 1.9 %shard_map.92 = (bf16[2,4,144,256]{3,2,1,0:T(8,128)(2,1)S(1)}, f32[2,4,144,256]{3,2,1,0:T(8,128)S(1)}) custom-call(s32[3]{0:T(128)S(1)} %pad_add_fusion.place_ref, bf16[1024,1024]{1,0:T(8,128)(2,1)S(1)} %get-tuple-element.55.refs_0_.refs_1_, f32[128,1024]{1,0:T(8,128)S(1)} %get-tuple-element.56.refs_1_.refs_2_, bf16[4,2,128,1024]{3,2,1,0:T(8,128)(2,1)S(1)} %bitcast.9), custom_call_target="tpu_custom_call" | custom-call | flops 1073741824 | bytes 6488064 | tf_op jit(solution)/shard_map/pallas_call | solution.py:69
  41.7 1.3 %shard_map.93.refs_0_ = bf16[2,4,144,256]{3,2,1,0:T(8,128)(2,1)S(1)} custom-call(s32[3]{0:T(128)S(1)} %pad_add_fusion.place_ref, f32[2,4,144,256]{3,2,1,0:T(8,128)S(1)} %get-tuple-element.57.refs_0_, bf16[1024,1024]{1,0:T(8,128)(2,1)S(1)} %get-tuple-element.55.refs_0_.refs_1_, f32[128,1024]{1,0:T(8,128)S(1)} %get-tuple-element.56.refs_1_.refs_2_, ...), custom_call_target="tpu_custom_call" | custom-call | flops 536870912 | bytes 5898240 | tf_op jit(solution)/shard_map/pallas_call | solution.py:69
  43.6 4.7 %shard_map.97 = (bf16[2,256,1024]{2,1,0:T(8,128)(2,1)S(1)}, bf16[2,256,1024]{2,1,0:T(8,128)(2,1)S(1)}, f32[2,256,1024]{2,1,0:T(8,128)S(1)}) custom-call(s32[3]{0:T(128)S(1)} %pad_add_fusion.place_ref, bf16[2,4,144,256]{3,2,1,0:T(8,128)(2,1)S(1)} %shard_map.93.refs_0_, bf16[1024,1024]{1,0:T(8,128)(2,1)S(1)} %get-tuple-element.55.refs_0_.refs_1_, ...), custom_call_target="tpu_custom_call" | custom-call | flops 3758096384 | bytes 9175040 | tf_op jit(solution)/shard_map/pallas_call | solution.py:69
  48.6 0.7 collective-permute-start.16
  49.4 3.6 %collective-permute-done.10.refs_2_ = bf16[2,4,144,256]{3,2,1,0:T(8,128)(2,1)S(1)} collective-permute-done((bf16[2,4,144,256]{3,2,1,0:T(8,128)(2,1)S(1)}, bf16[2,4,144,256]{3,2,1,0:T(8,128)(2,1)S(1)}, u32[]{:S(2)}, u32[]{:S(2)}) %collective-permute-start.10) | collective-permute-done | bytes 589856 | tf_op jit(solution)/shard_map/ppermute | solution.py:36
  53.0 0.7 shard_map.94
  54.3 6.1 %collective-permute-done.11.refs_1_ = bf16[1,4,144,256]{3,2,1,0:T(8,128)(2,1)S(1)} collective-permute-done((bf16[1,4,144,256]{3,2,1,0:T(8,128)(2,1)S(1)}, bf16[1,4,144,256]{3,2,1,0:T(8,128)(2,1)S(1)}, u32[]{:S(2)}, u32[]{:S(2)}) %collective-permute-start.11) | collective-permute-done | bytes 294944 | tf_op jit(solution)/shard_map/ppermute | solution.py:36
  61.1 5.5 %collective-permute-start.12 = (bf16[144,256]{1,0:T(8,128)(2,1)S(1)}, bf16[144,256]{1,0:T(8,128)(2,1)S(1)}, u32[]{:S(2)}, u32[]{:S(2)}) collective-permute-start(bf16[144,256]{1,0:T(8,128)(2,1)S(1)} %get-tuple-element.63), channel_id=1, source_target_pairs={{0,6},{1,7},{2,4},{3,5},{4,2},{5,3},{6,0},{7,1},{8,14},{9,15},{10,... | collective-permute-start | bytes 221192 | tf_op jit(solution)/shard_map/ppermute | solution.py:36
  67.3 6.6 %collective-permute-done.12.refs_1_ = bf16[144,256]{1,0:T(8,128)(2,1)S(1)} collective-permute-done((bf16[144,256]{1,0:T(8,128)(2,1)S(1)}, bf16[144,256]{1,0:T(8,128)(2,1)S(1)}, u32[]{:S(2)}, u32[]{:S(2)}) %collective-permute-start.12) | collective-permute-done | bytes 73760 | tf_op jit(solution)/shard_map/ppermute | solution.py:36
  73.8 2.1 %collective-permute-done.13.refs_2_ = bf16[144,256]{1,0:T(8,128)(2,1)S(1)} collective-permute-done((bf16[144,256]{1,0:T(8,128)(2,1)S(1)}, bf16[144,256]{1,0:T(8,128)(2,1)S(1)}, u32[]{:S(2)}, u32[]{:S(2)}) %collective-permute-start.13) | collective-permute-done | bytes 73760 | tf_op jit(solution)/shard_map/ppermute | solution.py:36
  76.5 1.9 %collective-permute-start.19 = (bf16[144,256]{1,0:T(8,128)(2,1)S(1)}, bf16[144,256]{1,0:T(8,128)(2,1)S(1)}, u32[]{:S(2)}, u32[]{:S(2)}) collective-permute-start(bf16[144,256]{1,0:T(8,128)(2,1)S(1)} %shard_map.96.refs_0_.refs_1_), channel_id=1, source_target_pairs={{0,24},{1,25},{2,26},{3,27},{4,28},{5,29},{6,30},{7,31},{8,16},{9,... | collective-permute-start | bytes 221192 | tf_op jit(solution)/shard_map/ppermute | solution.py:36
  78.8 1.2 %collective-permute-start.17 = (bf16[144,256]{1,0:T(8,128)(2,1)S(1)}, bf16[144,256]{1,0:T(8,128)(2,1)S(1)}, u32[]{:S(2)}, u32[]{:S(2)}) collective-permute-start(bf16[144,256]{1,0:T(8,128)(2,1)S(1)} %shard_map.96.refs_0_.refs_1_), channel_id=1, source_target_pairs={{0,8},{1,17},{2,10},{3,19},{4,12},{5,21},{6,14},{7,23},{8,0},{9,25... | collective-permute-start | bytes 221192 | tf_op jit(solution)/shard_map/ppermute | solution.py:36
  80.0 2.2 %shard_map.98 = (f32[2,256,1024]{2,1,0:T(8,128)}, f32[8,128]{1,0:T(8,128)S(1)}) custom-call(s32[3]{0:T(128)S(1)} %pad_add_fusion.place_ref, bf16[144,256]{1,0:T(8,128)(2,1)S(1)} %shard_map.96.refs_0_.refs_1_, f32[2,256,1024]{2,1,0:T(8,128)S(1)} %get-tuple-element.68.refs_1_, bf16[2,256,1024]{2,1,0:T(8,128)(2,1)S(1)} %collective-permute-done.15.refs_2_, ...), custom_call_target="tpu_custom_call" | custom-call | bytes 6295552 | tf_op jit(solution)/shard_map/pallas_call | solution.py:69
  83.2 1.4 %shard_map.99 = (f32[128,1024]{1,0:T(8,128)}, f32[100,128]{1,0:T(8,128)}) custom-call(s32[3]{0:T(128)S(1)} %pad_add_fusion.place_ref, f32[8,128]{1,0:T(8,128)S(1)} %get-tuple-element.72.refs_0_, bf16[144,256]{1,0:T(8,128)(2,1)S(1)} %shard_map.96.refs_0_.refs_1_, bf16[144,256]{1,0:T(8,128)(2,1)S(1)} %collective-permute-done.17.refs_2_, ...), custom_call_target="tpu_custom_call" | custom-call | bytes 870400 | tf_op jit(solution)/shard_map/pallas_call | solution.py:69
  (32 shorter events, 7.1 us)
Async XLA Ops:
  0.6 7.8 %collective-permute-start = (bf16[2,256,1024]{2,1,0:T(8,128)(2,1)}, bf16[2,256,1024]{2,1,0:T(8,128)(2,1)S(1)}, u32[]{:S(2)}, u32[]{:S(2)}) collective-permute-start(bf16[2,256,1024]{2,1,0:T(8,128)(2,1)} %refs_0_.1), channel_id=1, source_target_pairs={{0,1},{1,0},{2,3},{3,2},{4,5},{5,4},{6,7},{7,6},{8,9},{9,8},{10,11... | collective-permute-start | bytes 3145736 | tf_op jit(solution)/shard_map/ppermute | solution.py:20
  1.1 9.0 %collective-permute-start.1 = (bf16[2,256,1024]{2,1,0:T(8,128)(2,1)}, bf16[2,256,1024]{2,1,0:T(8,128)(2,1)S(1)}, u32[]{:S(2)}, u32[]{:S(2)}) collective-permute-start(bf16[2,256,1024]{2,1,0:T(8,128)(2,1)} %refs_0_.1), channel_id=1, source_target_pairs={{1,2},{3,4},{5,6},{2,1},{4,3},{6,5},{9,10},{11,12},{13,14},{10,9},... | collective-permute-start | bytes 3145736 | tf_op jit(solution)/shard_map/ppermute | solution.py:26
  2.0 0.9 %copy-start = (bf16[1024,100]{0,1:T(8,128)(2,1)S(1)}, bf16[1024,100]{0,1:T(8,128)(2,1)}, u32[]{:S(2)}) copy-start(bf16[1024,100]{0,1:T(8,128)(2,1)} %param.11) | copy-start | bytes 614404
  2.9 0.9 %copy-start.1 = (f32[100,512]{1,0:T(8,128)S(1)}, f32[100,512]{1,0:T(8,128)}, u32[]{:S(2)}) copy-start(f32[100,512]{1,0:T(8,128)} %refs_5_.1) | copy-start | bytes 614404
  3.8 0.7 copy-start.2
  4.5 0.7 copy-start.3
  14.4 6.0 %collective-permute-start.2 = (f32[208,128]{1,0:T(8,128)S(1)}, f32[208,128]{1,0:T(8,128)S(1)}, u32[]{:S(2)}, u32[]{:S(2)}) collective-permute-start(f32[208,128]{1,0:T(8,128)S(1)} %get-tuple-element.44.refs_1_), channel_id=1, source_target_pairs={{0,8},{1,17},{2,10},{3,19},{4,12},{5,21},{6,14},{7,23},{8,0},{9,25... | collective-permute-start | bytes 319496 | tf_op jit(solution)/shard_map/ppermute | solution.py:36
  17.0 4.7 %collective-permute-start.3 = (f32[208,128]{1,0:T(8,128)S(1)}, f32[208,128]{1,0:T(8,128)S(1)}, u32[]{:S(2)}, u32[]{:S(2)}) collective-permute-start(f32[208,128]{1,0:T(8,128)S(1)} %get-tuple-element.45.refs_2_), channel_id=1, source_target_pairs={{0,16},{1,9},{2,18},{3,11},{4,20},{5,13},{6,22},{7,15},{8,24},{9,1... | collective-permute-start | bytes 319496 | tf_op jit(solution)/shard_map/ppermute | solution.py:36
  18.5 5.6 %collective-permute-start.4 = (f32[208,128]{1,0:T(8,128)S(1)}, f32[208,128]{1,0:T(8,128)S(1)}, u32[]{:S(2)}, u32[]{:S(2)}) collective-permute-start(f32[208,128]{1,0:T(8,128)S(1)} %get-tuple-element.46.refs_3_), channel_id=1, source_target_pairs={{0,24},{1,25},{2,26},{3,27},{4,28},{5,29},{6,30},{7,31},{8,16},{9,... | collective-permute-start | bytes 319496 | tf_op jit(solution)/shard_map/ppermute | solution.py:36
  25.2 4.8 %collective-permute-start.5 = (bf16[208,128]{1,0:T(8,128)(2,1)S(1)}, bf16[208,128]{1,0:T(8,128)(2,1)S(1)}, u32[]{:S(2)}, u32[]{:S(2)}) collective-permute-start(bf16[208,128]{1,0:T(8,128)(2,1)S(1)} %get-tuple-element.51.refs_1_), channel_id=1, source_target_pairs={{0,8},{1,17},{2,10},{3,19},{4,12},{5,21},{6,14},{7,23},{8,0},{9,25... | collective-permute-start | bytes 159752 | tf_op jit(solution)/shard_map/ppermute | solution.py:36
  25.8 5.8 %collective-permute-start.6 = (bf16[208,128]{1,0:T(8,128)(2,1)S(1)}, bf16[208,128]{1,0:T(8,128)(2,1)S(1)}, u32[]{:S(2)}, u32[]{:S(2)}) collective-permute-start(bf16[208,128]{1,0:T(8,128)(2,1)S(1)} %get-tuple-element.52.refs_2_), channel_id=1, source_target_pairs={{0,16},{1,9},{2,18},{3,11},{4,20},{5,13},{6,22},{7,15},{8,24},{9,1... | collective-permute-start | bytes 159752 | tf_op jit(solution)/shard_map/ppermute | solution.py:36
  26.0 5.6 %collective-permute-start.7 = (bf16[208,128]{1,0:T(8,128)(2,1)S(1)}, bf16[208,128]{1,0:T(8,128)(2,1)S(1)}, u32[]{:S(2)}, u32[]{:S(2)}) collective-permute-start(bf16[208,128]{1,0:T(8,128)(2,1)S(1)} %get-tuple-element.53.refs_3_), channel_id=1, source_target_pairs={{0,24},{1,25},{2,26},{3,27},{4,28},{5,29},{6,30},{7,31},{8,16},{9,... | collective-permute-start | bytes 159752 | tf_op jit(solution)/shard_map/ppermute | solution.py:36
  33.8 7.9 %collective-permute-start.9 = (bf16[2,4,144,256]{3,2,1,0:T(8,128)(2,1)S(1)}, bf16[2,4,144,256]{3,2,1,0:T(8,128)(2,1)S(1)}, u32[]{:S(2)}, u32[]{:S(2)}) collective-permute-start(bf16[2,4,144,256]{3,2,1,0:T(8,128)(2,1)S(1)} %get-tuple-element.59), channel_id=1, source_target_pairs={{0,1},{1,0},{2,3},{3,2},{4,5},{5,4},{6,7},{7,6},{8,9},{9,8},{10,11... | collective-permute-start | bytes 1769480 | tf_op jit(solution)/shard_map/ppermute | solution.py:20
  41.6 7.8 %collective-permute-start.8 = (bf16[2,4,144,256]{3,2,1,0:T(8,128)(2,1)S(1)}, bf16[2,4,144,256]{3,2,1,0:T(8,128)(2,1)S(1)}, u32[]{:S(2)}, u32[]{:S(2)}) collective-permute-start(bf16[2,4,144,256]{3,2,1,0:T(8,128)(2,1)S(1)} %get-tuple-element.58), channel_id=1, source_target_pairs={{0,1},{1,0},{2,3},{3,2},{4,5},{5,4},{6,7},{7,6},{8,9},{9,8},{10,11... | collective-permute-start | bytes 1769480 | tf_op jit(solution)/shard_map/ppermute | solution.py:20
  43.0 9.9 %collective-permute-start.10 = (bf16[2,4,144,256]{3,2,1,0:T(8,128)(2,1)S(1)}, bf16[2,4,144,256]{3,2,1,0:T(8,128)(2,1)S(1)}, u32[]{:S(2)}, u32[]{:S(2)}) collective-permute-start(bf16[2,4,144,256]{3,2,1,0:T(8,128)(2,1)S(1)} %shard_map.93.refs_0_), channel_id=1, source_target_pairs={{0,8},{1,17},{2,10},{3,19},{4,12},{5,21},{6,14},{7,23},{8,0},{9,25... | collective-permute-start | bytes 1769480 | tf_op jit(solution)/shard_map/ppermute | solution.py:36
  48.3 31.7 %collective-permute-start.15 = (bf16[2,256,1024]{2,1,0:T(8,128)(2,1)S(1)}, bf16[2,256,1024]{2,1,0:T(8,128)(2,1)S(1)}, u32[]{:S(2)}, u32[]{:S(2)}) collective-permute-start(bf16[2,256,1024]{2,1,0:T(8,128)(2,1)S(1)} %get-tuple-element.69), channel_id=1, source_target_pairs={{0,1},{1,0},{2,3},{3,2},{4,5},{5,4},{6,7},{7,6},{8,9},{9,8},{10,11... | collective-permute-start | bytes 3145736 | tf_op jit(solution)/shard_map/ppermute | solution.py:20
  48.6 31.4 %collective-permute-start.16 = (bf16[2,256,1024]{2,1,0:T(8,128)(2,1)S(1)}, bf16[2,256,1024]{2,1,0:T(8,128)(2,1)S(1)}, u32[]{:S(2)}, u32[]{:S(2)}) collective-permute-start(bf16[2,256,1024]{2,1,0:T(8,128)(2,1)S(1)} %get-tuple-element.70), channel_id=1, source_target_pairs={{1,2},{3,4},{5,6},{2,1},{4,3},{6,5},{9,10},{11,12},{13,14},{10,9},... | collective-permute-start | bytes 3145736 | tf_op jit(solution)/shard_map/ppermute | solution.py:26
  53.7 6.8 %collective-permute-start.11 = (bf16[1,4,144,256]{3,2,1,0:T(8,128)(2,1)S(1)}, bf16[1,4,144,256]{3,2,1,0:T(8,128)(2,1)S(1)}, u32[]{:S(2)}, u32[]{:S(2)}) collective-permute-start(bf16[1,4,144,256]{3,2,1,0:T(8,128)(2,1)S(1)} %get-tuple-element.61), channel_id=1, source_target_pairs={{0,16},{1,9},{2,18},{3,11},{4,20},{5,13},{6,22},{7,15},{8,24},{9,1... | collective-permute-start | bytes 884744 | tf_op jit(solution)/shard_map/ppermute | solution.py:36
  61.1 12.8 %collective-permute-start.12 = (bf16[144,256]{1,0:T(8,128)(2,1)S(1)}, bf16[144,256]{1,0:T(8,128)(2,1)S(1)}, u32[]{:S(2)}, u32[]{:S(2)}) collective-permute-start(bf16[144,256]{1,0:T(8,128)(2,1)S(1)} %get-tuple-element.63), channel_id=1, source_target_pairs={{0,6},{1,7},{2,4},{3,5},{4,2},{5,3},{6,0},{7,1},{8,14},{9,15},{10,... | collective-permute-start | bytes 221192 | tf_op jit(solution)/shard_map/ppermute | solution.py:36
  66.6 9.3 %collective-permute-start.13 = (bf16[144,256]{1,0:T(8,128)(2,1)S(1)}, bf16[144,256]{1,0:T(8,128)(2,1)S(1)}, u32[]{:S(2)}, u32[]{:S(2)}) collective-permute-start(bf16[144,256]{1,0:T(8,128)(2,1)S(1)} %get-tuple-element.64), channel_id=1, source_target_pairs={{0,4},{1,5},{2,6},{3,7},{4,0},{5,1},{6,2},{7,3},{8,12},{9,13},{10,... | collective-permute-start | bytes 221192 | tf_op jit(solution)/shard_map/ppermute | solution.py:36
  66.9 9.0 %collective-permute-start.14 = (bf16[144,256]{1,0:T(8,128)(2,1)S(1)}, bf16[144,256]{1,0:T(8,128)(2,1)S(1)}, u32[]{:S(2)}, u32[]{:S(2)}) collective-permute-start(bf16[144,256]{1,0:T(8,128)(2,1)S(1)} %get-tuple-element.65), channel_id=1, source_target_pairs={{0,2},{1,3},{2,0},{3,1},{4,6},{5,7},{6,4},{7,5},{8,10},{9,11},{10,... | collective-permute-start | bytes 221192 | tf_op jit(solution)/shard_map/ppermute | solution.py:36
  76.5 5.8 %collective-permute-start.19 = (bf16[144,256]{1,0:T(8,128)(2,1)S(1)}, bf16[144,256]{1,0:T(8,128)(2,1)S(1)}, u32[]{:S(2)}, u32[]{:S(2)}) collective-permute-start(bf16[144,256]{1,0:T(8,128)(2,1)S(1)} %shard_map.96.refs_0_.refs_1_), channel_id=1, source_target_pairs={{0,24},{1,25},{2,26},{3,27},{4,28},{5,29},{6,30},{7,31},{8,16},{9,... | collective-permute-start | bytes 221192 | tf_op jit(solution)/shard_map/ppermute | solution.py:36
  78.4 4.4 %collective-permute-start.18 = (bf16[144,256]{1,0:T(8,128)(2,1)S(1)}, bf16[144,256]{1,0:T(8,128)(2,1)S(1)}, u32[]{:S(2)}, u32[]{:S(2)}) collective-permute-start(bf16[144,256]{1,0:T(8,128)(2,1)S(1)} %shard_map.96.refs_0_.refs_1_), channel_id=1, source_target_pairs={{0,16},{1,9},{2,18},{3,11},{4,20},{5,13},{6,22},{7,15},{8,24},{9,1... | collective-permute-start | bytes 221192 | tf_op jit(solution)/shard_map/ppermute | solution.py:36
  78.8 4.4 %collective-permute-start.17 = (bf16[144,256]{1,0:T(8,128)(2,1)S(1)}, bf16[144,256]{1,0:T(8,128)(2,1)S(1)}, u32[]{:S(2)}, u32[]{:S(2)}) collective-permute-start(bf16[144,256]{1,0:T(8,128)(2,1)S(1)} %shard_map.96.refs_0_.refs_1_), channel_id=1, source_target_pairs={{0,8},{1,17},{2,10},{3,19},{4,12},{5,21},{6,14},{7,23},{8,0},{9,25... | collective-permute-start | bytes 221192 | tf_op jit(solution)/shard_map/ppermute | solution.py:36
